TPU v7x, 256 devices: a whole 4x4x8 slice. The times are simulated.
256 devices in a mesh: seq: 64 (over z, x, core), head: 4 (over y).
Axes of the slice: x: 4, y: 4, z: 8, core: 2. Of those that a mesh axis runs over, the one named last changes fastest.
Arguments:
- query: bfloat16 [24576, 2048], P('seq', 'head'), may hold values from -200 to 200
- key: bfloat16 [24576, 2048], P('seq', 'head'), may hold values from -6 to 6
- value: bfloat16 [24576, 2048], P('seq', 'head'), may hold values from -6 to 6
- mixed_grad: bfloat16 [24576, 4096], P('seq', 'head'), may hold values from -6 to 6
- out_weight: bfloat16 [2048, 4096], P('head', 'seq'), may hold values from -0.125 to 0.125
- cluster: int32 [16, 24576, 1], P('head', 'seq'), may hold values from 0 to 63; in each aligned block of 384 rows (0 to 383, 384 to 767, ..., all dimensions but the last counted through in order) at most 12 rows name the same one
Outputs:
- mixed: bfloat16 [24576, 4096], P('seq', 'head')
- query_grad: bfloat16 [24576, 2048], P('seq', 'head')
- key_grad: bfloat16 [24576, 2048], P('seq', 'head')
- value_grad: bfloat16 [24576, 2048], P('seq', 'head')
Inputs may be any that keep to these rules, and one draw needn't show every extreme that they name: In each aligned block of 384 tokens of one head (the tokens of one index of seq) no cluster is named by more than 12 tokens, and some block reaches 12.
All inputs are finite; a program needn't handle non-finite values.
Results may differ from a plain program's by a relative error of at most 0.0058.
Values may be sent and summed in bfloat16 or wider, within the bound.
No kernel may reach another device: no remote copies, remote signals or barrier semaphores. Data moves between devices by JAX's collectives and lax.ppermute only.
A program may use at most 128 MiB of HBM per device.

v0:
```python
import math

import jax
import jax.numpy as jnp
from jax import lax
from jax.sharding import PartitionSpec as P

HD = 128
CLUSTERS = 64
CAP = 12


def attend_blocks(blocks, same):
    width = blocks.shape[-1] // 4
    q = blocks[..., :width]
    k = blocks[..., width : 2 * width]
    v = blocks[..., 2 * width : 3 * width]
    g = blocks[..., 3 * width :]
    scale = 1.0 / math.sqrt(width)
    scores = jnp.einsum("ipqd,ipkd->ipqk", q, k, preferred_element_type=jnp.float32) * scale
    scores = jnp.where(same, scores, -1e30)
    top = jnp.max(scores, axis=-1, keepdims=True)
    weights = jnp.where(same, jnp.exp(scores - top), 0.0)
    probs = weights / jnp.sum(weights, axis=-1, keepdims=True)
    probs16 = probs.astype(jnp.bfloat16)
    attended = jnp.einsum("ipqk,ipkd->ipqd", probs16, v, preferred_element_type=jnp.float32).astype(
        jnp.bfloat16
    )
    dprobs = jnp.einsum("ipqd,ipkd->ipqk", g, v, preferred_element_type=jnp.float32)
    delta = jnp.sum(probs * dprobs, axis=-1, keepdims=True)
    dscores = (probs * (dprobs - delta)).astype(jnp.bfloat16)
    query_grad = (
        jnp.einsum("ipqk,ipkd->ipqd", dscores, k, preferred_element_type=jnp.float32) * scale
    ).astype(jnp.bfloat16)
    key_grad = (
        jnp.einsum("ipqk,ipqd->ipkd", dscores, q, preferred_element_type=jnp.float32) * scale
    ).astype(jnp.bfloat16)
    value_grad = jnp.einsum(
        "ipqk,ipqd->ipkd", probs16, g, preferred_element_type=jnp.float32
    ).astype(jnp.bfloat16)
    return jnp.concatenate([attended, query_grad, key_grad, value_grad], axis=-1)


def owner_work(payload, tally):
    senders = payload.shape[0]
    items = payload.shape[1]
    slots = payload.shape[2]
    packed_width = payload.shape[3]
    per_owner = tally.shape[2]
    depth = slots // per_owner
    rows_all = senders * depth
    blocks = payload.reshape(senders, items, per_owner, depth, packed_width).transpose(
        1, 2, 0, 3, 4
    )
    blocks = blocks.reshape(items, per_owner, rows_all, packed_width)
    live_counts = tally.astype(jnp.int32).transpose(1, 2, 0)
    position = jnp.arange(rows_all, dtype=jnp.int32)
    sender = position // depth
    within = position % depth
    live = within[None, None, :] < live_counts[:, :, sender]
    eye = jnp.eye(rows_all, dtype=bool)
    same = live[:, :, None, :] | eye[None, None]
    results = attend_blocks(blocks, same)
    results = results.reshape(items, per_owner, senders, depth, packed_width).transpose(
        2, 0, 1, 3, 4
    )
    return results.reshape(senders, items, slots, packed_width)


def local(query, key, value, mixed_grad, out_weight, cluster):
    tok_rows = query.shape[0]
    heads_dev = cluster.shape[0]
    ranks_seq = lax.axis_size("seq")
    per_owner = CLUSTERS // ranks_seq
    slot_width = per_owner * CAP
    weight_full = lax.all_gather(out_weight, "seq", axis=1, tiled=True)
    grad_full = lax.all_gather(mixed_grad, "head", axis=1, tiled=True)
    ids = cluster[:, :, 0]
    onehot = (ids[:, :, None] == jnp.arange(CLUSTERS, dtype=jnp.int32)[None, None, :]).astype(
        jnp.int32
    )
    ranking = jnp.sum((jnp.cumsum(onehot, axis=1) - 1) * onehot, axis=2)
    counts = jnp.sum(onehot, axis=1)
    owner = ids // per_owner
    local_slot = ids % per_owner * CAP + ranking
    head_index = jnp.broadcast_to(jnp.arange(heads_dev, dtype=jnp.int32)[:, None], ids.shape)
    tallies = (
        counts.reshape(heads_dev, ranks_seq, per_owner).transpose(1, 0, 2).astype(jnp.bfloat16)
    )
    grad_att = jnp.dot(grad_full, weight_full.T, preferred_element_type=jnp.float32).astype(
        jnp.bfloat16
    )
    pieces = [query, key, value, grad_att]
    rows = jnp.concatenate([p.reshape(tok_rows, heads_dev, HD) for p in pieces], axis=2).transpose(
        1, 0, 2
    )
    buffer = jnp.zeros((ranks_seq, heads_dev, slot_width, rows.shape[2]), jnp.bfloat16)
    payload = buffer.at[owner, head_index, local_slot].set(rows)
    pieces = (
        lax.all_to_all(payload, "seq", split_axis=0, concat_axis=0, tiled=True),
        lax.all_to_all(tallies, "seq", split_axis=0, concat_axis=0, tiled=True),
    )
    done = owner_work(pieces[0], pieces[1])
    back = lax.all_to_all(done, "seq", split_axis=0, concat_axis=0, tiled=True)
    fetched = back[owner, head_index, local_slot].transpose(1, 0, 2)
    attended = fetched[:, :, :HD].reshape(tok_rows, heads_dev * HD)
    query_grad = fetched[:, :, HD : 2 * HD].reshape(tok_rows, heads_dev * HD)
    key_grad = fetched[:, :, 2 * HD : 3 * HD].reshape(tok_rows, heads_dev * HD)
    value_grad = fetched[:, :, 3 * HD :].reshape(tok_rows, heads_dev * HD)
    partial_sums = jnp.dot(attended, weight_full, preferred_element_type=jnp.float32)
    mixed = lax.psum_scatter(partial_sums, "head", scatter_dimension=1, tiled=True).astype(
        jnp.bfloat16
    )
    return (mixed, query_grad, key_grad, value_grad)


def solution(mesh):
    placed = (
        P("seq", "head"),
        P("seq", "head"),
        P("seq", "head"),
        P("seq", "head"),
        P("head", "seq"),
        P("head", "seq", None),
    )
    return jax.shard_map(
        local,
        mesh=mesh,
        in_specs=placed,
        out_specs=(P("seq", "head"), P("seq", "head"), P("seq", "head"), P("seq", "head")),
        check_vma=False,
    )
```

profile of v0, /device:TPU:2, one launch (start us, length us, event | category | flops | bytes accessed | tf_op | source)
XLA Modules:
  0.0 461.9 jit_solution(12940559924631858802)
XLA Ops:
  7.3 0.7 all-gather.3.cloned.1.call-update
  8.0 0.7 all-gather.5.cloned.1.call-update
  8.7 0.7 copy.165
  9.5 3.6 reduce-window.6
  13.2 0.2 copy.99
  13.4 0.3 convert_reduce_fusion
  13.7 0.7 copy.93
  14.5 12.0 %all-to-all-start = ((bf16[64,4,1]{1,2,0:T(2,128)(2,1)}), bf16[64,4,1]{1,2,0:T(2,128)(2,1)S(1)}, u32[]{:S(2)}, u32[]{:S(2)}) async-start(bf16[64,4,1]{1,2,0:T(2,128)(2,1)} %copy.93), calls=%async_computation | async-start | bytes 65536 | tf_op jit(solution)/shard_map/all_to_all | solution.py:101
  26.8 0.2 copy.104
  27.0 0.2 copy.102
  27.3 0.2 copy.103
  27.5 27.5 %all-gather.3.cloned.1.call-done = bf16[384,4096]{1,0:T(8,128)(2,1)} async-done(((bf16[384,1024]{1,0:T(8,128)(2,1)}), bf16[384,4096]{1,0:T(8,128)(2,1)}) %all-gather.3.cloned.1.call-update) | async-done | bytes 3145744 | tf_op jit(solution)/shard_map/all_gather | solution.py:77
  55.0 80.8 %all-gather.5.cloned.1.call-done = bf16[512,4096]{0,1:T(8,128)(2,1)} async-done(((bf16[512,64]{0,1:T(8,128)(2,1)}), bf16[512,4096]{0,1:T(8,128)(2,1)}) %all-gather.5.cloned.1.call-update) | async-done | bytes 4194320 | tf_op jit(solution)/shard_map/all_gather | solution.py:76
  135.8 4.9 %convolution_convert_fusion = bf16[384,512]{1,0:T(8,128)(2,1)S(1)} fusion(bf16[384,4096]{1,0:T(8,128)(2,1)} %all-gather.3.cloned.1.call-done, bf16[512,4096]{0,1:T(8,128)(2,1)} %all-gather.5.cloned.1.call-done), kind=kOutput, calls=%fused_computation.27 | convolution fusion | flops 1610809344 | bytes 7733248 | tf_op jit(solution)/shard_map/dot_general | solution.py:90
  140.8 0.2 copy.123
  141.1 1.7 copy.106
  142.8 8.8 %scatter_custom_fusion = bf16[3072,512]{1,0:T(8,128)(2,1)S(1)} fusion(s32[1536]{0:T(1024)S(1)} %reshape.273, bf16[1536,512]{1,0:T(8,128)(2,1)} %bitcast.110, bf16[]{:T(256)} %constant.63.clone.1), kind=kCustom, calls=%fused_computation.21 | custom fusion | bytes 3146240
  151.7 3.0 reshape.255
  154.7 7.7 %all-to-all-start.1 = ((bf16[64,4,12,512]{3,1,2,0:T(4,128)(2,1)}), bf16[64,4,12,512]{3,1,2,0:T(4,128)(2,1)S(1)}, u32[]{:S(2)}, u32[]{:S(2)}) async-start(bf16[64,4,12,512]{3,1,2,0:T(4,128)(2,1)} %bitcast.103), calls=%async_computation.1 | async-start | bytes 6291456 | tf_op jit(solution)/shard_map/all_to_all | solution.py:100
  162.4 1.0 iota_compare_fusion
  163.6 2.3 gather_fusion
  165.9 1.2 compare_bitcast_fusion
  167.2 68.8 %all-to-all-done.1 = bf16[64,4,12,512]{3,1,2,0:T(4,128)(2,1)S(1)} async-done(((bf16[64,4,12,512]{3,1,2,0:T(4,128)(2,1)}), bf16[64,4,12,512]{3,1,2,0:T(4,128)(2,1)S(1)}, u32[]{:S(2)}, u32[]{:S(2)}) %all-to-all-start.1) | async-done | bytes 3145760 | tf_op jit(solution)/shard_map/all_to_all | solution.py:100
  236.1 2.5 fusion.33
  238.6 9.6 %fusion.35 = (f32[4,768]{1,0:T(4,128)S(1)}, f32[4,768,768]{1,2,0:T(8,128)}) fusion(pred[768,768]{0,1:T(8,128)(4,1)} %iota_compare_fusion, pred[4,768]{1,0:T(4,128)(4,1)S(1)} %copy.96, bf16[4,1,768,128]{3,0,2,1:T(4,128)(2,1)} %get-tuple-element.24, bf16[4,1,768,128]{3,0,2,1:T(4,128)(2,1)} %get-tuple-element.23), kind=kOutput, calls=%fused_computation.73 | convolution fusion | flops 620495616 | bytes 11615232 | tf_op jit(solution)/shard_map/sub | solution.py:23
  248.2 5.6 %fusion.12 = bf16[4,768,128]{2,1,0:T(8,128)(2,1)S(1)} fusion(bf16[4,1,768,128]{3,0,2,1:T(4,128)(2,1)S(1)} %copy-done.5, f32[4,768,768]{1,2,0:T(8,128)} %get-tuple-element.36, f32[4,768]{1,0:T(4,128)S(1)} %get-tuple-element.35), kind=kOutput, calls=%fused_computation.25 | convolution fusion | flops 609091584 | bytes 11022336 | tf_op jit(solution)/shard_map/ipqk,ipkd->ipqd/dot_general | solution.py:26
  253.8 0.8 copy-done
  254.7 4.5 multiply_reduce_fusion
  259.1 10.0 %multiply_convert_fusion = bf16[4,768,768]{1,2,0:T(8,128)(2,1)} fusion(f32[4,768,768]{1,2,0:T(8,128)} %get-tuple-element.38, f32[4,768]{1,0:T(4,128)S(1)} %get-tuple-element.37, f32[4,768,768]{1,2,0:T(8,128)} %get-tuple-element.36, f32[4,768]{1,0:T(4,128)S(1)} %get-tuple-element.35), kind=kLoop, calls=%fused_computation.6 | loop fusion | flops 9437184 | bytes 23617536 | tf_op jit(solution)/shard_map/convert_element_type | solution.py:31
  269.2 4.2 multiply_convert_fusion.2
  273.4 1.4 multiply_convert_fusion.1
  274.8 5.1 %fusion.15 = bf16[4,768,128]{2,1,0:T(8,128)(2,1)S(1)} fusion(bf16[4,1,768,128]{3,0,2,1:T(4,128)(2,1)S(1)} %copy-done.2, f32[4,768,768]{1,2,0:T(8,128)} %get-tuple-element.36, f32[4,768]{1,0:T(4,128)S(1)} %get-tuple-element.35), kind=kOutput, calls=%fused_computation.26 | convolution fusion | flops 609091584 | bytes 11022336 | tf_op jit(solution)/shard_map/ipqk,ipqd->ipkd/dot_general | solution.py:38
  279.9 0.6 copy.111
  280.5 0.6 copy.114
  281.1 0.6 copy.115
  281.8 0.6 copy.116
  282.4 3.6 maximum_bitcast_fusion
  286.0 5.4 %all-to-all-start.2 = ((bf16[64,4,12,512]{3,1,2,0:T(4,128)(2,1)}), bf16[64,4,12,512]{3,1,2,0:T(4,128)(2,1)S(1)}, u32[]{:S(2)}, u32[]{:S(2)}) async-start(bf16[64,4,12,512]{3,1,2,0:T(4,128)(2,1)} %maximum_bitcast_fusion), calls=%async_computation.2 | async-start | bytes 6291456 | tf_op jit(solution)/shard_map/all_to_all | solution.py:104
  291.5 73.7 %all-to-all-done.2 = bf16[64,4,12,512]{3,1,2,0:T(4,128)(2,1)S(1)} async-done(((bf16[64,4,12,512]{3,1,2,0:T(4,128)(2,1)}), bf16[64,4,12,512]{3,1,2,0:T(4,128)(2,1)S(1)}, u32[]{:S(2)}, u32[]{:S(2)}) %all-to-all-start.2) | async-done | bytes 3145760 | tf_op jit(solution)/shard_map/all_to_all | solution.py:104
  365.1 16.0 %gather_fusion.1 = bf16[1536,512]{1,0:T(8,128)(2,1)} fusion(bf16[64,4,12,512]{3,1,2,0:T(4,128)(2,1)S(1)} %all-to-all-done.2, s32[1536]{0:T(1024)S(1)} %reshape.267), kind=kCustom, calls=%fused_computation.1 | custom fusion | bytes 3164160 | tf_op jit(solution)/shard_map/gather | solution.py:105
  381.2 1.9 copy.117
  383.1 0.2 fusion.34
  383.3 6.7 %fusion.36 = f32[384,4096]{1,0:T(8,128)} fusion(bf16[384,512]{0,1:T(8,128)(2,1)S(1)} %bitcast.118, bf16[512,4096]{0,1:T(8,128)(2,1)} %all-gather.5.cloned.1.call-done), kind=kOutput, calls=%fused_computation.74 | convolution fusion | flops 1610612736 | bytes 10878976 | tf_op jit(solution)/shard_map/dot_general | solution.py:110
  390.0 0.9 copy.118
  391.0 0.9 copy.119
  391.9 0.9 copy.120
  392.9 60.1 %reduce-scatter.2.cloned.1.call-done = f32[384,1024]{1,0:T(8,128)} async-done(((f32[384,4096]{1,0:T(8,128)}), f32[384,1024]{1,0:T(8,128)}) %reduce-scatter.2.cloned.1.call-update) | async-done | bytes 1572880 | tf_op jit(solution)/shard_map/reduce_scatter | solution.py:111
  452.9 2.4 convert_element_type.59
  (50 shorter events, 1.4 us)
Async XLA Ops:
  7.2 19.4 %copy-start.11 = (s32[3]{0:T(128)S(1)}, s32[3]{0:T(128)}, u32[]{:S(2)}) copy-start(s32[3]{0:T(128)} %constant.68) | copy-start | bytes 40
  7.2 19.5 %copy-start.10 = (s32[3]{0:T(128)S(1)}, s32[3]{0:T(128)}, u32[]{:S(2)}) copy-start(s32[3]{0:T(128)} %constant.71) | copy-start | bytes 40
  7.2 19.3 %copy-start.9 = (s32[4,384,1]{1,2,0:T(1,128)S(1)}, s32[4,384,1]{1,2,0:T(1,128)}, u32[]{:S(2)}) copy-start(s32[4,384,1]{1,2,0:T(1,128)} %param.11) | copy-start | bytes 18436
  7.2 19.6 %copy-start.6 = (bf16[384,512]{1,0:T(8,128)(2,1)S(1)}, bf16[384,512]{1,0:T(8,128)(2,1)}, u32[]{:S(2)}) copy-start(bf16[384,512]{1,0:T(8,128)(2,1)} %param.8) | copy-start | bytes 1179652
  7.2 19.8 %copy-start.7 = (bf16[384,512]{1,0:T(8,128)(2,1)S(1)}, bf16[384,512]{1,0:T(8,128)(2,1)}, u32[]{:S(2)}) copy-start(bf16[384,512]{1,0:T(8,128)(2,1)} %param.6) | copy-start | bytes 1179652
  7.2 20.0 %copy-start.8 = (bf16[384,512]{1,0:T(8,128)(2,1)S(1)}, bf16[384,512]{1,0:T(8,128)(2,1)}, u32[]{:S(2)}) copy-start(bf16[384,512]{1,0:T(8,128)(2,1)} %param.7) | copy-start | bytes 1179652
  7.2 47.8 %all-gather.3.cloned.1.call-start = ((), (), s32[]{:S(2)}) async-start(), calls=%async_computation.4 | async-start | bytes 3932160 | tf_op jit(solution)/shard_map/all_gather | solution.py:77
  8.0 127.9 %all-gather.5.cloned.1.call-start = ((), (), s32[]{:S(2)}) async-start(), calls=%async_computation.5 | async-start | bytes 4259840 | tf_op jit(solution)/shard_map/all_gather | solution.py:76
  14.5 140.2 %all-to-all-start = ((bf16[64,4,1]{1,2,0:T(2,128)(2,1)}), bf16[64,4,1]{1,2,0:T(2,128)(2,1)S(1)}, u32[]{:S(2)}, u32[]{:S(2)}) async-start(bf16[64,4,1]{1,2,0:T(2,128)(2,1)} %copy.93), calls=%async_computation | async-start | bytes 65536 | tf_op jit(solution)/shard_map/all_to_all | solution.py:101
  154.7 81.4 %all-to-all-start.1 = ((bf16[64,4,12,512]{3,1,2,0:T(4,128)(2,1)}), bf16[64,4,12,512]{3,1,2,0:T(4,128)(2,1)S(1)}, u32[]{:S(2)}, u32[]{:S(2)}) async-start(bf16[64,4,12,512]{3,1,2,0:T(4,128)(2,1)} %bitcast.103), calls=%async_computation.1 | async-start | bytes 6291456 | tf_op jit(solution)/shard_map/all_to_all | solution.py:100
  238.6 9.6 %copy-start.5 = (bf16[4,1,768,128]{3,0,2,1:T(4,128)(2,1)S(1)}, bf16[4,1,768,128]{3,0,2,1:T(4,128)(2,1)}, u32[]{:S(2)}) copy-start(bf16[4,1,768,128]{3,0,2,1:T(4,128)(2,1)} %get-tuple-element.22) | copy-start | bytes 2359300
  248.2 6.4 %copy-start = (f32[4,768,768]{1,2,0:T(8,128)S(1)}, f32[4,768,768]{1,2,0:T(8,128)}, u32[]{:S(2)}) copy-start(f32[4,768,768]{1,2,0:T(8,128)} %get-tuple-element.36) | copy-start | bytes 28311556
  248.2 6.5 %copy-start.2 = (bf16[4,1,768,128]{3,0,2,1:T(4,128)(2,1)S(1)}, bf16[4,1,768,128]{3,0,2,1:T(4,128)(2,1)}, u32[]{:S(2)}) copy-start(bf16[4,1,768,128]{3,0,2,1:T(4,128)(2,1)} %get-tuple-element.25) | copy-start | bytes 2359300
  259.1 10.0 %copy-start.4 = (bf16[4,1,768,128]{3,0,2,1:T(4,128)(2,1)S(1)}, bf16[4,1,768,128]{3,0,2,1:T(4,128)(2,1)}, u32[]{:S(2)}) copy-start(bf16[4,1,768,128]{3,0,2,1:T(4,128)(2,1)} %get-tuple-element.23) | copy-start | bytes 2359300
  269.2 4.2 copy-start.1
  269.2 4.3 copy-start.3
  286.0 79.2 %all-to-all-start.2 = ((bf16[64,4,12,512]{3,1,2,0:T(4,128)(2,1)}), bf16[64,4,12,512]{3,1,2,0:T(4,128)(2,1)S(1)}, u32[]{:S(2)}, u32[]{:S(2)}) async-start(bf16[64,4,12,512]{3,1,2,0:T(4,128)(2,1)} %maximum_bitcast_fusion), calls=%async_computation.2 | async-start | bytes 6291456 | tf_op jit(solution)/shard_map/all_to_all | solution.py:104
  291.4 161.5 %reduce-scatter.2.cloned.1.call-start = ((), (), s32[]{:S(2)}) async-start(), calls=%async_computation.6 | async-start | bytes 7864320 | tf_op jit(solution)/shard_map/reduce_scatter | solution.py:111
Sparse Core Ops, SparseCore 0:
  9.9 45.0 all-gather.2
  57.8 78.0 all-gather.4
  390.2 62.7 reduce-scatter.1
where the time goes:
time: 463 us; the launch traced here: 462 us
  waiting for transfers between devices  312 us (67%)
  local copies, waits for them, and re-layouts  45.6 us (10%)
  matrix products  42 us (9%)
  starting transfers between devices  25.2 us (5%)
  other arithmetic  22.6 us (5%)
  between operations  14.1 us (3%)
    all_gather x1, waiting for transfers between devices, local(): weight_full = lax.all_gather(out_weight, 'seq', axis=1, tiled=True)  80.8 us
    all_to_all x1, waiting for transfers between devices, local(): back = lax.all_to_all(done, 'seq', split_axis=0, concat_axis=0, tiled=True)  73.7 us
    all_to_all x1, waiting for transfers between devices, local(): lax.all_to_all(payload, 'seq', split_axis=0, concat_axis=0, tiled=True)  68.8 us
    reduce_scatter x1, waiting for transfers between devices, local(): lax.psum_scatter(partial_sums, 'head', scatter_dimension=1, tiled=True)  60.1 us
    all_gather x1, waiting for transfers between devices, local(): grad_full = lax.all_gather(mixed_grad, 'head', axis=1, tiled=True)  27.5 us
    gather x2, local copies, waits for them, and re-layouts, local(): fetched = back[owner, head_index, local_slot].transpose(1, 0, 2)  17.9 us
    unnamed x34, local copies, waits for them, and re-layouts  17 us
    all_to_all x1, starting transfers between devices, local(): lax.all_to_all(tallies, 'seq', split_axis=0, concat_axis=0, tiled=True)  12 us
  transfers between devices with their start and end apart: 6, of which 5 were waited for; matrix products, arithmetic and copies ran while one was open for 7% of the time, Pallas kernels for 0%

commit v1 on v0

v1 whole, which is shorter than its diff:
```python
import functools
import math

import jax
import jax.numpy as jnp
from jax import lax
from jax.experimental import pallas as pl
from jax.experimental.pallas import tpu as pltpu
from jax.sharding import PartitionSpec as P

HD = 128
CLUSTERS = 64
CAP = 12
EMPTY_MARK = 128.0
SCALE = 1.0 / math.sqrt(HD)
LOG2E = math.log2(math.e)

VMEM = pl.BlockSpec(memory_space=pltpu.VMEM)
SMEM = pl.BlockSpec(memory_space=pltpu.SMEM)
PARAMS = pltpu.CompilerParams(vmem_limit_bytes=56 * 1024 * 1024)


def dot_nt(a, b):
    return lax.dot_general(a, b, (((1,), (1,)), ((), ())), preferred_element_type=jnp.float32)


def dot_tn(a, b):
    return lax.dot_general(a, b, (((0,), (0,)), ((), ())), preferred_element_type=jnp.float32)


def dot_nn(a, b):
    return jnp.dot(a, b, preferred_element_type=jnp.float32)


def head_cols(h):
    return pl.ds(h * HD, HD)


def slot_onehot(slot_row):
    tokens = slot_row.shape[1]
    place = lax.broadcasted_iota(jnp.int32, (CLUSTERS * CAP, tokens), 0)
    return jnp.where(place == slot_row, 1.0, 0.0).astype(jnp.bfloat16)


def token_onehot(slot_row):
    tokens = slot_row.shape[1]
    spread = jnp.broadcast_to(slot_row.astype(jnp.float32), (HD, tokens)).T
    lane = lax.broadcasted_iota(jnp.int32, (tokens, HD), 1).astype(jnp.float32)
    pieces = [
        jnp.where(spread == lane + float(start), 1.0, 0.0).astype(jnp.bfloat16)
        for start in range(0, CLUSTERS * CAP, HD)
    ]
    return jnp.concatenate(pieces, axis=1)


def pack_kernel(ids_ref, q_ref, k_ref, v_ref, out_ref, slots_ref, wide):
    heads, tokens = ids_ref.shape
    rows = CLUSTERS * CAP
    before = (
        lax.broadcasted_iota(jnp.int32, (tokens, tokens), 0)
        < lax.broadcasted_iota(jnp.int32, (tokens, tokens), 1)
    )
    before = jnp.where(before, 1.0, 0.0).astype(jnp.bfloat16)
    cluster = lax.broadcasted_iota(jnp.int32, (CLUSTERS, tokens), 0)
    ones = jnp.ones((tokens, HD), jnp.bfloat16)
    first_lane = lax.broadcasted_iota(jnp.int32, (rows, HD), 1) == 0
    for h in range(heads):
        ids = ids_ref[h : h + 1, :]
        named = jnp.where(cluster == ids, 1.0, 0.0)
        earlier = dot_nn(named.astype(jnp.bfloat16), before)
        rank = jnp.sum(named * earlier, axis=0, keepdims=True)
        slot = ids * CAP + rank.astype(jnp.int32)
        slots_ref[h : h + 1, :] = slot
        data = jnp.concatenate(
            [q_ref[:, head_cols(h)], k_ref[:, head_cols(h)], v_ref[:, head_cols(h)], ones], axis=1
        )
        placed = dot_nn(slot_onehot(slot), data)
        used = placed[:, 3 * HD :]
        mark = jnp.where(first_lane, (1.0 - used) * EMPTY_MARK, 0.0)
        where = pl.ds(h, rows, stride=heads)
        wide[0, where, :] = placed[:, :HD]
        wide[1, where, :] = placed[:, HD : 2 * HD] + mark
        wide[2, where, :] = placed[:, 2 * HD : 3 * HD]
    for t in range(3):
        out_ref[:, t * HD : (t + 1) * HD] = wide[t].astype(jnp.bfloat16)


def grad_kernel(y_ref, slots_ref, m0, m1, m2, m3, wt_ref, out_ref, wide):
    heads = slots_ref.shape[0]
    rows = CLUSTERS * CAP
    y = y_ref[0]
    total = None
    for d, m_ref in enumerate((m0, m1, m2, m3)):
        cols = m_ref.shape[1]
        start = pl.multiple_of(lax.rem(y + (4 - d), 4) * cols, cols)
        part = dot_nn(m_ref[...], wt_ref[pl.ds(start, cols), :])
        total = part if total is None else total + part
    grad = total.astype(jnp.bfloat16)
    for h in range(heads):
        placed = dot_nn(slot_onehot(slots_ref[h : h + 1, :]), grad[:, h * HD : (h + 1) * HD])
        wide[pl.ds(h, rows, stride=heads), :] = placed
    out_ref[...] = wide[...].astype(jnp.bfloat16)


def forward_kernel(x_ref, att_ref, heads_ref, probs_ref, wide, back):
    heads = pl.num_programs(0)
    rows = CLUSTERS * CAP
    h = pl.program_id(0)

    @pl.when(h == 0)
    def _():
        for t in range(3):
            wide[t] = x_ref[:, t * HD : (t + 1) * HD].astype(jnp.float32)

    where = pl.ds(h, rows, stride=4)
    q = wide[0, where, :].astype(jnp.bfloat16)
    k_wide = wide[1, where, :]
    k = k_wide.astype(jnp.bfloat16)
    v = wide[2, where, :].astype(jnp.bfloat16)
    heads_ref[0] = q
    heads_ref[1] = k
    heads_ref[2] = v
    bias = jnp.where(k_wide[:, :1] > EMPTY_MARK / 2, -1e30, 0.0)
    scores = dot_nt(k, q) + bias
    top = jnp.max(scores, axis=0, keepdims=True)
    weights = jnp.exp2((scores - top) * (SCALE * LOG2E))
    probs = weights * (1.0 / jnp.sum(weights, axis=0, keepdims=True))
    probs_ref[0] = probs
    back[where, :] = dot_tn(v, probs.astype(jnp.bfloat16)).T

    @pl.when(h == heads - 1)
    def _():
        att_ref[...] = back[...].astype(jnp.bfloat16)


def backward_kernel(g_ref, heads_ref, probs_ref, out_ref, wide, back):
    heads = pl.num_programs(0)
    rows = CLUSTERS * CAP
    h = pl.program_id(0)

    @pl.when(h == 0)
    def _():
        wide[...] = g_ref[...].astype(jnp.float32)

    where = pl.ds(h, rows, stride=4)
    g = wide[where, :].astype(jnp.bfloat16)
    q, k, v = heads_ref[0], heads_ref[1], heads_ref[2]
    probs = probs_ref[0]
    dprobs = dot_nt(v, g)
    delta = jnp.sum(probs * dprobs, axis=0, keepdims=True)
    dscores = (probs * (dprobs - delta)).astype(jnp.bfloat16)
    back[0, where, :] = dot_tn(k, dscores).T * SCALE
    back[1, where, :] = dot_nn(dscores, q) * SCALE
    back[2, where, :] = dot_nn(probs.astype(jnp.bfloat16), g)

    @pl.when(h == heads - 1)
    def _():
        for t in range(3):
            out_ref[:, t * HD : (t + 1) * HD] = back[t].astype(jnp.bfloat16)


def mixed_kernel(y_ref, slots_ref, att_ref, wt_ref, own_ref, s1, s2, s3, wide):
    heads = slots_ref.shape[0]
    rows = CLUSTERS * CAP
    y = y_ref[0]
    wide[...] = att_ref[...].astype(jnp.float32)
    pieces = []
    for h in range(heads):
        held = wide[pl.ds(h, rows, stride=heads), :].astype(jnp.bfloat16)
        pieces.append(dot_nn(token_onehot(slots_ref[h : h + 1, :]), held).astype(jnp.bfloat16))
    att = jnp.concatenate(pieces, axis=1)
    for d, s_ref in enumerate((own_ref, s1, s2, s3)):
        cols = s_ref.shape[1]
        start = pl.multiple_of(lax.rem(y + d, 4) * cols, cols)
        s_ref[...] = dot_nt(att, wt_ref[pl.ds(start, cols), :]).astype(s_ref.dtype)


def unpack_kernel(slots_ref, x_ref, dq_ref, dk_ref, dv_ref, wide):
    heads = slots_ref.shape[0]
    rows = CLUSTERS * CAP
    for t in range(3):
        wide[t] = x_ref[:, t * HD : (t + 1) * HD].astype(jnp.float32)
    for h in range(heads):
        where = pl.ds(h, rows, stride=heads)
        held = jnp.concatenate(
            [wide[t, where, :].astype(jnp.bfloat16) for t in range(3)], axis=1
        )
        got = dot_nn(token_onehot(slots_ref[h : h + 1, :]), held).astype(jnp.bfloat16)
        for t, ref in enumerate((dq_ref, dk_ref, dv_ref)):
            ref[:, head_cols(h)] = got[:, t * HD : (t + 1) * HD]


def call(kernel, out, scratch, count, smem_first=False):
    specs = [VMEM] * count
    if smem_first:
        specs[0] = SMEM
    return pl.pallas_call(
        kernel,
        out_shape=out,
        in_specs=specs,
        out_specs=jax.tree.map(lambda _: VMEM, out),
        scratch_shapes=scratch,
        compiler_params=PARAMS,
    )


def sds(shape, dtype=jnp.bfloat16):
    return jax.ShapeDtypeStruct(shape, dtype)


def exchange(x):
    return lax.all_to_all(x, "seq", split_axis=0, concat_axis=0, tiled=True)


def local(query, key, value, mixed_grad, out_weight, cluster):
    tokens = query.shape[0]
    heads = cluster.shape[0]
    rows = CLUSTERS * CAP
    slots_all = heads * rows
    y = lax.axis_index("head").astype(jnp.int32).reshape(1)

    def turn(x, d):
        return lax.ppermute(x, "head", [(i, (i + d) % 4) for i in range(4)])

    wt = lax.all_gather(out_weight.T, "seq", axis=0, tiled=True)
    grads = [mixed_grad] + [turn(mixed_grad, d) for d in (1, 2, 3)]

    payload, slots = call(
        pack_kernel,
        (sds((slots_all, 3 * HD)), sds((heads, tokens), jnp.int32)),
        [pltpu.VMEM((3, slots_all, HD), jnp.float32)],
        4,
    )(cluster.reshape(heads, tokens), query, key, value)
    arrived = exchange(payload)

    att, held, probs = pl.pallas_call(
        forward_kernel,
        grid=(heads,),
        out_shape=(
            sds((slots_all, HD)),
            sds((heads * 3, rows, HD)),
            sds((heads, rows, rows), jnp.float32),
        ),
        in_specs=[pl.BlockSpec((slots_all, 3 * HD), lambda h: (0, 0))],
        out_specs=(
            pl.BlockSpec((slots_all, HD), lambda h: (0, 0)),
            pl.BlockSpec((3, rows, HD), lambda h: (h, 0, 0)),
            pl.BlockSpec((1, rows, rows), lambda h: (h, 0, 0)),
        ),
        scratch_shapes=[
            pltpu.VMEM((3, slots_all, HD), jnp.float32),
            pltpu.VMEM((slots_all, HD), jnp.float32),
        ],
        compiler_params=PARAMS,
    )(arrived)

    grad_payload = call(
        grad_kernel,
        sds((slots_all, HD)),
        [pltpu.VMEM((slots_all, HD), jnp.float32)],
        7,
        smem_first=True,
    )(y, slots, *grads, wt)
    att_back = exchange(att)
    grad_arrived = exchange(grad_payload)

    done = pl.pallas_call(
        backward_kernel,
        grid=(heads,),
        out_shape=sds((slots_all, 3 * HD)),
        in_specs=[
            pl.BlockSpec((slots_all, HD), lambda h: (0, 0)),
            pl.BlockSpec((3, rows, HD), lambda h: (h, 0, 0)),
            pl.BlockSpec((1, rows, rows), lambda h: (h, 0, 0)),
        ],
        out_specs=pl.BlockSpec((slots_all, 3 * HD), lambda h: (0, 0)),
        scratch_shapes=[
            pltpu.VMEM((slots_all, HD), jnp.float32),
            pltpu.VMEM((3, slots_all, HD), jnp.float32),
        ],
        compiler_params=PARAMS,
    )(grad_arrived, held, probs)
    back = exchange(done)

    cols = mixed_grad.shape[1]
    own, *sends = call(
        mixed_kernel,
        (sds((tokens, cols), jnp.float32),) + (sds((tokens, cols)),) * 3,
        [pltpu.VMEM((slots_all, HD), jnp.float32)],
        4,
        smem_first=True,
    )(y, slots, att_back, wt)
    mixed = own
    for d, part in zip((1, 2, 3), sends):
        mixed = mixed + turn(part, d).astype(jnp.float32)
    mixed = mixed.astype(jnp.bfloat16)

    query_grad, key_grad, value_grad = call(
        unpack_kernel,
        (sds((tokens, heads * HD)),) * 3,
        [pltpu.VMEM((3, slots_all, HD), jnp.float32)],
        2,
    )(slots, back)
    return (mixed, query_grad, key_grad, value_grad)


def solution(mesh):
    placed = (
        P("seq", "head"),
        P("seq", "head"),
        P("seq", "head"),
        P("seq", "head"),
        P("head", "seq"),
        P("head", "seq", None),
    )
    return jax.shard_map(
        local,
        mesh=mesh,
        in_specs=placed,
        out_specs=(P("seq", "head"), P("seq", "head"), P("seq", "head"), P("seq", "head")),
        check_vma=False,
    )
```

time: 463 us -> 246 us (0.53)
  waiting for transfers between devices: 312 us -> 138 us
  Pallas kernels: 0 us -> 43 us
  matrix products: 42 us -> 0 us
  local copies, waits for them, and re-layouts: 45.6 us -> 3.61 us
  other arithmetic: 22.6 us -> 2.86 us
  starting transfers between devices: 25.2 us -> 43.6 us
    all_to_all x3 -> x4, waiting for transfers between devices: 143 us -> 34.5 us  [exchange(): return lax.all_to_all(x, 'seq', split_axis=0, concat_axis=0, tiled=True)]
    all_gather x2 -> x1, waiting for transfers between devices: 108 us -> 35.5 us  [local(): wt = lax.all_gather(out_weight.T, 'seq', axis=0, tiled=True)]
    ppermute x0 -> x6, waiting for transfers between devices: none -> 67.1 us  [turn(): return lax.ppermute(x, 'head', [(i, (i + d) % 4) for i in range(4)])]
    reduce_scatter x1 -> x0, waiting for transfers between devices: 60.1 us -> none  [local(): lax.psum_scatter(partial_sums, 'head', scatter_dimension=1, tiled=True)]
    pallas_call x0 -> x6, Pallas kernels: none -> 43 us  [the longest x1 10.6 us: local(): pl.pallas_call(backward_kernel, grid=(heads,), out_shape=sds((slots_all,...]
    dot_general x7 -> x0, matrix products: 32.4 us -> none  [the longest x1 6.74 us: local(): jnp.dot(attended, weight_full, preferred_element_type=jnp.float32)]
    gather x3 -> x0, local copies, waits for them, and re-layouts: 20.2 us -> none  [the longest x2 17.9 us: local(): fetched = back[owner, head_index, local_slot].transpose(1, 0, 2)]
    unnamed x34 -> x11, local copies, waits for them, and re-layouts: 17 us -> 3.61 us
  transfers between devices with their start and end apart: 6 -> 11, of which waited for: 5 -> 8; matrix products, arithmetic and copies ran while one was open for 7% -> 2% of each run, Pallas kernels for 0% -> 16%
where the time goes in v1:
time: 246 us; the launch traced here: 245 us
  waiting for transfers between devices  138 us (56%)
  starting transfers between devices  43.6 us (18%)
  Pallas kernels  43 us (17%)
  between operations  14.1 us (6%)
  local copies, waits for them, and re-layouts  3.61 us (1%)
  other arithmetic  2.86 us (1%)
    ppermute x6, waiting for transfers between devices, turn(): return lax.ppermute(x, 'head', [(i, (i + d) % 4) for i in range(4)])  67.1 us
    all_gather x1, waiting for transfers between devices, local(): wt = lax.all_gather(out_weight.T, 'seq', axis=0, tiled=True)  35.5 us
    all_to_all x4, waiting for transfers between devices, exchange(): return lax.all_to_all(x, 'seq', split_axis=0, concat_axis=0, tiled=True)  34.5 us
    all_to_all x4, starting transfers between devices, exchange(): return lax.all_to_all(x, 'seq', split_axis=0, concat_axis=0, tiled=True)  32.1 us
    ppermute x6, starting transfers between devices, turn(): return lax.ppermute(x, 'head', [(i, (i + d) % 4) for i in range(4)])  11.4 us
    pallas_call x1, Pallas kernels, local(): pl.pallas_call(backward_kernel, grid=(heads,), out_shape=sds((slots_all,...  10.6 us
    pallas_call x1, Pallas kernels, local(): pl.pallas_call(forward_kernel, grid=(heads,), out_shape=(sds((slots_all,...  9.95 us
    pallas_call x1, Pallas kernels, local(): call(grad_kernel, sds((slots_all, HD)), [pltpu.VMEM((slots_all, HD), jnp....  6.69 us
  transfers between devices with their start and end apart: 11, of which 8 were waited for; matrix products, arithmetic and copies ran while one was open for 2% of the time, Pallas kernels for 16%

profile of v1, /device:TPU:2, one launch (start us, length us, event | category | flops | bytes accessed | tf_op | source)
XLA Modules:
  0.0 244.9 jit_solution(6507055959900129972)
XLA Ops:
  7.2 0.0 all-gather.2.cloned.1.call-start
  7.2 0.7 all-gather.2.cloned.1.call-update
  7.9 1.3 copy.12
  9.2 5.6 %shard_map.93 = (bf16[3072,384]{1,0:T(8,128)(2,1)}, s32[4,384]{1,0:T(4,128)}) custom-call(s32[4,384]{1,0:T(4,128)} %bitcast.22, bf16[384,512]{1,0:T(8,128)(2,1)} %q_ref.1, bf16[384,512]{1,0:T(8,128)(2,1)} %k_ref.1, bf16[384,512]{1,0:T(8,128)(2,1)} %v_ref.1), custom_call_target="tpu_custom_call" | custom-call | tf_op jit(solution)/shard_map/pallas_call | solution.py:228
  14.7 0.0 copy-start.4
  14.7 12.2 %all-to-all-start = ((bf16[64,48,384]{2,1,0:T(8,128)(2,1)}), bf16[64,48,384]{2,1,0:T(8,128)(2,1)S(1)}, u32[]{:S(2)}, u32[]{:S(2)}) async-start(bf16[64,48,384]{2,1,0:T(8,128)(2,1)} %bitcast.19), calls=%async_computation | async-start | bytes 4718592 | tf_op jit(solution)/shard_map/all_to_all | solution.py:212
  26.9 0.0 copy-done.4
  26.9 1.7 collective-permute-start.3
  28.6 2.9 %collective-permute-start.4 = (bf16[384,1024]{1,0:T(8,128)(2,1)S(1)}, bf16[384,1024]{1,0:T(8,128)(2,1)}, u32[]{:S(2)}, u32[]{:S(2)}) collective-permute-start(bf16[384,1024]{1,0:T(8,128)(2,1)S(1)} %copy-done.4), channel_id=1, source_target_pairs={{0,2},{1,3},{2,0},{3,1},{4,6},{5,7},{6,4},{7,5},{8,10},{9,11},{10,... | collective-permute-start | bytes 2359304 | tf_op jit(solution)/shard_map/ppermute | solution.py:223
  31.5 1.3 collective-permute-start.5
  32.8 15.1 %collective-permute-done.3.m1 = bf16[384,1024]{1,0:T(8,128)(2,1)} collective-permute-done((bf16[384,1024]{1,0:T(8,128)(2,1)S(1)}, bf16[384,1024]{1,0:T(8,128)(2,1)}, u32[]{:S(2)}, u32[]{:S(2)}) %collective-permute-start.3) | collective-permute-done | bytes 786464 | tf_op jit(solution)/shard_map/ppermute | solution.py:223
  48.0 18.0 %collective-permute-done.4.m2 = bf16[384,1024]{1,0:T(8,128)(2,1)} collective-permute-done((bf16[384,1024]{1,0:T(8,128)(2,1)S(1)}, bf16[384,1024]{1,0:T(8,128)(2,1)}, u32[]{:S(2)}, u32[]{:S(2)}) %collective-permute-start.4) | collective-permute-done | bytes 786464 | tf_op jit(solution)/shard_map/ppermute | solution.py:223
  66.0 0.0 collective-permute-done.5.m3
  66.0 35.5 %all-gather.2.cloned.1.call-done.wt_ref = bf16[4096,512]{1,0:T(8,128)(2,1)} async-done(((bf16[64,512]{1,0:T(8,128)(2,1)}), bf16[4096,512]{1,0:T(8,128)(2,1)}) %all-gather.2.cloned.1.call-update) | async-done | bytes 4194320 | tf_op jit(solution)/shard_map/all_gather | solution.py:225
  101.5 6.7 %shard_map.96 = bf16[3072,128]{1,0:T(8,128)(2,1)} custom-call(s32[1]{0:T(128)} %bitcast.y_ref, s32[4,384]{1,0:T(4,128)} %get-tuple-element.16.slots_ref, bf16[384,1024]{1,0:T(8,128)(2,1)} %m0.1, bf16[384,1024]{1,0:T(8,128)(2,1)} %collective-permute-done.3.m1, bf16[384,1024]{1,0:T(8,128)(2,1)} %collective-permute-done.4.m2, ...), custom_call_target="tpu_custom_call" | custom-call | tf_op jit(solution)/shard_map/pallas_call | solution.py:257
  108.2 0.0 all-to-all-done
  108.2 0.0 copy-start
  108.2 8.3 %all-to-all-start.2 = ((bf16[64,48,128]{2,1,0:T(8,128)(2,1)}), bf16[64,48,128]{2,1,0:T(8,128)(2,1)S(1)}, u32[]{:S(2)}, u32[]{:S(2)}) async-start(bf16[64,48,128]{2,1,0:T(8,128)(2,1)} %bitcast.17), calls=%async_computation.2 | async-start | bytes 1572864 | tf_op jit(solution)/shard_map/all_to_all | solution.py:212
  116.5 0.0 copy-done
  116.5 10.0 %shard_map.94 = (bf16[3072,128]{1,0:T(8,128)(2,1)}, bf16[12,768,128]{2,1,0:T(8,128)(2,1)}, f32[4,768,768]{2,1,0:T(8,128)}) custom-call(bf16[3072,384]{1,0:T(8,128)(2,1)} %bitcast.14), custom_call_target="tpu_custom_call" | custom-call | tf_op jit(solution)/shard_map/pallas_call | solution.py:236
  126.5 13.2 %all-to-all-done.2 = bf16[64,48,128]{2,1,0:T(8,128)(2,1)S(1)} async-done(((bf16[64,48,128]{2,1,0:T(8,128)(2,1)}), bf16[64,48,128]{2,1,0:T(8,128)(2,1)S(1)}, u32[]{:S(2)}, u32[]{:S(2)}) %all-to-all-start.2) | async-done | bytes 786464 | tf_op jit(solution)/shard_map/all_to_all | solution.py:212
  139.7 0.0 copy-start.2
  139.7 5.8 %all-to-all-start.1 = ((bf16[64,48,128]{2,1,0:T(8,128)(2,1)}), bf16[64,48,128]{2,1,0:T(8,128)(2,1)S(1)}, u32[]{:S(2)}, u32[]{:S(2)}) async-start(bf16[64,48,128]{2,1,0:T(8,128)(2,1)} %bitcast.20), calls=%async_computation.1 | async-start | bytes 1572864 | tf_op jit(solution)/shard_map/all_to_all | solution.py:212
  145.5 0.0 copy-done.2
  145.5 10.6 %shard_map.97 = bf16[3072,384]{1,0:T(8,128)(2,1)} custom-call(bf16[3072,128]{1,0:T(8,128)(2,1)} %bitcast.16, bf16[12,768,128]{2,1,0:T(8,128)(2,1)} %get-tuple-element.23.heads_ref, f32[4,768,768]{2,1,0:T(8,128)} %get-tuple-element.24.probs_ref), custom_call_target="tpu_custom_call" | custom-call | tf_op jit(solution)/shard_map/pallas_call | solution.py:267
  156.2 12.5 %all-to-all-done.1 = bf16[64,48,128]{2,1,0:T(8,128)(2,1)S(1)} async-done(((bf16[64,48,128]{2,1,0:T(8,128)(2,1)}), bf16[64,48,128]{2,1,0:T(8,128)(2,1)S(1)}, u32[]{:S(2)}, u32[]{:S(2)}) %all-to-all-start.1) | async-done | bytes 786464 | tf_op jit(solution)/shard_map/all_to_all | solution.py:212
  168.7 0.0 copy-start.3
  168.7 0.9 copy-done.3
  169.6 5.8 %all-to-all-start.3 = ((bf16[64,48,384]{2,1,0:T(8,128)(2,1)}), bf16[64,48,384]{2,1,0:T(8,128)(2,1)S(1)}, u32[]{:S(2)}, u32[]{:S(2)}) async-start(bf16[64,48,384]{2,1,0:T(8,128)(2,1)} %bitcast.13), calls=%async_computation.3 | async-start | bytes 4718592 | tf_op jit(solution)/shard_map/all_to_all | solution.py:212
  175.4 5.8 %shard_map.95 = (f32[384,1024]{1,0:T(8,128)}, bf16[384,1024]{1,0:T(8,128)(2,1)}, bf16[384,1024]{1,0:T(8,128)(2,1)}, bf16[384,1024]{1,0:T(8,128)(2,1)}) custom-call(s32[1]{0:T(128)} %bitcast.y_ref, s32[4,384]{1,0:T(4,128)} %get-tuple-element.16.slots_ref, bf16[3072,128]{1,0:T(8,128)(2,1)} %bitcast.18, bf16[4096,512]{1,0:T(8,128)(2,1)} %all-gather.2.cloned.1.call-done.wt_ref), custom_call_target="tpu_custom_call" | custom-call | tf_op jit(solution)/shard_map/pallas_call | solution.py:286
  181.2 1.5 collective-permute-start
  182.7 3.4 %collective-permute-start.1 = (bf16[384,1024]{1,0:T(8,128)(2,1)}, bf16[384,1024]{1,0:T(8,128)(2,1)S(1)}, u32[]{:S(2)}, u32[]{:S(2)}) collective-permute-start(bf16[384,1024]{1,0:T(8,128)(2,1)} %get-tuple-element.21), channel_id=1, source_target_pairs={{0,2},{1,3},{2,0},{3,1},{4,6},{5,7},{6,4},{7,5},{8,10},{9,11},{10,... | collective-permute-start | bytes 2359304 | tf_op jit(solution)/shard_map/ppermute | solution.py:223
  186.1 0.7 collective-permute-start.2
  186.7 15.9 %collective-permute-done = bf16[384,1024]{1,0:T(8,128)(2,1)S(1)} collective-permute-done((bf16[384,1024]{1,0:T(8,128)(2,1)}, bf16[384,1024]{1,0:T(8,128)(2,1)S(1)}, u32[]{:S(2)}, u32[]{:S(2)}) %collective-permute-start) | collective-permute-done | bytes 786464 | tf_op jit(solution)/shard_map/ppermute | solution.py:223
  202.7 18.0 %collective-permute-done.1 = bf16[384,1024]{1,0:T(8,128)(2,1)S(1)} collective-permute-done((bf16[384,1024]{1,0:T(8,128)(2,1)}, bf16[384,1024]{1,0:T(8,128)(2,1)S(1)}, u32[]{:S(2)}, u32[]{:S(2)}) %collective-permute-start.1) | collective-permute-done | bytes 786464 | tf_op jit(solution)/shard_map/ppermute | solution.py:223
  220.7 0.0 collective-permute-done.2
  220.7 2.9 %add_convert_fusion = bf16[384,1024]{1,0:T(8,128)(2,1)} fusion(bf16[384,1024]{1,0:T(8,128)(2,1)S(1)} %collective-permute-done.2, bf16[384,1024]{1,0:T(8,128)(2,1)S(1)} %collective-permute-done.1, f32[384,1024]{1,0:T(8,128)} %get-tuple-element.19, bf16[384,1024]{1,0:T(8,128)(2,1)S(1)} %collective-permute-done), kind=kLoop, calls=%fused_computation | loop fusion | flops 2752512 | bytes 4718592 | tf_op jit(solution)/shard_map/convert_element_type | solution.py:296
  223.6 8.7 %all-to-all-done.3 = bf16[64,48,384]{2,1,0:T(8,128)(2,1)S(1)} async-done(((bf16[64,48,384]{2,1,0:T(8,128)(2,1)}), bf16[64,48,384]{2,1,0:T(8,128)(2,1)S(1)}, u32[]{:S(2)}, u32[]{:S(2)}) %all-to-all-start.3) | async-done | bytes 2359328 | tf_op jit(solution)/shard_map/all_to_all | solution.py:212
  232.3 0.0 copy-start.1
  232.3 1.4 copy-done.1
  233.7 4.3 %shard_map.98 = (bf16[384,512]{1,0:T(8,128)(2,1)}, bf16[384,512]{1,0:T(8,128)(2,1)}, bf16[384,512]{1,0:T(8,128)(2,1)}) custom-call(s32[4,384]{1,0:T(4,128)} %get-tuple-element.16.slots_ref, bf16[3072,384]{1,0:T(8,128)(2,1)} %bitcast.15), custom_call_target="tpu_custom_call" | custom-call | tf_op jit(solution)/shard_map/pallas_call | solution.py:298
Async XLA Ops:
  7.2 94.3 %all-gather.2.cloned.1.call-start = ((), (), s32[]{:S(2)}) async-start(), calls=%async_computation.4 | async-start | bytes 4259840 | tf_op jit(solution)/shard_map/all_gather | solution.py:225
  14.7 12.2 %copy-start.4 = (bf16[384,1024]{1,0:T(8,128)(2,1)S(1)}, bf16[384,1024]{1,0:T(8,128)(2,1)}, u32[]{:S(2)}) copy-start(bf16[384,1024]{1,0:T(8,128)(2,1)} %m0.1) | copy-start | bytes 2359300
  14.7 93.4 %all-to-all-start = ((bf16[64,48,384]{2,1,0:T(8,128)(2,1)}), bf16[64,48,384]{2,1,0:T(8,128)(2,1)S(1)}, u32[]{:S(2)}, u32[]{:S(2)}) async-start(bf16[64,48,384]{2,1,0:T(8,128)(2,1)} %bitcast.19), calls=%async_computation | async-start | bytes 4718592 | tf_op jit(solution)/shard_map/all_to_all | solution.py:212
  26.9 21.0 %collective-permute-start.3 = (bf16[384,1024]{1,0:T(8,128)(2,1)S(1)}, bf16[384,1024]{1,0:T(8,128)(2,1)}, u32[]{:S(2)}, u32[]{:S(2)}) collective-permute-start(bf16[384,1024]{1,0:T(8,128)(2,1)S(1)} %copy-done.4), channel_id=1, source_target_pairs={{0,1},{1,2},{2,3},{3,0},{4,5},{5,6},{6,7},{7,4},{8,9},{9,10},{10,1... | collective-permute-start | bytes 2359304 | tf_op jit(solution)/shard_map/ppermute | solution.py:223
  28.6 37.4 %collective-permute-start.4 = (bf16[384,1024]{1,0:T(8,128)(2,1)S(1)}, bf16[384,1024]{1,0:T(8,128)(2,1)}, u32[]{:S(2)}, u32[]{:S(2)}) collective-permute-start(bf16[384,1024]{1,0:T(8,128)(2,1)S(1)} %copy-done.4), channel_id=1, source_target_pairs={{0,2},{1,3},{2,0},{3,1},{4,6},{5,7},{6,4},{7,5},{8,10},{9,11},{10,... | collective-permute-start | bytes 2359304 | tf_op jit(solution)/shard_map/ppermute | solution.py:223
  31.5 34.5 %collective-permute-start.5 = (bf16[384,1024]{1,0:T(8,128)(2,1)S(1)}, bf16[384,1024]{1,0:T(8,128)(2,1)}, u32[]{:S(2)}, u32[]{:S(2)}) collective-permute-start(bf16[384,1024]{1,0:T(8,128)(2,1)S(1)} %copy-done.4), channel_id=1, source_target_pairs={{0,3},{1,0},{2,1},{3,2},{4,7},{5,4},{6,5},{7,6},{8,11},{9,8},{10,9... | collective-permute-start | bytes 2359304 | tf_op jit(solution)/shard_map/ppermute | solution.py:223
  108.2 8.3 %copy-start = (bf16[64,48,384]{2,1,0:T(8,128)(2,1)}, bf16[64,48,384]{2,1,0:T(8,128)(2,1)S(1)}, u32[]{:S(2)}) copy-start(bf16[64,48,384]{2,1,0:T(8,128)(2,1)S(1)} %all-to-all-done) | copy-start | bytes 7077892
  108.2 31.5 %all-to-all-start.2 = ((bf16[64,48,128]{2,1,0:T(8,128)(2,1)}), bf16[64,48,128]{2,1,0:T(8,128)(2,1)S(1)}, u32[]{:S(2)}, u32[]{:S(2)}) async-start(bf16[64,48,128]{2,1,0:T(8,128)(2,1)} %bitcast.17), calls=%async_computation.2 | async-start | bytes 1572864 | tf_op jit(solution)/shard_map/all_to_all | solution.py:212
  139.7 5.8 %copy-start.2 = (bf16[64,48,128]{2,1,0:T(8,128)(2,1)}, bf16[64,48,128]{2,1,0:T(8,128)(2,1)S(1)}, u32[]{:S(2)}) copy-start(bf16[64,48,128]{2,1,0:T(8,128)(2,1)S(1)} %all-to-all-done.2) | copy-start | bytes 2359300
  139.7 29.0 %all-to-all-start.1 = ((bf16[64,48,128]{2,1,0:T(8,128)(2,1)}), bf16[64,48,128]{2,1,0:T(8,128)(2,1)S(1)}, u32[]{:S(2)}, u32[]{:S(2)}) async-start(bf16[64,48,128]{2,1,0:T(8,128)(2,1)} %bitcast.20), calls=%async_computation.1 | async-start | bytes 1572864 | tf_op jit(solution)/shard_map/all_to_all | solution.py:212
  168.7 0.9 copy-start.3
  169.6 62.7 %all-to-all-start.3 = ((bf16[64,48,384]{2,1,0:T(8,128)(2,1)}), bf16[64,48,384]{2,1,0:T(8,128)(2,1)S(1)}, u32[]{:S(2)}, u32[]{:S(2)}) async-start(bf16[64,48,384]{2,1,0:T(8,128)(2,1)} %bitcast.13), calls=%async_computation.3 | async-start | bytes 4718592 | tf_op jit(solution)/shard_map/all_to_all | solution.py:212
  181.2 21.4 %collective-permute-start = (bf16[384,1024]{1,0:T(8,128)(2,1)}, bf16[384,1024]{1,0:T(8,128)(2,1)S(1)}, u32[]{:S(2)}, u32[]{:S(2)}) collective-permute-start(bf16[384,1024]{1,0:T(8,128)(2,1)} %get-tuple-element.20), channel_id=1, source_target_pairs={{0,1},{1,2},{2,3},{3,0},{4,5},{5,6},{6,7},{7,4},{8,9},{9,10},{10,1... | collective-permute-start | bytes 2359304 | tf_op jit(solution)/shard_map/ppermute | solution.py:223
  182.7 38.0 %collective-permute-start.1 = (bf16[384,1024]{1,0:T(8,128)(2,1)}, bf16[384,1024]{1,0:T(8,128)(2,1)S(1)}, u32[]{:S(2)}, u32[]{:S(2)}) collective-permute-start(bf16[384,1024]{1,0:T(8,128)(2,1)} %get-tuple-element.21), channel_id=1, source_target_pairs={{0,2},{1,3},{2,0},{3,1},{4,6},{5,7},{6,4},{7,5},{8,10},{9,11},{10,... | collective-permute-start | bytes 2359304 | tf_op jit(solution)/shard_map/ppermute | solution.py:223
  186.1 34.6 %collective-permute-start.2 = (bf16[384,1024]{1,0:T(8,128)(2,1)}, bf16[384,1024]{1,0:T(8,128)(2,1)S(1)}, u32[]{:S(2)}, u32[]{:S(2)}) collective-permute-start(bf16[384,1024]{1,0:T(8,128)(2,1)} %get-tuple-element.22), channel_id=1, source_target_pairs={{0,3},{1,0},{2,1},{3,2},{4,7},{5,4},{6,5},{7,6},{8,11},{9,8},{10,9... | collective-permute-start | bytes 2359304 | tf_op jit(solution)/shard_map/ppermute | solution.py:223
  232.3 1.4 copy-start.1
Sparse Core Ops, SparseCore 0:
  10.8 90.6 all-gather.1

commit v2 on v1

--- a/solution.py
+++ b/solution.py
@@ -16,7 +16,6 @@
 LOG2E = math.log2(math.e)
 
 VMEM = pl.BlockSpec(memory_space=pltpu.VMEM)
-SMEM = pl.BlockSpec(memory_space=pltpu.SMEM)
 PARAMS = pltpu.CompilerParams(vmem_limit_bytes=56 * 1024 * 1024)
 
 
@@ -54,7 +53,7 @@
 
 
 def pack_kernel(ids_ref, q_ref, k_ref, v_ref, out_ref, slots_ref, wide):
-    heads, tokens = ids_ref.shape
+    heads, _, tokens = ids_ref.shape
     rows = CLUSTERS * CAP
     before = (
         lax.broadcasted_iota(jnp.int32, (tokens, tokens), 0)
@@ -65,7 +64,7 @@
     ones = jnp.ones((tokens, HD), jnp.bfloat16)
     first_lane = lax.broadcasted_iota(jnp.int32, (rows, HD), 1) == 0
     for h in range(heads):
-        ids = ids_ref[h : h + 1, :]
+        ids = ids_ref[h]
         named = jnp.where(cluster == ids, 1.0, 0.0)
         earlier = dot_nn(named.astype(jnp.bfloat16), before)
         rank = jnp.sum(named * earlier, axis=0, keepdims=True)
@@ -85,12 +84,22 @@
         out_ref[:, t * HD : (t + 1) * HD] = wide[t].astype(jnp.bfloat16)
 
 
-def grad_kernel(y_ref, slots_ref, m0, m1, m2, m3, wt_ref, out_ref, wide):
+def grad_kernel(slots_ref, *refs):
+    grads, own_core, other_core = refs[:4], refs[4:8], refs[8:12]
+    out_ref, wt_ref, wide = refs[12:]
     heads = slots_ref.shape[0]
     rows = CLUSTERS * CAP
-    y = y_ref[0]
+    seq, y = lax.axis_index("seq"), lax.axis_index("head")
+    x, core = lax.rem(seq // 2, 4), lax.rem(seq, 2)
+    depth = own_core[0].shape[0] // 8
+    for d in range(4):
+        for c, refs_of in enumerate((own_core, other_core)):
+            part = lax.rem(x + (4 - d), 4) * 2 + (core if c == 0 else 1 - core)
+            for z in range(8):
+                start = pl.multiple_of((part + z * 8) * depth, depth)
+                wt_ref[pl.ds(start, depth), :] = refs_of[d][z * depth : (z + 1) * depth, :]
     total = None
-    for d, m_ref in enumerate((m0, m1, m2, m3)):
+    for d, m_ref in enumerate(grads):
         cols = m_ref.shape[1]
         start = pl.multiple_of(lax.rem(y + (4 - d), 4) * cols, cols)
         part = dot_nn(m_ref[...], wt_ref[pl.ds(start, cols), :])
@@ -102,17 +111,27 @@
     out_ref[...] = wide[...].astype(jnp.bfloat16)
 
 
-def forward_kernel(x_ref, att_ref, heads_ref, probs_ref, wide, back):
-    heads = pl.num_programs(0)
+def split_heads(x_ref, wide):
+    for t in range(wide.shape[0]):
+        wide[t] = x_ref[:, t * HD : (t + 1) * HD].astype(jnp.float32)
+
+
+def scores_of(q, k, k_wide):
+    first = lax.broadcasted_iota(jnp.int32, k.shape, 1) == 0
+    mask = jnp.where(first & (k_wide > EMPTY_MARK / 2), -1e30, 0.0).astype(jnp.bfloat16)
+    ones = jnp.ones(q.shape, jnp.bfloat16)
+    return dot_nt(jnp.concatenate([k, mask], axis=1), jnp.concatenate([q, ones], axis=1))
+
+
+def forward_kernel(x_ref, att_ref, heads_ref, probs_ref, att_wide_ref, wide, back):
     rows = CLUSTERS * CAP
     h = pl.program_id(0)
 
     @pl.when(h == 0)
     def _():
-        for t in range(3):
-            wide[t] = x_ref[:, t * HD : (t + 1) * HD].astype(jnp.float32)
-
-    where = pl.ds(h, rows, stride=4)
+        split_heads(x_ref, wide)
+
+    where = pl.ds(h, rows, stride=x_ref.shape[0] // rows)
     q = wide[0, where, :].astype(jnp.bfloat16)
     k_wide = wide[1, where, :]
     k = k_wide.astype(jnp.bfloat16)
@@ -120,49 +139,49 @@
     heads_ref[0] = q
     heads_ref[1] = k
     heads_ref[2] = v
-    bias = jnp.where(k_wide[:, :1] > EMPTY_MARK / 2, -1e30, 0.0)
-    scores = dot_nt(k, q) + bias
+    scores = scores_of(q, k, k_wide)
     top = jnp.max(scores, axis=0, keepdims=True)
     weights = jnp.exp2((scores - top) * (SCALE * LOG2E))
-    probs = weights * (1.0 / jnp.sum(weights, axis=0, keepdims=True))
+    probs = (weights * (1.0 / jnp.sum(weights, axis=0, keepdims=True))).astype(jnp.bfloat16)
     probs_ref[0] = probs
-    back[where, :] = dot_tn(v, probs.astype(jnp.bfloat16)).T
-
-    @pl.when(h == heads - 1)
+    att = dot_tn(v, probs)
+    att_wide_ref[0] = att
+    back[where, :] = att.T
+
+    @pl.when(h == pl.num_programs(0) - 1)
     def _():
         att_ref[...] = back[...].astype(jnp.bfloat16)
 
 
-def backward_kernel(g_ref, heads_ref, probs_ref, out_ref, wide, back):
-    heads = pl.num_programs(0)
+def backward_kernel(g_ref, heads_ref, probs_ref, att_ref, out_ref, wide, back):
     rows = CLUSTERS * CAP
     h = pl.program_id(0)
 
     @pl.when(h == 0)
     def _():
-        wide[...] = g_ref[...].astype(jnp.float32)
-
-    where = pl.ds(h, rows, stride=4)
-    g = wide[where, :].astype(jnp.bfloat16)
+        split_heads(g_ref, wide)
+
+    where = pl.ds(h, rows, stride=g_ref.shape[0] // rows)
+    g_wide = wide[0, where, :]
+    g = g_wide.astype(jnp.bfloat16)
     q, k, v = heads_ref[0], heads_ref[1], heads_ref[2]
     probs = probs_ref[0]
-    dprobs = dot_nt(v, g)
-    delta = jnp.sum(probs * dprobs, axis=0, keepdims=True)
-    dscores = (probs * (dprobs - delta)).astype(jnp.bfloat16)
+    delta = jnp.sum(g_wide.T * att_ref[0], axis=0, keepdims=True)
+    dscores = (probs.astype(jnp.float32) * (dot_nt(v, g) - delta)).astype(jnp.bfloat16)
     back[0, where, :] = dot_tn(k, dscores).T * SCALE
     back[1, where, :] = dot_nn(dscores, q) * SCALE
-    back[2, where, :] = dot_nn(probs.astype(jnp.bfloat16), g)
-
-    @pl.when(h == heads - 1)
+    back[2, where, :] = dot_nn(probs, g)
+
+    @pl.when(h == pl.num_programs(0) - 1)
     def _():
         for t in range(3):
             out_ref[:, t * HD : (t + 1) * HD] = back[t].astype(jnp.bfloat16)
 
 
-def mixed_kernel(y_ref, slots_ref, att_ref, wt_ref, own_ref, s1, s2, s3, wide):
+def mixed_kernel(slots_ref, att_ref, wt_ref, own_ref, s1, s2, s3, wide):
     heads = slots_ref.shape[0]
     rows = CLUSTERS * CAP
-    y = y_ref[0]
+    y = lax.axis_index("head")
     wide[...] = att_ref[...].astype(jnp.float32)
     pieces = []
     for h in range(heads):
@@ -190,14 +209,11 @@
             ref[:, head_cols(h)] = got[:, t * HD : (t + 1) * HD]
 
 
-def call(kernel, out, scratch, count, smem_first=False):
-    specs = [VMEM] * count
-    if smem_first:
-        specs[0] = SMEM
+def call(kernel, out, scratch, count):
     return pl.pallas_call(
         kernel,
         out_shape=out,
-        in_specs=specs,
+        in_specs=[VMEM] * count,
         out_specs=jax.tree.map(lambda _: VMEM, out),
         scratch_shapes=scratch,
         compiler_params=PARAMS,
@@ -217,35 +233,61 @@
     heads = cluster.shape[0]
     rows = CLUSTERS * CAP
     slots_all = heads * rows
-    y = lax.axis_index("head").astype(jnp.int32).reshape(1)
 
     def turn(x, d):
         return lax.ppermute(x, "head", [(i, (i + d) % 4) for i in range(4)])
 
-    wt = lax.all_gather(out_weight.T, "seq", axis=0, tiled=True)
-    grads = [mixed_grad] + [turn(mixed_grad, d) for d in (1, 2, 3)]
+    spots = [(z, x, c) for z in range(8) for x in range(4) for c in range(2)]
+
+    def place(z, x, c):
+        return z % 8 * 8 + x % 4 * 2 + c % 2
+
+    def along(x, move):
+        return lax.ppermute(x, "seq", [(place(*s), place(*move(*s))) for s in spots])
+
+    columns = [[place(z, x, c) for z in range(8)] for x in range(4) for c in range(2)]
+
+    shard = out_weight.T
+    depth, width = shard.shape
+    column = lax.all_to_all(
+        jnp.broadcast_to(shard[None], (8, depth, width)).reshape(8 * depth, width),
+        "seq",
+        split_axis=0,
+        concat_axis=0,
+        axis_index_groups=columns,
+        tiled=True,
+    )
+    right, left = turn(mixed_grad, 1), turn(mixed_grad, 3)
 
     payload, slots = call(
         pack_kernel,
         (sds((slots_all, 3 * HD)), sds((heads, tokens), jnp.int32)),
         [pltpu.VMEM((3, slots_all, HD), jnp.float32)],
         4,
-    )(cluster.reshape(heads, tokens), query, key, value)
+    )(cluster.transpose(0, 2, 1), query, key, value)
+    payload, column = lax.optimization_barrier((payload, column))
     arrived = exchange(payload)
-
-    att, held, probs = pl.pallas_call(
+    own_core = [column] + [along(column, lambda z, x, c, d=d: (z, x + d, c)) for d in (1, 2, 3)]
+    other_core = [along(part, lambda z, x, c: (z, x, c + 1)) for part in own_core]
+    across = turn(mixed_grad, 2)
+
+
+    by_head = lambda *shape: pl.BlockSpec(shape, lambda h: (h, 0, 0))
+    att, held, probs, att_wide = pl.pallas_call(
         forward_kernel,
         grid=(heads,),
         out_shape=(
             sds((slots_all, HD)),
             sds((heads * 3, rows, HD)),
-            sds((heads, rows, rows), jnp.float32),
+            sds((heads, rows, rows)),
+            sds((heads, HD, rows), jnp.float32),
         ),
         in_specs=[pl.BlockSpec((slots_all, 3 * HD), lambda h: (0, 0))],
         out_specs=(
             pl.BlockSpec((slots_all, HD), lambda h: (0, 0)),
-            pl.BlockSpec((3, rows, HD), lambda h: (h, 0, 0)),
-            pl.BlockSpec((1, rows, rows), lambda h: (h, 0, 0)),
+            by_head(3, rows, HD),
+            by_head(1, rows, rows),
+            by_head(1, HD, rows),
         ),
         scratch_shapes=[
             pltpu.VMEM((3, slots_all, HD), jnp.float32),
@@ -254,15 +296,15 @@
         compiler_params=PARAMS,
     )(arrived)
 
-    grad_payload = call(
+    grad_payload, wt = call(
         grad_kernel,
-        sds((slots_all, HD)),
+        (sds((slots_all, HD)), sds((64 * depth, width))),
         [pltpu.VMEM((slots_all, HD), jnp.float32)],
-        7,
-        smem_first=True,
-    )(y, slots, *grads, wt)
+        13,
+    )(slots, mixed_grad, right, across, left, *own_core, *other_core)
+    grad_arrived = exchange(grad_payload)
+    att, grad_arrived = lax.optimization_barrier((att, grad_arrived))
     att_back = exchange(att)
-    grad_arrived = exchange(grad_payload)
 
     done = pl.pallas_call(
         backward_kernel,
@@ -270,16 +312,17 @@
         out_shape=sds((slots_all, 3 * HD)),
         in_specs=[
             pl.BlockSpec((slots_all, HD), lambda h: (0, 0)),
-            pl.BlockSpec((3, rows, HD), lambda h: (h, 0, 0)),
-            pl.BlockSpec((1, rows, rows), lambda h: (h, 0, 0)),
+            by_head(3, rows, HD),
+            by_head(1, rows, rows),
+            by_head(1, HD, rows),
         ],
         out_specs=pl.BlockSpec((slots_all, 3 * HD), lambda h: (0, 0)),
         scratch_shapes=[
-            pltpu.VMEM((slots_all, HD), jnp.float32),
+            pltpu.VMEM((1, slots_all, HD), jnp.float32),
             pltpu.VMEM((3, slots_all, HD), jnp.float32),
         ],
         compiler_params=PARAMS,
-    )(grad_arrived, held, probs)
+    )(grad_arrived, held, probs, att_wide)
     back = exchange(done)
 
     cols = mixed_grad.shape[1]
@@ -287,9 +330,8 @@
         mixed_kernel,
         (sds((tokens, cols), jnp.float32),) + (sds((tokens, cols)),) * 3,
         [pltpu.VMEM((slots_all, HD), jnp.float32)],
-        4,
-        smem_first=True,
-    )(y, slots, att_back, wt)
+        3,
+    )(slots, att_back, wt)
     mixed = own
     for d, part in zip((1, 2, 3), sends):
         mixed = mixed + turn(part, d).astype(jnp.float32)

time: 246 us -> 227 us (0.923)
  waiting for transfers between devices: 138 us -> 124 us
  between operations: 14.1 us -> 0.79 us
  starting transfers between devices: 43.6 us -> 52.8 us
    all_gather x1 -> x0, waiting for transfers between devices: 35.5 us -> none  [local(): wt = lax.all_gather(out_weight.T, 'seq', axis=0, tiled=True)]
    ppermute x0 -> x7, waiting for transfers between devices: none -> 14.6 us  [along(): lax.ppermute(x, 'seq', [(place(*s), place(*move(*s))) for s in spots])]
    all_to_all x0 -> x1, waiting for transfers between devices: none -> 11.9 us  [local(): lax.all_to_all(jnp.broadcast_to(shard[None], (8, depth, width)).reshape(8...]
    all_to_all x0 -> x1, starting transfers between devices: none -> 8.47 us  [local(): lax.all_to_all(jnp.broadcast_to(shard[None], (8, depth, width)).reshape(8...]
    ppermute x6, waiting for transfers between devices: 67.1 us -> 60.8 us  [turn(): return lax.ppermute(x, 'head', [(i, (i + d) % 4) for i in range(4)])]
    ppermute x0 -> x7, starting transfers between devices: none -> 5.71 us  [along(): lax.ppermute(x, 'seq', [(place(*s), place(*move(*s))) for s in spots])]
    all_to_all x4, starting transfers between devices: 32.1 us -> 26.7 us  [exchange(): return lax.all_to_all(x, 'seq', split_axis=0, concat_axis=0, tiled=True)]
  transfers between devices with their start and end apart: 11 -> 18, of which waited for: 8 -> 11; matrix products, arithmetic and copies ran while one was open for 2% -> 1% of each run, Pallas kernels for 16% -> 16%
where the time goes in v2:
time: 227 us
  waiting for transfers between devices  124 us (55%)
  starting transfers between devices  52.8 us (23%)
  Pallas kernels  41.2 us (18%)
  local copies, waits for them, and re-layouts  4.87 us (2%)
  other arithmetic  2.86 us (1%)
    ppermute x6, waiting for transfers between devices, turn(): return lax.ppermute(x, 'head', [(i, (i + d) % 4) for i in range(4)])  60.8 us
    all_to_all x4, waiting for transfers between devices, exchange(): return lax.all_to_all(x, 'seq', split_axis=0, concat_axis=0, tiled=True)  36.9 us
    all_to_all x4, starting transfers between devices, exchange(): return lax.all_to_all(x, 'seq', split_axis=0, concat_axis=0, tiled=True)  26.7 us
    ppermute x7, waiting for transfers between devices, along(): lax.ppermute(x, 'seq', [(place(*s), place(*move(*s))) for s in spots])  14.6 us
    all_to_all x1, waiting for transfers between devices, local(): lax.all_to_all(jnp.broadcast_to(shard[None], (8, depth, width)).reshape(8...  11.9 us
    ppermute x6, starting transfers between devices, turn(): return lax.ppermute(x, 'head', [(i, (i + d) % 4) for i in range(4)])  11.9 us
    pallas_call x1, Pallas kernels, local(): pl.pallas_call(backward_kernel, grid=(heads,), out_shape=sds((slots_all,...  9.51 us
    pallas_call x1, Pallas kernels, local(): pl.pallas_call(forward_kernel, grid=(heads,), out_shape=(sds((slots_all,...  9.03 us
  transfers between devices with their start and end apart: 18, of which 11 were waited for; matrix products, arithmetic and copies ran while one was open for 1% of the time, Pallas kernels for 16%

profile of v2, /device:TPU:2, one launch (start us, length us, event | category | flops | bytes accessed | tf_op | source)
XLA Modules:
  0.0 226.6 jit_solution(5154197005742362819)
XLA Ops:
  0.6 1.7 broadcast_in_dim.2
  2.3 8.5 %all-to-all-start = ((bf16[8,64,512]{2,1,0:T(8,128)(2,1)}), bf16[8,64,512]{2,1,0:T(8,128)(2,1)S(1)}, u32[]{:S(2)}, u32[]{:S(2)}) async-start(bf16[8,64,512]{2,1,0:T(8,128)(2,1)} %broadcast_in_dim.2), calls=%async_computation | async-start | bytes 1048576 | tf_op jit(solution)/shard_map/all_to_all | solution.py:252
  10.8 5.5 %shard_map.93 = (bf16[3072,384]{1,0:T(8,128)(2,1)}, s32[4,384]{1,0:T(4,128)}) custom-call(s32[4,1,384]{2,1,0:T(1,128)} %bitcast.25, bf16[384,512]{1,0:T(8,128)(2,1)} %q_ref.1, bf16[384,512]{1,0:T(8,128)(2,1)} %k_ref.1, bf16[384,512]{1,0:T(8,128)(2,1)} %v_ref.1), custom_call_target="tpu_custom_call" | custom-call | tf_op jit(solution)/shard_map/pallas_call | solution.py:262
  16.3 11.9 %all-to-all-done = bf16[8,64,512]{2,1,0:T(8,128)(2,1)S(1)} async-done(((bf16[8,64,512]{2,1,0:T(8,128)(2,1)}), bf16[8,64,512]{2,1,0:T(8,128)(2,1)S(1)}, u32[]{:S(2)}, u32[]{:S(2)}) %all-to-all-start) | async-done | bytes 524320 | tf_op jit(solution)/shard_map/all_to_all | solution.py:252
  28.3 5.4 %all-to-all-start.1 = ((bf16[64,48,384]{2,1,0:T(8,128)(2,1)}), bf16[64,48,384]{2,1,0:T(8,128)(2,1)S(1)}, u32[]{:S(2)}, u32[]{:S(2)}) async-start(bf16[64,48,384]{2,1,0:T(8,128)(2,1)} %bitcast.16), calls=%async_computation.1 | async-start | bytes 4718592 | tf_op jit(solution)/shard_map/all_to_all | solution.py:228
  33.7 3.3 %collective-permute-start.1 = (bf16[384,1024]{1,0:T(8,128)(2,1)}, bf16[384,1024]{1,0:T(8,128)(2,1)S(1)}, u32[]{:S(2)}, u32[]{:S(2)}) collective-permute-start(bf16[384,1024]{1,0:T(8,128)(2,1)} %refs_0_.1), channel_id=1, source_target_pairs={{0,2},{1,3},{2,0},{3,1},{4,6},{5,7},{6,4},{7,5},{8,10},{9,11},{10,... | collective-permute-start | bytes 2359304 | tf_op jit(solution)/shard_map/ppermute | solution.py:238
  36.9 0.7 collective-permute-start
  37.6 0.5 collective-permute-start.5
  38.1 2.5 %collective-permute-start.4 = (bf16[512,512]{1,0:T(8,128)(2,1)S(1)}, bf16[512,512]{1,0:T(8,128)(2,1)S(1)}, u32[]{:S(2)}, u32[]{:S(2)}) collective-permute-start(bf16[512,512]{1,0:T(8,128)(2,1)S(1)} %bitcast.18), channel_id=1, source_target_pairs={{0,16},{4,20},{8,24},{12,28},{16,0},{20,4},{24,8},{28,12},{32,48},... | collective-permute-start | bytes 1572872 | tf_op jit(solution)/shard_map/ppermute | solution.py:246
  40.6 1.8 collective-permute-start.3
  42.3 13.6 %collective-permute-done.1.refs_2_ = bf16[384,1024]{1,0:T(8,128)(2,1)S(1)} collective-permute-done((bf16[384,1024]{1,0:T(8,128)(2,1)}, bf16[384,1024]{1,0:T(8,128)(2,1)S(1)}, u32[]{:S(2)}, u32[]{:S(2)}) %collective-permute-start.1) | collective-permute-done | bytes 786464 | tf_op jit(solution)/shard_map/ppermute | solution.py:238
  55.9 2.2 collective-permute-start.2
  58.1 13.8 %collective-permute-done.refs_1_ = bf16[384,1024]{1,0:T(8,128)(2,1)S(1)} collective-permute-done((bf16[384,1024]{1,0:T(8,128)(2,1)}, bf16[384,1024]{1,0:T(8,128)(2,1)S(1)}, u32[]{:S(2)}, u32[]{:S(2)}) %collective-permute-start) | collective-permute-done | bytes 786464 | tf_op jit(solution)/shard_map/ppermute | solution.py:238
  71.9 0.0 collective-permute-start.6
  71.9 0.0 collective-permute-done.5.refs_7_
  71.9 0.5 collective-permute-start.9
  72.4 12.4 %collective-permute-done.4.refs_6_ = bf16[512,512]{1,0:T(8,128)(2,1)S(1)} collective-permute-done((bf16[512,512]{1,0:T(8,128)(2,1)S(1)}, bf16[512,512]{1,0:T(8,128)(2,1)S(1)}, u32[]{:S(2)}, u32[]{:S(2)}) %collective-permute-start.4) | collective-permute-done | bytes 524320 | tf_op jit(solution)/shard_map/ppermute | solution.py:246
  84.9 0.0 collective-permute-start.8
  84.9 0.0 collective-permute-done.3.refs_5_
  84.9 0.5 collective-permute-start.7
  85.4 0.0 collective-permute-done.2.refs_3_
  85.4 0.0 collective-permute-done.6.refs_8_
  85.4 0.0 collective-permute-done.9.refs_11_
  85.4 1.4 collective-permute-done.8.refs_10_
  86.8 0.7 collective-permute-done.7.refs_9_
  87.5 0.1 copy-done.13
  87.6 0.8 copy-done.14
  88.5 6.9 %shard_map.95 = (bf16[3072,128]{1,0:T(8,128)(2,1)}, bf16[4096,512]{1,0:T(8,128)(2,1)}) custom-call(s32[4,384]{1,0:T(4,128)} %get-tuple-element.23.slots_ref, bf16[384,1024]{1,0:T(8,128)(2,1)} %refs_0_.1, bf16[384,1024]{1,0:T(8,128)(2,1)} %copy-done.6, bf16[384,1024]{1,0:T(8,128)(2,1)} %copy-done.5, bf16[384,1024]{1,0:T(8,128)(2,1)} %copy-done.7, ...), custom_call_target="tpu_custom_call" | custom-call | tf_op jit(solution)/shard_map/pallas_call | solution.py:299
  95.4 0.0 all-to-all-done.1
  95.4 9.7 %all-to-all-start.2 = ((bf16[64,48,128]{2,1,0:T(8,128)(2,1)}), bf16[64,48,128]{2,1,0:T(8,128)(2,1)S(1)}, u32[]{:S(2)}, u32[]{:S(2)}) async-start(bf16[64,48,128]{2,1,0:T(8,128)(2,1)} %bitcast.22), calls=%async_computation.2 | async-start | bytes 1572864 | tf_op jit(solution)/shard_map/all_to_all | solution.py:228
  105.1 9.0 %shard_map.94 = (bf16[3072,128]{1,0:T(8,128)(2,1)}, bf16[12,768,128]{2,1,0:T(8,128)(2,1)}, bf16[4,768,768]{2,1,0:T(8,128)(2,1)}, f32[4,128,768]{2,1,0:T(8,128)}) custom-call(bf16[3072,384]{1,0:T(8,128)(2,1)} %bitcast.11), custom_call_target="tpu_custom_call" | custom-call | tf_op jit(solution)/shard_map/pallas_call | solution.py:276
  114.1 14.1 %all-to-all-done.2 = bf16[64,48,128]{2,1,0:T(8,128)(2,1)S(1)} async-done(((bf16[64,48,128]{2,1,0:T(8,128)(2,1)}), bf16[64,48,128]{2,1,0:T(8,128)(2,1)S(1)}, u32[]{:S(2)}, u32[]{:S(2)}) %all-to-all-start.2) | async-done | bytes 786464 | tf_op jit(solution)/shard_map/all_to_all | solution.py:228
  128.3 5.8 %all-to-all-start.3 = ((bf16[64,48,128]{2,1,0:T(8,128)(2,1)}), bf16[64,48,128]{2,1,0:T(8,128)(2,1)S(1)}, u32[]{:S(2)}, u32[]{:S(2)}) async-start(bf16[64,48,128]{2,1,0:T(8,128)(2,1)} %bitcast.23), calls=%async_computation.3 | async-start | bytes 1572864 | tf_op jit(solution)/shard_map/all_to_all | solution.py:228
  134.1 9.5 %shard_map.97 = bf16[3072,384]{1,0:T(8,128)(2,1)} custom-call(bf16[3072,128]{1,0:T(8,128)(2,1)} %bitcast.14, bf16[12,768,128]{2,1,0:T(8,128)(2,1)} %get-tuple-element.36.heads_ref, bf16[4,768,768]{2,1,0:T(8,128)(2,1)} %get-tuple-element.37.probs_ref, f32[4,128,768]{2,1,0:T(8,128)} %get-tuple-element.38.att_ref), custom_call_target="tpu_custom_call" | custom-call | tf_op jit(solution)/shard_map/pallas_call | solution.py:309
  143.6 13.7 %all-to-all-done.3 = bf16[64,48,128]{2,1,0:T(8,128)(2,1)S(1)} async-done(((bf16[64,48,128]{2,1,0:T(8,128)(2,1)}), bf16[64,48,128]{2,1,0:T(8,128)(2,1)S(1)}, u32[]{:S(2)}, u32[]{:S(2)}) %all-to-all-start.3) | async-done | bytes 786464 | tf_op jit(solution)/shard_map/all_to_all | solution.py:228
  157.3 0.9 copy-done.3
  158.1 5.8 %all-to-all-start.4 = ((bf16[64,48,384]{2,1,0:T(8,128)(2,1)}), bf16[64,48,384]{2,1,0:T(8,128)(2,1)S(1)}, u32[]{:S(2)}, u32[]{:S(2)}) async-start(bf16[64,48,384]{2,1,0:T(8,128)(2,1)} %bitcast.13), calls=%async_computation.4 | async-start | bytes 4718592 | tf_op jit(solution)/shard_map/all_to_all | solution.py:228
  164.0 5.8 %shard_map.96 = (f32[384,1024]{1,0:T(8,128)}, bf16[384,1024]{1,0:T(8,128)(2,1)}, bf16[384,1024]{1,0:T(8,128)(2,1)}, bf16[384,1024]{1,0:T(8,128)(2,1)}) custom-call(s32[4,384]{1,0:T(4,128)} %get-tuple-element.23.slots_ref, bf16[3072,128]{1,0:T(8,128)(2,1)} %bitcast.15, bf16[4096,512]{1,0:T(8,128)(2,1)} %get-tuple-element.30.wt_ref), custom_call_target="tpu_custom_call" | custom-call | tf_op jit(solution)/shard_map/pallas_call | solution.py:329
  169.8 1.5 collective-permute-start.10
  171.3 3.0 %collective-permute-start.11 = (bf16[384,1024]{1,0:T(8,128)(2,1)}, bf16[384,1024]{1,0:T(8,128)(2,1)S(1)}, u32[]{:S(2)}, u32[]{:S(2)}) collective-permute-start(bf16[384,1024]{1,0:T(8,128)(2,1)} %get-tuple-element.33), channel_id=1, source_target_pairs={{0,2},{1,3},{2,0},{3,1},{4,6},{5,7},{6,4},{7,5},{8,10},{9,11},{10,... | collective-permute-start | bytes 2359304 | tf_op jit(solution)/shard_map/ppermute | solution.py:238
  174.2 1.3 collective-permute-start.12
  175.5 15.3 %collective-permute-done.10 = bf16[384,1024]{1,0:T(8,128)(2,1)S(1)} collective-permute-done((bf16[384,1024]{1,0:T(8,128)(2,1)}, bf16[384,1024]{1,0:T(8,128)(2,1)S(1)}, u32[]{:S(2)}, u32[]{:S(2)}) %collective-permute-start.10) | collective-permute-done | bytes 786464 | tf_op jit(solution)/shard_map/ppermute | solution.py:238
  190.8 18.0 %collective-permute-done.11 = bf16[384,1024]{1,0:T(8,128)(2,1)S(1)} collective-permute-done((bf16[384,1024]{1,0:T(8,128)(2,1)}, bf16[384,1024]{1,0:T(8,128)(2,1)S(1)}, u32[]{:S(2)}, u32[]{:S(2)}) %collective-permute-start.11) | collective-permute-done | bytes 786464 | tf_op jit(solution)/shard_map/ppermute | solution.py:238
  208.9 0.0 collective-permute-done.12
  208.9 2.9 %add_convert_fusion = bf16[384,1024]{1,0:T(8,128)(2,1)} fusion(bf16[384,1024]{1,0:T(8,128)(2,1)S(1)} %collective-permute-done.12, bf16[384,1024]{1,0:T(8,128)(2,1)S(1)} %collective-permute-done.11, f32[384,1024]{1,0:T(8,128)} %get-tuple-element.31, bf16[384,1024]{1,0:T(8,128)(2,1)S(1)} %collective-permute-done.10), kind=kLoop, calls=%fused_computation | loop fusion | flops 2752512 | bytes 4718592 | tf_op jit(solution)/shard_map/convert_element_type | solution.py:338
  211.8 9.1 %all-to-all-done.4 = bf16[64,48,384]{2,1,0:T(8,128)(2,1)S(1)} async-done(((bf16[64,48,384]{2,1,0:T(8,128)(2,1)}), bf16[64,48,384]{2,1,0:T(8,128)(2,1)S(1)}, u32[]{:S(2)}, u32[]{:S(2)}) %all-to-all-start.4) | async-done | bytes 2359328 | tf_op jit(solution)/shard_map/all_to_all | solution.py:228
  220.9 1.4 copy-done.1
  222.3 4.3 %shard_map.98 = (bf16[384,512]{1,0:T(8,128)(2,1)}, bf16[384,512]{1,0:T(8,128)(2,1)}, bf16[384,512]{1,0:T(8,128)(2,1)}) custom-call(s32[4,384]{1,0:T(4,128)} %get-tuple-element.23.slots_ref, bf16[3072,384]{1,0:T(8,128)(2,1)} %bitcast.12), custom_call_target="tpu_custom_call" | custom-call | tf_op jit(solution)/shard_map/pallas_call | solution.py:340
  (26 shorter events, 0.0 us)
Async XLA Ops:
  2.3 26.0 %all-to-all-start = ((bf16[8,64,512]{2,1,0:T(8,128)(2,1)}), bf16[8,64,512]{2,1,0:T(8,128)(2,1)S(1)}, u32[]{:S(2)}, u32[]{:S(2)}) async-start(bf16[8,64,512]{2,1,0:T(8,128)(2,1)} %broadcast_in_dim.2), calls=%async_computation | async-start | bytes 1048576 | tf_op jit(solution)/shard_map/all_to_all | solution.py:252
  28.3 43.7 %copy-start.4 = (bf16[8,64,512]{2,1,0:T(8,128)(2,1)}, bf16[8,64,512]{2,1,0:T(8,128)(2,1)S(1)}, u32[]{:S(2)}) copy-start(bf16[8,64,512]{2,1,0:T(8,128)(2,1)S(1)} %all-to-all-done) | copy-start | bytes 1572868
  28.3 67.1 %all-to-all-start.1 = ((bf16[64,48,384]{2,1,0:T(8,128)(2,1)}), bf16[64,48,384]{2,1,0:T(8,128)(2,1)S(1)}, u32[]{:S(2)}, u32[]{:S(2)}) async-start(bf16[64,48,384]{2,1,0:T(8,128)(2,1)} %bitcast.16), calls=%async_computation.1 | async-start | bytes 4718592 | tf_op jit(solution)/shard_map/all_to_all | solution.py:228
  33.7 22.2 %collective-permute-start.1 = (bf16[384,1024]{1,0:T(8,128)(2,1)}, bf16[384,1024]{1,0:T(8,128)(2,1)S(1)}, u32[]{:S(2)}, u32[]{:S(2)}) collective-permute-start(bf16[384,1024]{1,0:T(8,128)(2,1)} %refs_0_.1), channel_id=1, source_target_pairs={{0,2},{1,3},{2,0},{3,1},{4,6},{5,7},{6,4},{7,5},{8,10},{9,11},{10,... | collective-permute-start | bytes 2359304 | tf_op jit(solution)/shard_map/ppermute | solution.py:238
  36.9 35.0 %collective-permute-start = (bf16[384,1024]{1,0:T(8,128)(2,1)}, bf16[384,1024]{1,0:T(8,128)(2,1)S(1)}, u32[]{:S(2)}, u32[]{:S(2)}) collective-permute-start(bf16[384,1024]{1,0:T(8,128)(2,1)} %refs_0_.1), channel_id=1, source_target_pairs={{0,1},{1,2},{2,3},{3,0},{4,5},{5,6},{6,7},{7,4},{8,9},{9,10},{10,1... | collective-permute-start | bytes 2359304 | tf_op jit(solution)/shard_map/ppermute | solution.py:238
  37.6 34.3 %collective-permute-start.5 = (bf16[512,512]{1,0:T(8,128)(2,1)S(1)}, bf16[512,512]{1,0:T(8,128)(2,1)S(1)}, u32[]{:S(2)}, u32[]{:S(2)}) collective-permute-start(bf16[512,512]{1,0:T(8,128)(2,1)S(1)} %bitcast.17), channel_id=1, source_target_pairs={{0,24},{4,28},{8,0},{12,4},{16,8},{20,12},{24,16},{28,20},{32,56},... | collective-permute-start | bytes 1572872 | tf_op jit(solution)/shard_map/ppermute | solution.py:246
  38.1 46.8 %collective-permute-start.4 = (bf16[512,512]{1,0:T(8,128)(2,1)S(1)}, bf16[512,512]{1,0:T(8,128)(2,1)S(1)}, u32[]{:S(2)}, u32[]{:S(2)}) collective-permute-start(bf16[512,512]{1,0:T(8,128)(2,1)S(1)} %bitcast.18), channel_id=1, source_target_pairs={{0,16},{4,20},{8,24},{12,28},{16,0},{20,4},{24,8},{28,12},{32,48},... | collective-permute-start | bytes 1572872 | tf_op jit(solution)/shard_map/ppermute | solution.py:246
  40.6 44.3 %collective-permute-start.3 = (bf16[512,512]{1,0:T(8,128)(2,1)S(1)}, bf16[512,512]{1,0:T(8,128)(2,1)S(1)}, u32[]{:S(2)}, u32[]{:S(2)}) collective-permute-start(bf16[512,512]{1,0:T(8,128)(2,1)S(1)} %bitcast.19), channel_id=1, source_target_pairs={{0,8},{4,12},{8,16},{12,20},{16,24},{20,28},{24,0},{28,4},{32,40},... | collective-permute-start | bytes 1572872 | tf_op jit(solution)/shard_map/ppermute | solution.py:246
  55.9 32.5 %copy-start.5 = (bf16[384,1024]{1,0:T(8,128)(2,1)}, bf16[384,1024]{1,0:T(8,128)(2,1)S(1)}, u32[]{:S(2)}) copy-start(bf16[384,1024]{1,0:T(8,128)(2,1)S(1)} %collective-permute-done.1.refs_2_) | copy-start | bytes 2359300
  55.9 29.5 %collective-permute-start.2 = (bf16[384,1024]{1,0:T(8,128)(2,1)}, bf16[384,1024]{1,0:T(8,128)(2,1)S(1)}, u32[]{:S(2)}, u32[]{:S(2)}) collective-permute-start(bf16[384,1024]{1,0:T(8,128)(2,1)} %refs_0_.1), channel_id=1, source_target_pairs={{0,3},{1,0},{2,1},{3,2},{4,7},{5,4},{6,5},{7,6},{8,11},{9,8},{10,9... | collective-permute-start | bytes 2359304 | tf_op jit(solution)/shard_map/ppermute | solution.py:238
  71.9 16.5 %copy-start.6 = (bf16[384,1024]{1,0:T(8,128)(2,1)}, bf16[384,1024]{1,0:T(8,128)(2,1)S(1)}, u32[]{:S(2)}) copy-start(bf16[384,1024]{1,0:T(8,128)(2,1)S(1)} %collective-permute-done.refs_1_) | copy-start | bytes 2359300
  71.9 13.5 %collective-permute-start.6 = (bf16[512,512]{1,0:T(8,128)(2,1)S(1)}, bf16[512,512]{1,0:T(8,128)(2,1)S(1)}, u32[]{:S(2)}, u32[]{:S(2)}) collective-permute-start(bf16[512,512]{1,0:T(8,128)(2,1)S(1)} %bitcast.20), channel_id=1, source_target_pairs={{0,4},{4,0},{8,12},{12,8},{16,20},{20,16},{24,28},{28,24},{32,36},... | collective-permute-start | bytes 1572872 | tf_op jit(solution)/shard_map/ppermute | solution.py:246
  71.9 16.5 %copy-start.8 = (bf16[512,512]{1,0:T(8,128)(2,1)}, bf16[512,512]{1,0:T(8,128)(2,1)S(1)}, u32[]{:S(2)}) copy-start(bf16[512,512]{1,0:T(8,128)(2,1)S(1)} %collective-permute-done.5.refs_7_) | copy-start | bytes 1572868
  71.9 13.5 %collective-permute-start.9 = (bf16[512,512]{1,0:T(8,128)(2,1)S(1)}, bf16[512,512]{1,0:T(8,128)(2,1)S(1)}, u32[]{:S(2)}, u32[]{:S(2)}) collective-permute-start(bf16[512,512]{1,0:T(8,128)(2,1)S(1)} %collective-permute-done.5.refs_7_), channel_id=1, source_target_pairs={{0,4},{4,0},{8,12},{12,8},{16,20},{20,16},{24,28},{28,24},{32,36},... | collective-permute-start | bytes 1572872 | tf_op jit(solution)/shard_map/ppermute | solution.py:246
  84.9 3.5 %copy-start.9 = (bf16[512,512]{1,0:T(8,128)(2,1)}, bf16[512,512]{1,0:T(8,128)(2,1)S(1)}, u32[]{:S(2)}) copy-start(bf16[512,512]{1,0:T(8,128)(2,1)S(1)} %collective-permute-done.4.refs_6_) | copy-start | bytes 1572868
  84.9 1.9 collective-permute-start.8
  84.9 3.5 %copy-start.10 = (bf16[512,512]{1,0:T(8,128)(2,1)}, bf16[512,512]{1,0:T(8,128)(2,1)S(1)}, u32[]{:S(2)}) copy-start(bf16[512,512]{1,0:T(8,128)(2,1)S(1)} %collective-permute-done.3.refs_5_) | copy-start | bytes 1572868
  84.9 2.6 %collective-permute-start.7 = (bf16[512,512]{1,0:T(8,128)(2,1)S(1)}, bf16[512,512]{1,0:T(8,128)(2,1)S(1)}, u32[]{:S(2)}, u32[]{:S(2)}) collective-permute-start(bf16[512,512]{1,0:T(8,128)(2,1)S(1)} %collective-permute-done.3.refs_5_), channel_id=1, source_target_pairs={{0,4},{4,0},{8,12},{12,8},{16,20},{20,16},{24,28},{28,24},{32,36},... | collective-permute-start | bytes 1572872 | tf_op jit(solution)/shard_map/ppermute | solution.py:246
  85.4 3.0 %copy-start.7 = (bf16[384,1024]{1,0:T(8,128)(2,1)}, bf16[384,1024]{1,0:T(8,128)(2,1)S(1)}, u32[]{:S(2)}) copy-start(bf16[384,1024]{1,0:T(8,128)(2,1)S(1)} %collective-permute-done.2.refs_3_) | copy-start | bytes 2359300
  85.4 3.0 %copy-start.11 = (bf16[512,512]{1,0:T(8,128)(2,1)}, bf16[512,512]{1,0:T(8,128)(2,1)S(1)}, u32[]{:S(2)}) copy-start(bf16[512,512]{1,0:T(8,128)(2,1)S(1)} %collective-permute-done.6.refs_8_) | copy-start | bytes 1572868
  85.4 3.0 %copy-start.12 = (bf16[512,512]{1,0:T(8,128)(2,1)}, bf16[512,512]{1,0:T(8,128)(2,1)S(1)}, u32[]{:S(2)}) copy-start(bf16[512,512]{1,0:T(8,128)(2,1)S(1)} %collective-permute-done.9.refs_11_) | copy-start | bytes 1572868
  86.8 0.8 copy-start.13
  87.6 0.8 copy-start.14
  95.4 9.7 %copy-start = (bf16[64,48,384]{2,1,0:T(8,128)(2,1)}, bf16[64,48,384]{2,1,0:T(8,128)(2,1)S(1)}, u32[]{:S(2)}) copy-start(bf16[64,48,384]{2,1,0:T(8,128)(2,1)S(1)} %all-to-all-done.1) | copy-start | bytes 7077892
  95.4 32.9 %all-to-all-start.2 = ((bf16[64,48,128]{2,1,0:T(8,128)(2,1)}), bf16[64,48,128]{2,1,0:T(8,128)(2,1)S(1)}, u32[]{:S(2)}, u32[]{:S(2)}) async-start(bf16[64,48,128]{2,1,0:T(8,128)(2,1)} %bitcast.22), calls=%async_computation.2 | async-start | bytes 1572864 | tf_op jit(solution)/shard_map/all_to_all | solution.py:228
  128.3 5.8 %copy-start.2 = (bf16[64,48,128]{2,1,0:T(8,128)(2,1)}, bf16[64,48,128]{2,1,0:T(8,128)(2,1)S(1)}, u32[]{:S(2)}) copy-start(bf16[64,48,128]{2,1,0:T(8,128)(2,1)S(1)} %all-to-all-done.2) | copy-start | bytes 2359300
  128.3 29.0 %all-to-all-start.3 = ((bf16[64,48,128]{2,1,0:T(8,128)(2,1)}), bf16[64,48,128]{2,1,0:T(8,128)(2,1)S(1)}, u32[]{:S(2)}, u32[]{:S(2)}) async-start(bf16[64,48,128]{2,1,0:T(8,128)(2,1)} %bitcast.23), calls=%async_computation.3 | async-start | bytes 1572864 | tf_op jit(solution)/shard_map/all_to_all | solution.py:228
  157.3 0.9 copy-start.3
  158.1 62.7 %all-to-all-start.4 = ((bf16[64,48,384]{2,1,0:T(8,128)(2,1)}), bf16[64,48,384]{2,1,0:T(8,128)(2,1)S(1)}, u32[]{:S(2)}, u32[]{:S(2)}) async-start(bf16[64,48,384]{2,1,0:T(8,128)(2,1)} %bitcast.13), calls=%async_computation.4 | async-start | bytes 4718592 | tf_op jit(solution)/shard_map/all_to_all | solution.py:228
  169.8 21.1 %collective-permute-start.10 = (bf16[384,1024]{1,0:T(8,128)(2,1)}, bf16[384,1024]{1,0:T(8,128)(2,1)S(1)}, u32[]{:S(2)}, u32[]{:S(2)}) collective-permute-start(bf16[384,1024]{1,0:T(8,128)(2,1)} %get-tuple-element.32), channel_id=1, source_target_pairs={{0,1},{1,2},{2,3},{3,0},{4,5},{5,6},{6,7},{7,4},{8,9},{9,10},{10,1... | collective-permute-start | bytes 2359304 | tf_op jit(solution)/shard_map/ppermute | solution.py:238
  171.3 37.6 %collective-permute-start.11 = (bf16[384,1024]{1,0:T(8,128)(2,1)}, bf16[384,1024]{1,0:T(8,128)(2,1)S(1)}, u32[]{:S(2)}, u32[]{:S(2)}) collective-permute-start(bf16[384,1024]{1,0:T(8,128)(2,1)} %get-tuple-element.33), channel_id=1, source_target_pairs={{0,2},{1,3},{2,0},{3,1},{4,6},{5,7},{6,4},{7,5},{8,10},{9,11},{10,... | collective-permute-start | bytes 2359304 | tf_op jit(solution)/shard_map/ppermute | solution.py:238
  174.2 34.6 %collective-permute-start.12 = (bf16[384,1024]{1,0:T(8,128)(2,1)}, bf16[384,1024]{1,0:T(8,128)(2,1)S(1)}, u32[]{:S(2)}, u32[]{:S(2)}) collective-permute-start(bf16[384,1024]{1,0:T(8,128)(2,1)} %get-tuple-element.34), channel_id=1, source_target_pairs={{0,3},{1,0},{2,1},{3,2},{4,7},{5,4},{6,5},{7,6},{8,11},{9,8},{10,9... | collective-permute-start | bytes 2359304 | tf_op jit(solution)/shard_map/ppermute | solution.py:238
  220.9 1.4 copy-start.1

commit v3 on v2

--- a/solution.py
+++ b/solution.py
@@ -16,7 +16,7 @@
 LOG2E = math.log2(math.e)
 
 VMEM = pl.BlockSpec(memory_space=pltpu.VMEM)
-PARAMS = pltpu.CompilerParams(vmem_limit_bytes=56 * 1024 * 1024)
+PARAMS = pltpu.CompilerParams(vmem_limit_bytes=32 * 1024 * 1024)
 
 
 def dot_nt(a, b):
@@ -84,25 +84,39 @@
         out_ref[:, t * HD : (t + 1) * HD] = wide[t].astype(jnp.bfloat16)
 
 
+def collect_kernel(*refs):
+    start = 0
+    for ref in refs[:-1]:
+        refs[-1][start : start + ref.shape[0], :] = ref[...]
+        start += ref.shape[0]
+
+
 def grad_kernel(slots_ref, *refs):
-    grads, own_core, other_core = refs[:4], refs[4:8], refs[8:12]
-    out_ref, wt_ref, wide = refs[12:]
+    grads, own_core, other_core = refs[:5], refs[5:9], refs[9:13]
+    out_ref, wt_ref, wide = refs[13:]
     heads = slots_ref.shape[0]
     rows = CLUSTERS * CAP
     seq, y = lax.axis_index("seq"), lax.axis_index("head")
-    x, core = lax.rem(seq // 2, 4), lax.rem(seq, 2)
+    z, x, core = seq // 8, lax.rem(seq // 2, 4), lax.rem(seq, 2)
     depth = own_core[0].shape[0] // 8
-    for d in range(4):
-        for c, refs_of in enumerate((own_core, other_core)):
-            part = lax.rem(x + (4 - d), 4) * 2 + (core if c == 0 else 1 - core)
-            for z in range(8):
-                start = pl.multiple_of((part + z * 8) * depth, depth)
-                wt_ref[pl.ds(start, depth), :] = refs_of[d][z * depth : (z + 1) * depth, :]
+    for other, refs_of in enumerate((own_core, other_core)):
+        side = core if other == 0 else 1 - core
+        way = 1 - 2 * side
+        for x_of, ref in zip((x, x - way, x + way, x + 2), refs_of):
+            blocks = [(z, side), (z + 4, side)]
+            for d in (1, 2, 3):
+                blocks += [(z - d * way, side), (z - d * way, 1 - side)]
+            for i, (z_of, core_of) in enumerate(blocks):
+                row = lax.rem(z_of + 8, 8) * 8 + lax.rem(x_of + 4, 4) * 2 + core_of
+                start = pl.multiple_of(row * depth, depth)
+                wt_ref[pl.ds(start, depth), :] = ref[i * depth : (i + 1) * depth, :]
     total = None
-    for d, m_ref in enumerate(grads):
-        cols = m_ref.shape[1]
+    own, right, across_up, across_down, left = [ref[...] for ref in grads]
+    across = jnp.concatenate([across_up, across_down], axis=0)
+    for d, held in enumerate((own, right, across, left)):
+        cols = held.shape[1]
         start = pl.multiple_of(lax.rem(y + (4 - d), 4) * cols, cols)
-        part = dot_nn(m_ref[...], wt_ref[pl.ds(start, cols), :])
+        part = dot_nn(held, wt_ref[pl.ds(start, cols), :])
         total = part if total is None else total + part
     grad = total.astype(jnp.bfloat16)
     for h in range(heads):
@@ -142,10 +156,14 @@
     scores = scores_of(q, k, k_wide)
     top = jnp.max(scores, axis=0, keepdims=True)
     weights = jnp.exp2((scores - top) * (SCALE * LOG2E))
-    probs = (weights * (1.0 / jnp.sum(weights, axis=0, keepdims=True))).astype(jnp.bfloat16)
+    probs = weights * (1.0 / jnp.sum(weights, axis=0, keepdims=True))
     probs_ref[0] = probs
-    att = dot_tn(v, probs)
-    att_wide_ref[0] = att
+    high = probs.astype(jnp.bfloat16)
+    rest = probs - high.astype(jnp.float32)
+    middle = rest.astype(jnp.bfloat16)
+    low = (rest - middle.astype(jnp.float32)).astype(jnp.bfloat16)
+    att = dot_tn(v, high)
+    att_wide_ref[0] = att + (dot_tn(v, middle) + dot_tn(v, low))
     back[where, :] = att.T
 
     @pl.when(h == pl.num_programs(0) - 1)
@@ -167,10 +185,10 @@
     q, k, v = heads_ref[0], heads_ref[1], heads_ref[2]
     probs = probs_ref[0]
     delta = jnp.sum(g_wide.T * att_ref[0], axis=0, keepdims=True)
-    dscores = (probs.astype(jnp.float32) * (dot_nt(v, g) - delta)).astype(jnp.bfloat16)
+    dscores = (probs * (dot_nt(v, g) - delta)).astype(jnp.bfloat16)
     back[0, where, :] = dot_tn(k, dscores).T * SCALE
     back[1, where, :] = dot_nn(dscores, q) * SCALE
-    back[2, where, :] = dot_nn(probs, g)
+    back[2, where, :] = dot_nn(probs.astype(jnp.bfloat16), g)
 
     @pl.when(h == pl.num_programs(0) - 1)
     def _():
@@ -220,8 +238,16 @@
     )
 
 
+def far_out(shape):
+    return pltpu.HBM(shape, jnp.bfloat16)
+
+
 def sds(shape, dtype=jnp.bfloat16):
     return jax.ShapeDtypeStruct(shape, dtype)
+
+
+def near(x):
+    return pltpu.with_memory_space_constraint(x, pltpu.VMEM)
 
 
 def exchange(x):
@@ -245,31 +271,31 @@
     def along(x, move):
         return lax.ppermute(x, "seq", [(place(*s), place(*move(*s))) for s in spots])
 
-    columns = [[place(z, x, c) for z in range(8)] for x in range(4) for c in range(2)]
-
     shard = out_weight.T
     depth, width = shard.shape
-    column = lax.all_to_all(
-        jnp.broadcast_to(shard[None], (8, depth, width)).reshape(8 * depth, width),
-        "seq",
-        split_axis=0,
-        concat_axis=0,
-        axis_index_groups=columns,
-        tiled=True,
-    )
+    pair = jnp.concatenate([shard, along(shard, lambda z, x, c: (z, x, c + 1))], axis=0)
+    far = along(shard, lambda z, x, c: (z + 4, x, c))
+    near_by = [along(pair, lambda z, x, c, d=d: (z + d * (1 - 2 * c), x, c)) for d in (1, 2, 3)]
+    column = call(collect_kernel, sds((8 * depth, width)), [], 5)(shard, far, *near_by)
     right, left = turn(mixed_grad, 1), turn(mixed_grad, 3)
 
     payload, slots = call(
         pack_kernel,
-        (sds((slots_all, 3 * HD)), sds((heads, tokens), jnp.int32)),
+        (far_out((slots_all, 3 * HD)), sds((heads, tokens), jnp.int32)),
         [pltpu.VMEM((3, slots_all, HD), jnp.float32)],
         4,
     )(cluster.transpose(0, 2, 1), query, key, value)
     payload, column = lax.optimization_barrier((payload, column))
     arrived = exchange(payload)
-    own_core = [column] + [along(column, lambda z, x, c, d=d: (z, x + d, c)) for d in (1, 2, 3)]
+    onward = lambda x: along(x, lambda z, x, c: (z, x + 1 - 2 * c, c))
+    passed = onward(column)
+    against = along(column, lambda z, x, c: (z, x - 1 + 2 * c, c))
+    half = tokens // 2
+    across = [turn(right[:half], 1), turn(left[half:], 3)]
+    relayed = onward(passed)
+    relayed, *across = lax.optimization_barrier((relayed, *across))
+    own_core = [column, passed, against, relayed]
     other_core = [along(part, lambda z, x, c: (z, x, c + 1)) for part in own_core]
-    across = turn(mixed_grad, 2)
 
 
     by_head = lambda *shape: pl.BlockSpec(shape, lambda h: (h, 0, 0))
@@ -277,9 +303,9 @@
         forward_kernel,
         grid=(heads,),
         out_shape=(
-            sds((slots_all, HD)),
+            far_out((slots_all, HD)),
             sds((heads * 3, rows, HD)),
-            sds((heads, rows, rows)),
+            sds((heads, rows, rows), jnp.float32),
             sds((heads, HD, rows), jnp.float32),
         ),
         in_specs=[pl.BlockSpec((slots_all, 3 * HD), lambda h: (0, 0))],
@@ -294,14 +320,14 @@
             pltpu.VMEM((slots_all, HD), jnp.float32),
         ],
         compiler_params=PARAMS,
-    )(arrived)
+    )(near(arrived))
 
     grad_payload, wt = call(
         grad_kernel,
-        (sds((slots_all, HD)), sds((64 * depth, width))),
+        (far_out((slots_all, HD)), sds((64 * depth, width))),
         [pltpu.VMEM((slots_all, HD), jnp.float32)],
-        13,
-    )(slots, mixed_grad, right, across, left, *own_core, *other_core)
+        14,
+    )(slots, mixed_grad, right, *across, left, *own_core, *other_core)
     grad_arrived = exchange(grad_payload)
     att, grad_arrived = lax.optimization_barrier((att, grad_arrived))
     att_back = exchange(att)
@@ -309,7 +335,7 @@
     done = pl.pallas_call(
         backward_kernel,
         grid=(heads,),
-        out_shape=sds((slots_all, 3 * HD)),
+        out_shape=far_out((slots_all, 3 * HD)),
         in_specs=[
             pl.BlockSpec((slots_all, HD), lambda h: (0, 0)),
             by_head(3, rows, HD),
@@ -322,7 +348,7 @@
             pltpu.VMEM((3, slots_all, HD), jnp.float32),
         ],
         compiler_params=PARAMS,
-    )(grad_arrived, held, probs, att_wide)
+    )(near(grad_arrived), held, probs, att_wide)
     back = exchange(done)
 
     cols = mixed_grad.shape[1]
@@ -331,7 +357,7 @@
         (sds((tokens, cols), jnp.float32),) + (sds((tokens, cols)),) * 3,
         [pltpu.VMEM((slots_all, HD), jnp.float32)],
         3,
-    )(slots, att_back, wt)
+    )(slots, near(att_back), near(wt))
     mixed = own
     for d, part in zip((1, 2, 3), sends):
         mixed = mixed + turn(part, d).astype(jnp.float32)
@@ -342,7 +368,7 @@
         (sds((tokens, heads * HD)),) * 3,
         [pltpu.VMEM((3, slots_all, HD), jnp.float32)],
         2,
-    )(slots, back)
+    )(slots, near(back))
     return (mixed, query_grad, key_grad, value_grad)
 
 

time: 227 us -> 216 us (0.952)
  local copies, waits for them, and re-layouts: 4.87 us -> 21.3 us
  waiting for transfers between devices: 124 us -> 109 us
  Pallas kernels: 41.2 us -> 29.6 us
    ppermute x6 -> x7, waiting for transfers between devices: 60.8 us -> 38.7 us  [turn(): return lax.ppermute(x, 'head', [(i, (i + d) % 4) for i in range(4)])]
    ppermute x7 -> x12, waiting for transfers between devices: 14.6 us -> 33.7 us  [along(): lax.ppermute(x, 'seq', [(place(*s), place(*move(*s))) for s in spots])]
    unnamed x30 -> x32, local copies, waits for them, and re-layouts: 3.19 us -> 21.2 us
    all_to_all x1 -> x0, waiting for transfers between devices: 11.9 us -> none  [local(): lax.all_to_all(jnp.broadcast_to(shard[None], (8, depth, width)).reshape(8...]
    all_to_all x1 -> x0, starting transfers between devices: 8.47 us -> none  [local(): lax.all_to_all(jnp.broadcast_to(shard[None], (8, depth, width)).reshape(8...]
    ppermute x7 -> x12, starting transfers between devices: 5.71 us -> 13.5 us  [along(): lax.ppermute(x, 'seq', [(place(*s), place(*move(*s))) for s in spots])]
    pallas_call x4 -> x5, Pallas kernels: 31 us -> 24.5 us  [the longest x1 9.12 us: local(): pl.pallas_call(forward_kernel, grid=(heads,), out_shape=(far_out((slots_a...]
    pallas_call x1, Pallas kernels: 5.81 us -> 2.47 us  [local(): call(mixed_kernel, (sds((tokens, cols), jnp.float32),) + (sds((tokens, co...]
  transfers between devices with their start and end apart: 18 -> 23, of which waited for: 11 -> 13; matrix products, arithmetic and copies ran while one was open for 1% -> 1% of each run, Pallas kernels for 16% -> 13%
where the time goes in v3:
time: 216 us; the launch traced here: 215 us
  waiting for transfers between devices  109 us (50%)
  starting transfers between devices  51.7 us (24%)
  Pallas kernels  29.6 us (14%)
  local copies, waits for them, and re-layouts  21.3 us (10%)
  other arithmetic  2.3 us (1%)
    ppermute x7, waiting for transfers between devices, turn(): return lax.ppermute(x, 'head', [(i, (i + d) % 4) for i in range(4)])  38.7 us
    all_to_all x4, waiting for transfers between devices, exchange(): return lax.all_to_all(x, 'seq', split_axis=0, concat_axis=0, tiled=True)  36.9 us
    ppermute x12, waiting for transfers between devices, along(): lax.ppermute(x, 'seq', [(place(*s), place(*move(*s))) for s in spots])  33.7 us
    all_to_all x4, starting transfers between devices, exchange(): return lax.all_to_all(x, 'seq', split_axis=0, concat_axis=0, tiled=True)  26.1 us
    unnamed x32, local copies, waits for them, and re-layouts  21.2 us
    ppermute x12, starting transfers between devices, along(): lax.ppermute(x, 'seq', [(place(*s), place(*move(*s))) for s in spots])  13.5 us
    ppermute x7, starting transfers between devices, turn(): return lax.ppermute(x, 'head', [(i, (i + d) % 4) for i in range(4)])  12.2 us
    pallas_call x1, Pallas kernels, local(): pl.pallas_call(forward_kernel, grid=(heads,), out_shape=(far_out((slots_a...  9.12 us
  transfers between devices with their start and end apart: 23, of which 13 were waited for; matrix products, arithmetic and copies ran while one was open for 1% of the time, Pallas kernels for 13%

profile of v3, /device:TPU:2, one launch (start us, length us, event | category | flops | bytes accessed | tf_op | source)
XLA Modules:
  0.0 215.0 jit_solution(7133250240411995883)
XLA Ops:
  0.7 1.4 collective-permute-done.1
  2.2 0.8 pad_maximum_fusion
  3.0 4.7 %collective-permute-start.4 = (bf16[128,512]{1,0:T(8,128)(2,1)S(1)}, bf16[128,512]{1,0:T(8,128)(2,1)S(1)}, u32[]{:S(2)}, u32[]{:S(2)}) collective-permute-start(bf16[128,512]{1,0:T(8,128)(2,1)S(1)} %pad_maximum_fusion), channel_id=1, source_target_pairs={{0,96},{4,164},{8,104},{12,172},{16,112},{20,180},{24,120},{28,188... | collective-permute-start | bytes 393224 | tf_op jit(solution)/shard_map/ppermute | solution.py:272
  7.7 3.6 %collective-permute-start.3 = (bf16[128,512]{1,0:T(8,128)(2,1)S(1)}, bf16[128,512]{1,0:T(8,128)(2,1)S(1)}, u32[]{:S(2)}, u32[]{:S(2)}) collective-permute-start(bf16[128,512]{1,0:T(8,128)(2,1)S(1)} %pad_maximum_fusion), channel_id=1, source_target_pairs={{0,64},{4,196},{8,72},{12,204},{16,80},{20,212},{24,88},{28,220},{... | collective-permute-start | bytes 393224 | tf_op jit(solution)/shard_map/ppermute | solution.py:272
  11.3 1.0 collective-permute-start.2
  12.9 1.0 copy-done.11
  13.9 1.0 copy-done.12
  14.9 1.0 copy-done.13
  16.6 4.3 %shard_map.93 = (bf16[3072,384]{1,0:T(8,128)(2,1)}, s32[4,384]{1,0:T(4,128)S(1)}) custom-call(s32[4,1,384]{2,1,0:T(1,128)S(1)} %bitcast.18, bf16[384,512]{1,0:T(8,128)(2,1)S(1)} %copy-done.11, bf16[384,512]{1,0:T(8,128)(2,1)S(1)} %copy-done.12, bf16[384,512]{1,0:T(8,128)(2,1)S(1)} %copy-done.13), custom_call_target="tpu_custom_call" | custom-call | tf_op jit(solution)/shard_map/pallas_call | solution.py:282
  20.9 3.5 %collective-permute-done.refs_1_ = bf16[64,512]{1,0:T(8,128)(2,1)S(1)} collective-permute-done((bf16[64,512]{1,0:T(8,128)(2,1)}, bf16[64,512]{1,0:T(8,128)(2,1)S(1)}, u32[]{:S(2)}, u32[]{:S(2)}) %collective-permute-start) | collective-permute-done | bytes 65568 | tf_op jit(solution)/shard_map/ppermute | solution.py:272
  24.4 0.8 copy-done.14
  25.2 7.7 %all-to-all-start = ((bf16[64,48,384]{2,1,0:T(8,128)(2,1)}), bf16[64,48,384]{2,1,0:T(8,128)(2,1)S(1)}, u32[]{:S(2)}, u32[]{:S(2)}) async-start(bf16[64,48,384]{2,1,0:T(8,128)(2,1)} %bitcast.20), calls=%async_computation | async-start | bytes 4718592 | tf_op jit(solution)/shard_map/all_to_all | solution.py:254
  33.0 1.7 collective-permute-start.5
  34.7 1.7 collective-permute-start.9
  36.3 1.5 collective-permute-start.6
  38.3 24.0 %collective-permute-done.6.refs_6_ = bf16[512,512]{1,0:T(8,128)(2,1)S(1)} collective-permute-done((bf16[512,512]{1,0:T(8,128)(2,1)S(1)}, bf16[512,512]{1,0:T(8,128)(2,1)S(1)}, u32[]{:S(2)}, u32[]{:S(2)}) %collective-permute-start.6) | collective-permute-done | bytes 524320 | tf_op jit(solution)/shard_map/ppermute | solution.py:272
  62.3 1.0 collective-permute-start.7
  63.3 1.7 collective-permute-start.8
  65.0 1.7 collective-permute-start.10
  67.3 5.1 %collective-permute-done.8.refs_2_ = bf16[192,1024]{1,0:T(8,128)(2,1)S(1)} collective-permute-done((bf16[192,1024]{1,0:T(8,128)(2,1)S(1)}, bf16[192,1024]{1,0:T(8,128)(2,1)S(1)}, u32[]{:S(2)}, u32[]{:S(2)}) %collective-permute-start.8) | collective-permute-done | bytes 393248 | tf_op jit(solution)/shard_map/ppermute | solution.py:264
  72.9 3.0 %collective-permute-done.7.refs_8_ = bf16[512,512]{1,0:T(8,128)(2,1)S(1)} collective-permute-done((bf16[512,512]{1,0:T(8,128)(2,1)S(1)}, bf16[512,512]{1,0:T(8,128)(2,1)S(1)}, u32[]{:S(2)}, u32[]{:S(2)}) %collective-permute-start.7) | collective-permute-done | bytes 524320 | tf_op jit(solution)/shard_map/ppermute | solution.py:272
  75.8 1.9 collective-permute-done.15.refs_12_
  77.7 3.8 %shard_map.96 = (bf16[3072,128]{1,0:T(8,128)(2,1)}, bf16[4096,512]{1,0:T(8,128)(2,1)S(1)}) custom-call(s32[4,384]{1,0:T(4,128)S(1)} %get-tuple-element.26.slots_ref, bf16[384,1024]{1,0:T(8,128)(2,1)S(1)} %copy-done.10, bf16[384,1024]{1,0:T(8,128)(2,1)S(1)} %collective-permute-done.5.refs_1_, bf16[192,1024]{1,0:T(8,128)(2,1)S(1)} %collective-permute-done.8.refs_2_, ...), custom_call_target="tpu_custom_call" | custom-call | tf_op jit(solution)/shard_map/pallas_call | solution.py:325
  81.5 2.1 copy-done.2
  83.6 6.3 %all-to-all-done = bf16[64,48,384]{2,1,0:T(8,128)(2,1)S(1)} async-done(((bf16[64,48,384]{2,1,0:T(8,128)(2,1)}), bf16[64,48,384]{2,1,0:T(8,128)(2,1)S(1)}, u32[]{:S(2)}, u32[]{:S(2)}) %all-to-all-start) | async-done | bytes 2359328 | tf_op jit(solution)/shard_map/all_to_all | solution.py:254
  89.9 6.4 %all-to-all-start.1 = ((bf16[64,48,128]{2,1,0:T(8,128)(2,1)}), bf16[64,48,128]{2,1,0:T(8,128)(2,1)S(1)}, u32[]{:S(2)}, u32[]{:S(2)}) async-start(bf16[64,48,128]{2,1,0:T(8,128)(2,1)} %bitcast.21), calls=%async_computation.1 | async-start | bytes 1572864 | tf_op jit(solution)/shard_map/all_to_all | solution.py:254
  96.3 9.1 %shard_map.95 = (bf16[3072,128]{1,0:T(8,128)(2,1)}, bf16[12,768,128]{2,1,0:T(8,128)(2,1)S(1)}, f32[4,768,768]{2,1,0:T(8,128)S(1)}, f32[4,128,768]{2,1,0:T(8,128)S(1)}) custom-call(bf16[3072,384]{1,0:T(8,128)(2,1)S(1)} %bitcast.10), custom_call_target="tpu_custom_call" | custom-call | tf_op jit(solution)/shard_map/pallas_call | solution.py:302
  105.4 3.6 %copy-done = f32[4,768,768]{2,1,0:T(8,128)} copy-done((f32[4,768,768]{2,1,0:T(8,128)}, f32[4,768,768]{2,1,0:T(8,128)S(1)}, u32[]{:S(2)}) %copy-start) | copy-done | bytes 9437208
  109.1 1.4 copy-done.6
  110.5 1.2 copy-done.8
  111.7 7.8 %all-to-all-done.1 = bf16[64,48,128]{2,1,0:T(8,128)(2,1)S(1)} async-done(((bf16[64,48,128]{2,1,0:T(8,128)(2,1)}), bf16[64,48,128]{2,1,0:T(8,128)(2,1)S(1)}, u32[]{:S(2)}, u32[]{:S(2)}) %all-to-all-start.1) | async-done | bytes 786464 | tf_op jit(solution)/shard_map/all_to_all | solution.py:254
  119.5 5.9 %all-to-all-start.2 = ((bf16[64,48,128]{2,1,0:T(8,128)(2,1)}), bf16[64,48,128]{2,1,0:T(8,128)(2,1)S(1)}, u32[]{:S(2)}, u32[]{:S(2)}) async-start(bf16[64,48,128]{2,1,0:T(8,128)(2,1)} %bitcast.22), calls=%async_computation.2 | async-start | bytes 1572864 | tf_op jit(solution)/shard_map/all_to_all | solution.py:254
  125.5 3.7 %copy-done.1 = f32[4,768,768]{2,1,0:T(8,128)S(1)} copy-done((f32[4,768,768]{2,1,0:T(8,128)S(1)}, f32[4,768,768]{2,1,0:T(8,128)}, u32[]{:S(2)}) %copy-start.1) | copy-done | bytes 9437208
  129.1 1.7 copy-done.7
  130.8 7.2 %shard_map.98 = bf16[3072,384]{1,0:T(8,128)(2,1)} custom-call(bf16[3072,128]{1,0:T(8,128)(2,1)S(1)} %bitcast.12, bf16[12,768,128]{2,1,0:T(8,128)(2,1)S(1)} %copy-done.7, f32[4,768,768]{2,1,0:T(8,128)S(1)} %copy-done.1, f32[4,128,768]{2,1,0:T(8,128)S(1)} %copy-done.9), custom_call_target="tpu_custom_call" | custom-call | tf_op jit(solution)/shard_map/pallas_call | solution.py:335
  138.0 10.6 %all-to-all-done.2 = bf16[64,48,128]{2,1,0:T(8,128)(2,1)S(1)} async-done(((bf16[64,48,128]{2,1,0:T(8,128)(2,1)}), bf16[64,48,128]{2,1,0:T(8,128)(2,1)S(1)}, u32[]{:S(2)}, u32[]{:S(2)}) %all-to-all-start.2) | async-done | bytes 786464 | tf_op jit(solution)/shard_map/all_to_all | solution.py:254
  148.6 0.9 copy-done.4
  149.5 6.0 %all-to-all-start.3 = ((bf16[64,48,384]{2,1,0:T(8,128)(2,1)}), bf16[64,48,384]{2,1,0:T(8,128)(2,1)S(1)}, u32[]{:S(2)}, u32[]{:S(2)}) async-start(bf16[64,48,384]{2,1,0:T(8,128)(2,1)} %bitcast.19), calls=%async_computation.3 | async-start | bytes 4718592 | tf_op jit(solution)/shard_map/all_to_all | solution.py:254
  155.5 2.2 %copy-done.3 = bf16[4096,512]{1,0:T(8,128)(2,1)S(1)} copy-done((bf16[4096,512]{1,0:T(8,128)(2,1)S(1)}, bf16[4096,512]{1,0:T(8,128)(2,1)}, u32[]{:S(2)}) %copy-start.3) | copy-done | bytes 4194328
  157.7 2.5 %shard_map.97 = (f32[384,1024]{1,0:T(8,128)S(1)}, bf16[384,1024]{1,0:T(8,128)(2,1)S(1)}, bf16[384,1024]{1,0:T(8,128)(2,1)S(1)}, bf16[384,1024]{1,0:T(8,128)(2,1)S(1)}) custom-call(s32[4,384]{1,0:T(4,128)S(1)} %get-tuple-element.26.slots_ref, bf16[3072,128]{1,0:T(8,128)(2,1)S(1)} %bitcast.13, bf16[4096,512]{1,0:T(8,128)(2,1)S(1)} %copy-done.3), custom_call_target="tpu_custom_call" | custom-call | tf_op jit(solution)/shard_map/pallas_call | solution.py:355
  160.1 1.2 collective-permute-start.16
  161.4 2.9 %collective-permute-start.17 = (bf16[384,1024]{1,0:T(8,128)(2,1)S(1)}, bf16[384,1024]{1,0:T(8,128)(2,1)S(1)}, u32[]{:S(2)}, u32[]{:S(2)}) collective-permute-start(bf16[384,1024]{1,0:T(8,128)(2,1)S(1)} %get-tuple-element.39), channel_id=1, source_target_pairs={{0,2},{1,3},{2,0},{3,1},{4,6},{5,7},{6,4},{7,5},{8,10},{9,11},{10,... | collective-permute-start | bytes 2359304 | tf_op jit(solution)/shard_map/ppermute | solution.py:264
  164.3 1.3 collective-permute-start.18
  165.6 15.4 %collective-permute-done.16 = bf16[384,1024]{1,0:T(8,128)(2,1)S(1)} collective-permute-done((bf16[384,1024]{1,0:T(8,128)(2,1)S(1)}, bf16[384,1024]{1,0:T(8,128)(2,1)S(1)}, u32[]{:S(2)}, u32[]{:S(2)}) %collective-permute-start.16) | collective-permute-done | bytes 786464 | tf_op jit(solution)/shard_map/ppermute | solution.py:264
  181.0 17.7 %collective-permute-done.17 = bf16[384,1024]{1,0:T(8,128)(2,1)S(1)} collective-permute-done((bf16[384,1024]{1,0:T(8,128)(2,1)S(1)}, bf16[384,1024]{1,0:T(8,128)(2,1)S(1)}, u32[]{:S(2)}, u32[]{:S(2)}) %collective-permute-start.17) | collective-permute-done | bytes 786464 | tf_op jit(solution)/shard_map/ppermute | solution.py:264
  198.7 1.4 add_convert_fusion
  200.1 12.2 %all-to-all-done.3 = bf16[64,48,384]{2,1,0:T(8,128)(2,1)S(1)} async-done(((bf16[64,48,384]{2,1,0:T(8,128)(2,1)}), bf16[64,48,384]{2,1,0:T(8,128)(2,1)S(1)}, u32[]{:S(2)}, u32[]{:S(2)}) %all-to-all-start.3) | async-done | bytes 2359328 | tf_op jit(solution)/shard_map/all_to_all | solution.py:254
  212.3 2.7 %shard_map.99 = (bf16[384,512]{1,0:T(8,128)(2,1)}, bf16[384,512]{1,0:T(8,128)(2,1)}, bf16[384,512]{1,0:T(8,128)(2,1)}) custom-call(s32[4,384]{1,0:T(4,128)S(1)} %get-tuple-element.26.slots_ref, bf16[3072,384]{1,0:T(8,128)(2,1)S(1)} %bitcast.11), custom_call_target="tpu_custom_call" | custom-call | tf_op jit(solution)/shard_map/pallas_call | solution.py:366
  (41 shorter events, 3.0 us)
Async XLA Ops:
  0.6 1.6 collective-permute-start.1
  3.0 21.3 %collective-permute-start.4 = (bf16[128,512]{1,0:T(8,128)(2,1)S(1)}, bf16[128,512]{1,0:T(8,128)(2,1)S(1)}, u32[]{:S(2)}, u32[]{:S(2)}) collective-permute-start(bf16[128,512]{1,0:T(8,128)(2,1)S(1)} %pad_maximum_fusion), channel_id=1, source_target_pairs={{0,96},{4,164},{8,104},{12,172},{16,112},{20,180},{24,120},{28,188... | collective-permute-start | bytes 393224 | tf_op jit(solution)/shard_map/ppermute | solution.py:272
  7.7 16.6 %collective-permute-start.3 = (bf16[128,512]{1,0:T(8,128)(2,1)S(1)}, bf16[128,512]{1,0:T(8,128)(2,1)S(1)}, u32[]{:S(2)}, u32[]{:S(2)}) collective-permute-start(bf16[128,512]{1,0:T(8,128)(2,1)S(1)} %pad_maximum_fusion), channel_id=1, source_target_pairs={{0,64},{4,196},{8,72},{12,204},{16,80},{20,212},{24,88},{28,220},{... | collective-permute-start | bytes 393224 | tf_op jit(solution)/shard_map/ppermute | solution.py:272
  11.3 13.0 %collective-permute-start.2 = (bf16[128,512]{1,0:T(8,128)(2,1)S(1)}, bf16[128,512]{1,0:T(8,128)(2,1)S(1)}, u32[]{:S(2)}, u32[]{:S(2)}) collective-permute-start(bf16[128,512]{1,0:T(8,128)(2,1)S(1)} %pad_maximum_fusion), channel_id=1, source_target_pairs={{0,32},{4,228},{8,40},{12,236},{16,48},{20,244},{24,56},{28,252},{... | collective-permute-start | bytes 393224 | tf_op jit(solution)/shard_map/ppermute | solution.py:272
  12.3 12.0 %collective-permute-start = (bf16[64,512]{1,0:T(8,128)(2,1)}, bf16[64,512]{1,0:T(8,128)(2,1)S(1)}, u32[]{:S(2)}, u32[]{:S(2)}) collective-permute-start(bf16[64,512]{1,0:T(8,128)(2,1)} %bitcast.16), channel_id=1, source_target_pairs={{0,128},{4,132},{8,136},{12,140},{16,144},{20,148},{24,152},{28,15... | collective-permute-start | bytes 196616 | tf_op jit(solution)/shard_map/ppermute | solution.py:272
  12.9 1.0 copy-start.11
  13.9 1.0 copy-start.12
  14.9 1.0 copy-start.13
  15.9 0.7 copy-start.15
  24.4 0.8 copy-start.14
  25.2 64.6 %all-to-all-start = ((bf16[64,48,384]{2,1,0:T(8,128)(2,1)}), bf16[64,48,384]{2,1,0:T(8,128)(2,1)S(1)}, u32[]{:S(2)}, u32[]{:S(2)}) async-start(bf16[64,48,384]{2,1,0:T(8,128)(2,1)} %bitcast.20), calls=%async_computation | async-start | bytes 4718592 | tf_op jit(solution)/shard_map/all_to_all | solution.py:254
  33.0 44.7 %copy-start.10 = (bf16[384,1024]{1,0:T(8,128)(2,1)S(1)}, bf16[384,1024]{1,0:T(8,128)(2,1)}, u32[]{:S(2)}) copy-start(bf16[384,1024]{1,0:T(8,128)(2,1)} %refs_0_.1) | copy-start | bytes 2359300
  33.0 30.3 %collective-permute-start.5 = (bf16[384,1024]{1,0:T(8,128)(2,1)}, bf16[384,1024]{1,0:T(8,128)(2,1)S(1)}, u32[]{:S(2)}, u32[]{:S(2)}) collective-permute-start(bf16[384,1024]{1,0:T(8,128)(2,1)} %refs_0_.1), channel_id=1, source_target_pairs={{0,1},{1,2},{2,3},{3,0},{4,5},{5,6},{6,7},{7,4},{8,9},{9,10},{10,1... | collective-permute-start | bytes 2359304 | tf_op jit(solution)/shard_map/ppermute | solution.py:264
  34.7 30.3 %collective-permute-start.9 = (bf16[384,1024]{1,0:T(8,128)(2,1)}, bf16[384,1024]{1,0:T(8,128)(2,1)S(1)}, u32[]{:S(2)}, u32[]{:S(2)}) collective-permute-start(bf16[384,1024]{1,0:T(8,128)(2,1)} %refs_0_.1), channel_id=1, source_target_pairs={{0,3},{1,0},{2,1},{3,2},{4,7},{5,4},{6,5},{7,6},{8,11},{9,8},{10,9... | collective-permute-start | bytes 2359304 | tf_op jit(solution)/shard_map/ppermute | solution.py:264
  36.3 26.0 %collective-permute-start.6 = (bf16[512,512]{1,0:T(8,128)(2,1)S(1)}, bf16[512,512]{1,0:T(8,128)(2,1)S(1)}, u32[]{:S(2)}, u32[]{:S(2)}) collective-permute-start(bf16[512,512]{1,0:T(8,128)(2,1)S(1)} %shard_map.94.refs_5_), channel_id=1, source_target_pairs={{0,8},{4,28},{8,16},{12,4},{16,24},{20,12},{24,0},{28,20},{32,40},... | collective-permute-start | bytes 1572872 | tf_op jit(solution)/shard_map/ppermute | solution.py:272
  37.8 29.0 %collective-permute-start.11 = (bf16[512,512]{1,0:T(8,128)(2,1)S(1)}, bf16[512,512]{1,0:T(8,128)(2,1)S(1)}, u32[]{:S(2)}, u32[]{:S(2)}) collective-permute-start(bf16[512,512]{1,0:T(8,128)(2,1)S(1)} %shard_map.94.refs_5_), channel_id=1, source_target_pairs={{0,24},{4,12},{8,0},{12,20},{16,8},{20,28},{24,16},{28,4},{32,56},... | collective-permute-start | bytes 1572872 | tf_op jit(solution)/shard_map/ppermute | solution.py:272
  62.3 13.5 %collective-permute-start.7 = (bf16[512,512]{1,0:T(8,128)(2,1)S(1)}, bf16[512,512]{1,0:T(8,128)(2,1)S(1)}, u32[]{:S(2)}, u32[]{:S(2)}) collective-permute-start(bf16[512,512]{1,0:T(8,128)(2,1)S(1)} %collective-permute-done.6.refs_6_), channel_id=1, source_target_pairs={{0,8},{4,28},{8,16},{12,4},{16,24},{20,12},{24,0},{28,20},{32,40},... | collective-permute-start | bytes 1572872 | tf_op jit(solution)/shard_map/ppermute | solution.py:272
  63.3 9.1 %collective-permute-start.8 = (bf16[192,1024]{1,0:T(8,128)(2,1)S(1)}, bf16[192,1024]{1,0:T(8,128)(2,1)S(1)}, u32[]{:S(2)}, u32[]{:S(2)}) collective-permute-start(bf16[192,1024]{1,0:T(8,128)(2,1)S(1)} %slice.8), channel_id=1, source_target_pairs={{0,1},{1,2},{2,3},{3,0},{4,5},{5,6},{6,7},{7,4},{8,9},{9,10},{10,1... | collective-permute-start | bytes 1179656 | tf_op jit(solution)/shard_map/ppermute | solution.py:264
  65.0 7.9 %collective-permute-start.10 = (bf16[192,1024]{1,0:T(8,128)(2,1)S(1)}, bf16[192,1024]{1,0:T(8,128)(2,1)S(1)}, u32[]{:S(2)}, u32[]{:S(2)}) collective-permute-start(bf16[192,1024]{1,0:T(8,128)(2,1)S(1)} %slice.9), channel_id=1, source_target_pairs={{0,3},{1,0},{2,1},{3,2},{4,7},{5,4},{6,5},{7,6},{8,11},{9,8},{10,9... | collective-permute-start | bytes 1179656 | tf_op jit(solution)/shard_map/ppermute | solution.py:264
  66.8 9.1 %collective-permute-start.12 = (bf16[512,512]{1,0:T(8,128)(2,1)S(1)}, bf16[512,512]{1,0:T(8,128)(2,1)S(1)}, u32[]{:S(2)}, u32[]{:S(2)}) collective-permute-start(bf16[512,512]{1,0:T(8,128)(2,1)S(1)} %shard_map.94.refs_5_), channel_id=1, source_target_pairs={{0,4},{4,0},{8,12},{12,8},{16,20},{20,16},{24,28},{28,24},{32,36},... | collective-permute-start | bytes 1572872 | tf_op jit(solution)/shard_map/ppermute | solution.py:272
  66.8 9.1 %collective-permute-start.13 = (bf16[512,512]{1,0:T(8,128)(2,1)S(1)}, bf16[512,512]{1,0:T(8,128)(2,1)S(1)}, u32[]{:S(2)}, u32[]{:S(2)}) collective-permute-start(bf16[512,512]{1,0:T(8,128)(2,1)S(1)} %collective-permute-done.6.refs_6_), channel_id=1, source_target_pairs={{0,4},{4,0},{8,12},{12,8},{16,20},{20,16},{24,28},{28,24},{32,36},... | collective-permute-start | bytes 1572872 | tf_op jit(solution)/shard_map/ppermute | solution.py:272
  72.4 3.4 %collective-permute-start.14 = (bf16[512,512]{1,0:T(8,128)(2,1)S(1)}, bf16[512,512]{1,0:T(8,128)(2,1)S(1)}, u32[]{:S(2)}, u32[]{:S(2)}) collective-permute-start(bf16[512,512]{1,0:T(8,128)(2,1)S(1)} %collective-permute-done.11.refs_7_), channel_id=1, source_target_pairs={{0,4},{4,0},{8,12},{12,8},{16,20},{20,16},{24,28},{28,24},{32,36},... | collective-permute-start | bytes 1572872 | tf_op jit(solution)/shard_map/ppermute | solution.py:272
  75.8 1.9 collective-permute-start.15
  81.5 2.1 copy-start.2
  89.9 29.6 %all-to-all-start.1 = ((bf16[64,48,128]{2,1,0:T(8,128)(2,1)}), bf16[64,48,128]{2,1,0:T(8,128)(2,1)S(1)}, u32[]{:S(2)}, u32[]{:S(2)}) async-start(bf16[64,48,128]{2,1,0:T(8,128)(2,1)} %bitcast.21), calls=%async_computation.1 | async-start | bytes 1572864 | tf_op jit(solution)/shard_map/all_to_all | solution.py:254
  105.4 3.6 %copy-start = (f32[4,768,768]{2,1,0:T(8,128)}, f32[4,768,768]{2,1,0:T(8,128)S(1)}, u32[]{:S(2)}) copy-start(f32[4,768,768]{2,1,0:T(8,128)S(1)} %get-tuple-element.43.probs_ref) | copy-start | bytes 28311556
  109.1 1.4 copy-start.6
  110.5 1.2 copy-start.8
  119.5 6.0 %copy-start.9 = (f32[4,128,768]{2,1,0:T(8,128)S(1)}, f32[4,128,768]{2,1,0:T(8,128)}, u32[]{:S(2)}) copy-start(f32[4,128,768]{2,1,0:T(8,128)} %copy-done.8) | copy-start | bytes 4718596
  119.5 29.1 %all-to-all-start.2 = ((bf16[64,48,128]{2,1,0:T(8,128)(2,1)}), bf16[64,48,128]{2,1,0:T(8,128)(2,1)S(1)}, u32[]{:S(2)}, u32[]{:S(2)}) async-start(bf16[64,48,128]{2,1,0:T(8,128)(2,1)} %bitcast.22), calls=%async_computation.2 | async-start | bytes 1572864 | tf_op jit(solution)/shard_map/all_to_all | solution.py:254
  125.5 3.7 %copy-start.1 = (f32[4,768,768]{2,1,0:T(8,128)S(1)}, f32[4,768,768]{2,1,0:T(8,128)}, u32[]{:S(2)}) copy-start(f32[4,768,768]{2,1,0:T(8,128)} %copy-done) | copy-start | bytes 28311556
  129.1 1.7 copy-start.7
  148.6 0.9 copy-start.4
  149.5 6.0 %copy-start.5 = (bf16[64,48,128]{2,1,0:T(8,128)(2,1)S(1)}, bf16[64,48,128]{2,1,0:T(8,128)(2,1)}, u32[]{:S(2)}) copy-start(bf16[64,48,128]{2,1,0:T(8,128)(2,1)} %copy-done.4) | copy-start | bytes 2359300
  149.5 62.8 %all-to-all-start.3 = ((bf16[64,48,384]{2,1,0:T(8,128)(2,1)}), bf16[64,48,384]{2,1,0:T(8,128)(2,1)S(1)}, u32[]{:S(2)}, u32[]{:S(2)}) async-start(bf16[64,48,384]{2,1,0:T(8,128)(2,1)} %bitcast.19), calls=%async_computation.3 | async-start | bytes 4718592 | tf_op jit(solution)/shard_map/all_to_all | solution.py:254
  155.5 2.2 %copy-start.3 = (bf16[4096,512]{1,0:T(8,128)(2,1)S(1)}, bf16[4096,512]{1,0:T(8,128)(2,1)}, u32[]{:S(2)}) copy-start(bf16[4096,512]{1,0:T(8,128)(2,1)} %copy-done.2) | copy-start | bytes 12582916
  160.1 20.9 %collective-permute-start.16 = (bf16[384,1024]{1,0:T(8,128)(2,1)S(1)}, bf16[384,1024]{1,0:T(8,128)(2,1)S(1)}, u32[]{:S(2)}, u32[]{:S(2)}) collective-permute-start(bf16[384,1024]{1,0:T(8,128)(2,1)S(1)} %get-tuple-element.38), channel_id=1, source_target_pairs={{0,1},{1,2},{2,3},{3,0},{4,5},{5,6},{6,7},{7,4},{8,9},{9,10},{10,1... | collective-permute-start | bytes 2359304 | tf_op jit(solution)/shard_map/ppermute | solution.py:264
  161.4 37.3 %collective-permute-start.17 = (bf16[384,1024]{1,0:T(8,128)(2,1)S(1)}, bf16[384,1024]{1,0:T(8,128)(2,1)S(1)}, u32[]{:S(2)}, u32[]{:S(2)}) collective-permute-start(bf16[384,1024]{1,0:T(8,128)(2,1)S(1)} %get-tuple-element.39), channel_id=1, source_target_pairs={{0,2},{1,3},{2,0},{3,1},{4,6},{5,7},{6,4},{7,5},{8,10},{9,11},{10,... | collective-permute-start | bytes 2359304 | tf_op jit(solution)/shard_map/ppermute | solution.py:264
  164.3 34.4 %collective-permute-start.18 = (bf16[384,1024]{1,0:T(8,128)(2,1)S(1)}, bf16[384,1024]{1,0:T(8,128)(2,1)S(1)}, u32[]{:S(2)}, u32[]{:S(2)}) collective-permute-start(bf16[384,1024]{1,0:T(8,128)(2,1)S(1)} %get-tuple-element.40), channel_id=1, source_target_pairs={{0,3},{1,0},{2,1},{3,2},{4,7},{5,4},{6,5},{7,6},{8,11},{9,8},{10,9... | collective-permute-start | bytes 2359304 | tf_op jit(solution)/shard_map/ppermute | solution.py:264

commit v4 on v3

--- a/solution.py
+++ b/solution.py
@@ -227,9 +227,13 @@
             ref[:, head_cols(h)] = got[:, t * HD : (t + 1) * HD]
 
 
-def call(kernel, out, scratch, count):
+def call(kernel, out, scratch, count, micros=None):
+    cost = None
+    if micros is not None:
+        cost = pl.CostEstimate(flops=int(micros * 1.15e9), bytes_accessed=0, transcendentals=0)
     return pl.pallas_call(
         kernel,
+        cost_estimate=cost,
         out_shape=out,
         in_specs=[VMEM] * count,
         out_specs=jax.tree.map(lambda _: VMEM, out),
@@ -250,6 +254,10 @@
     return pltpu.with_memory_space_constraint(x, pltpu.VMEM)
 
 
+def far(x):
+    return pltpu.with_memory_space_constraint(x, pltpu.HBM)
+
+
 def exchange(x):
     return lax.all_to_all(x, "seq", split_axis=0, concat_axis=0, tiled=True)
 
@@ -274,9 +282,9 @@
     shard = out_weight.T
     depth, width = shard.shape
     pair = jnp.concatenate([shard, along(shard, lambda z, x, c: (z, x, c + 1))], axis=0)
-    far = along(shard, lambda z, x, c: (z + 4, x, c))
+    opposite = along(shard, lambda z, x, c: (z + 4, x, c))
     near_by = [along(pair, lambda z, x, c, d=d: (z + d * (1 - 2 * c), x, c)) for d in (1, 2, 3)]
-    column = call(collect_kernel, sds((8 * depth, width)), [], 5)(shard, far, *near_by)
+    column = call(collect_kernel, sds((8 * depth, width)), [], 5, micros=60)(shard, opposite, *near_by)
     right, left = turn(mixed_grad, 1), turn(mixed_grad, 3)
 
     payload, slots = call(
@@ -284,8 +292,7 @@
         (far_out((slots_all, 3 * HD)), sds((heads, tokens), jnp.int32)),
         [pltpu.VMEM((3, slots_all, HD), jnp.float32)],
         4,
-    )(cluster.transpose(0, 2, 1), query, key, value)
-    payload, column = lax.optimization_barrier((payload, column))
+    )(far(cluster.transpose(0, 2, 1)), far(query), far(key), far(value))
     arrived = exchange(payload)
     onward = lambda x: along(x, lambda z, x, c: (z, x + 1 - 2 * c, c))
     passed = onward(column)

time: 216 us -> 214 us (level)
  local copies, waits for them, and re-layouts: 21.3 us -> 16.7 us
  waiting for transfers between devices: 109 us -> 106 us
  starting transfers between devices: 51.7 us -> 54.5 us
    ppermute x12, waiting for transfers between devices: 33.7 us -> 29.1 us  [along(): lax.ppermute(x, 'seq', [(place(*s), place(*move(*s))) for s in spots])]
    unnamed x32 -> x24, local copies, waits for them, and re-layouts: 21.2 us -> 16.7 us
    all_to_all x4, starting transfers between devices: 26.1 us -> 28.7 us  [exchange(): return lax.all_to_all(x, 'seq', split_axis=0, concat_axis=0, tiled=True)]
  transfers between devices with their start and end apart: 23 -> 23, of which waited for: 13 -> 13; matrix products, arithmetic and copies ran while one was open for 1% -> 1% of each run, Pallas kernels for 13% -> 14%
where the time goes in v4:
time: 214 us; the launch traced here: 213 us
  waiting for transfers between devices  106 us (50%)
  starting transfers between devices  54.5 us (25%)
  Pallas kernels  31.7 us (15%)
  local copies, waits for them, and re-layouts  16.7 us (8%)
  other arithmetic  2.95 us (1%)
    ppermute x7, waiting for transfers between devices, turn(): return lax.ppermute(x, 'head', [(i, (i + d) % 4) for i in range(4)])  38.7 us
    all_to_all x4, waiting for transfers between devices, exchange(): return lax.all_to_all(x, 'seq', split_axis=0, concat_axis=0, tiled=True)  38.4 us
    ppermute x12, waiting for transfers between devices, along(): lax.ppermute(x, 'seq', [(place(*s), place(*move(*s))) for s in spots])  29.1 us
    all_to_all x4, starting transfers between devices, exchange(): return lax.all_to_all(x, 'seq', split_axis=0, concat_axis=0, tiled=True)  28.7 us
    unnamed x24, local copies, waits for them, and re-layouts  16.7 us
    ppermute x12, starting transfers between devices, along(): lax.ppermute(x, 'seq', [(place(*s), place(*move(*s))) for s in spots])  14 us
    ppermute x7, starting transfers between devices, turn(): return lax.ppermute(x, 'head', [(i, (i + d) % 4) for i in range(4)])  11.9 us
    pallas_call x1, Pallas kernels, local(): pl.pallas_call(forward_kernel, grid=(heads,), out_shape=(far_out((slots_a...  9.13 us
  transfers between devices with their start and end apart: 23, of which 13 were waited for; matrix products, arithmetic and copies ran while one was open for 1% of the time, Pallas kernels for 14%

profile of v4, /device:TPU:2, one launch (start us, length us, event | category | flops | bytes accessed | tf_op | source)
XLA Modules:
  0.0 212.9 jit_solution(1914877364344037052)
XLA Ops:
  0.7 1.4 collective-permute-done.2
  2.2 1.5 pad_maximum_fusion
  3.7 4.6 %collective-permute-start.5 = (bf16[128,512]{1,0:T(8,128)(2,1)}, bf16[128,512]{1,0:T(8,128)(2,1)S(1)}, u32[]{:S(2)}, u32[]{:S(2)}) collective-permute-start(bf16[128,512]{1,0:T(8,128)(2,1)} %pad_maximum_fusion), channel_id=1, source_target_pairs={{0,96},{4,164},{8,104},{12,172},{16,112},{20,180},{24,120},{28,188... | collective-permute-start | bytes 393224 | tf_op jit(solution)/shard_map/ppermute | solution.py:280
  8.3 3.6 %collective-permute-start.4 = (bf16[128,512]{1,0:T(8,128)(2,1)}, bf16[128,512]{1,0:T(8,128)(2,1)S(1)}, u32[]{:S(2)}, u32[]{:S(2)}) collective-permute-start(bf16[128,512]{1,0:T(8,128)(2,1)} %pad_maximum_fusion), channel_id=1, source_target_pairs={{0,64},{4,196},{8,72},{12,204},{16,80},{20,212},{24,88},{28,220},{... | collective-permute-start | bytes 393224 | tf_op jit(solution)/shard_map/ppermute | solution.py:280
  11.9 1.0 collective-permute-start.3
  12.9 0.5 collective-permute-start.1
  13.5 1.6 collective-permute-start
  15.0 5.6 %shard_map.93 = (bf16[3072,384]{1,0:T(8,128)(2,1)}, s32[4,384]{1,0:T(4,128)S(1)}) custom-call(s32[4,1,384]{2,1,0:T(1,128)} %bitcast.22, bf16[384,512]{1,0:T(8,128)(2,1)} %q_ref.1, bf16[384,512]{1,0:T(8,128)(2,1)} %k_ref.1, bf16[384,512]{1,0:T(8,128)(2,1)} %v_ref.1), custom_call_target="tpu_custom_call" | custom-call | tf_op jit(solution)/shard_map/pallas_call | solution.py:290
  20.6 10.4 %all-to-all-start = ((bf16[64,48,384]{2,1,0:T(8,128)(2,1)}), bf16[64,48,384]{2,1,0:T(8,128)(2,1)S(1)}, u32[]{:S(2)}, u32[]{:S(2)}) async-start(bf16[64,48,384]{2,1,0:T(8,128)(2,1)} %bitcast.19), calls=%async_computation | async-start | bytes 4718592 | tf_op jit(solution)/shard_map/all_to_all | solution.py:262
  31.0 1.7 collective-permute-start.9
  32.7 0.9 shard_map.95.refs_5_
  33.7 1.5 collective-permute-start.6
  35.2 0.6 collective-permute-start.11
  35.8 24.0 %collective-permute-done.6.refs_6_ = bf16[512,512]{1,0:T(8,128)(2,1)S(1)} collective-permute-done((bf16[512,512]{1,0:T(8,128)(2,1)S(1)}, bf16[512,512]{1,0:T(8,128)(2,1)S(1)}, u32[]{:S(2)}, u32[]{:S(2)}) %collective-permute-start.6) | collective-permute-done | bytes 524320 | tf_op jit(solution)/shard_map/ppermute | solution.py:280
  59.8 1.5 collective-permute-start.7
  61.3 1.6 collective-permute-start.8
  63.0 1.7 collective-permute-start.10
  64.7 0.5 collective-permute-start.13
  65.2 5.1 %collective-permute-done.8.refs_2_ = bf16[192,1024]{1,0:T(8,128)(2,1)S(1)} collective-permute-done((bf16[192,1024]{1,0:T(8,128)(2,1)S(1)}, bf16[192,1024]{1,0:T(8,128)(2,1)S(1)}, u32[]{:S(2)}, u32[]{:S(2)}) %collective-permute-start.8) | collective-permute-done | bytes 393248 | tf_op jit(solution)/shard_map/ppermute | solution.py:272
  70.8 1.7 collective-permute-done.7.refs_8_
  72.6 1.9 collective-permute-done.15.refs_12_
  74.5 3.8 %shard_map.96 = (bf16[3072,128]{1,0:T(8,128)(2,1)}, bf16[4096,512]{1,0:T(8,128)(2,1)S(1)}) custom-call(s32[4,384]{1,0:T(4,128)S(1)} %get-tuple-element.24.slots_ref, bf16[384,1024]{1,0:T(8,128)(2,1)S(1)} %copy-done.10, bf16[384,1024]{1,0:T(8,128)(2,1)S(1)} %collective-permute-done.refs_1_, bf16[192,1024]{1,0:T(8,128)(2,1)S(1)} %collective-permute-done.8.refs_2_, ...), custom_call_target="tpu_custom_call" | custom-call | tf_op jit(solution)/shard_map/pallas_call | solution.py:332
  78.3 2.0 copy-done.2
  80.3 7.5 %all-to-all-done = bf16[64,48,384]{2,1,0:T(8,128)(2,1)S(1)} async-done(((bf16[64,48,384]{2,1,0:T(8,128)(2,1)}), bf16[64,48,384]{2,1,0:T(8,128)(2,1)S(1)}, u32[]{:S(2)}, u32[]{:S(2)}) %all-to-all-start) | async-done | bytes 2359328 | tf_op jit(solution)/shard_map/all_to_all | solution.py:262
  87.8 6.4 %all-to-all-start.1 = ((bf16[64,48,128]{2,1,0:T(8,128)(2,1)}), bf16[64,48,128]{2,1,0:T(8,128)(2,1)S(1)}, u32[]{:S(2)}, u32[]{:S(2)}) async-start(bf16[64,48,128]{2,1,0:T(8,128)(2,1)} %bitcast.20), calls=%async_computation.1 | async-start | bytes 1572864 | tf_op jit(solution)/shard_map/all_to_all | solution.py:262
  94.2 9.1 %shard_map.94 = (bf16[3072,128]{1,0:T(8,128)(2,1)}, bf16[12,768,128]{2,1,0:T(8,128)(2,1)S(1)}, f32[4,768,768]{2,1,0:T(8,128)S(1)}, f32[4,128,768]{2,1,0:T(8,128)S(1)}) custom-call(bf16[3072,384]{1,0:T(8,128)(2,1)S(1)} %bitcast.10), custom_call_target="tpu_custom_call" | custom-call | tf_op jit(solution)/shard_map/pallas_call | solution.py:309
  103.4 3.6 %copy-done = f32[4,768,768]{2,1,0:T(8,128)} copy-done((f32[4,768,768]{2,1,0:T(8,128)}, f32[4,768,768]{2,1,0:T(8,128)S(1)}, u32[]{:S(2)}) %copy-start) | copy-done | bytes 9437208
  107.0 1.4 copy-done.6
  108.4 1.2 copy-done.8
  109.6 7.8 %all-to-all-done.1 = bf16[64,48,128]{2,1,0:T(8,128)(2,1)S(1)} async-done(((bf16[64,48,128]{2,1,0:T(8,128)(2,1)}), bf16[64,48,128]{2,1,0:T(8,128)(2,1)S(1)}, u32[]{:S(2)}, u32[]{:S(2)}) %all-to-all-start.1) | async-done | bytes 786464 | tf_op jit(solution)/shard_map/all_to_all | solution.py:262
  117.4 5.9 %all-to-all-start.2 = ((bf16[64,48,128]{2,1,0:T(8,128)(2,1)}), bf16[64,48,128]{2,1,0:T(8,128)(2,1)S(1)}, u32[]{:S(2)}, u32[]{:S(2)}) async-start(bf16[64,48,128]{2,1,0:T(8,128)(2,1)} %bitcast.21), calls=%async_computation.2 | async-start | bytes 1572864 | tf_op jit(solution)/shard_map/all_to_all | solution.py:262
  123.4 3.7 %copy-done.1 = f32[4,768,768]{2,1,0:T(8,128)S(1)} copy-done((f32[4,768,768]{2,1,0:T(8,128)S(1)}, f32[4,768,768]{2,1,0:T(8,128)}, u32[]{:S(2)}) %copy-start.1) | copy-done | bytes 9437208
  127.1 1.7 copy-done.7
  128.7 7.2 %shard_map.98 = bf16[3072,384]{1,0:T(8,128)(2,1)} custom-call(bf16[3072,128]{1,0:T(8,128)(2,1)S(1)} %bitcast.12, bf16[12,768,128]{2,1,0:T(8,128)(2,1)S(1)} %copy-done.7, f32[4,768,768]{2,1,0:T(8,128)S(1)} %copy-done.1, f32[4,128,768]{2,1,0:T(8,128)S(1)} %copy-done.9), custom_call_target="tpu_custom_call" | custom-call | tf_op jit(solution)/shard_map/pallas_call | solution.py:342
  135.9 10.6 %all-to-all-done.2 = bf16[64,48,128]{2,1,0:T(8,128)(2,1)S(1)} async-done(((bf16[64,48,128]{2,1,0:T(8,128)(2,1)}), bf16[64,48,128]{2,1,0:T(8,128)(2,1)S(1)}, u32[]{:S(2)}, u32[]{:S(2)}) %all-to-all-start.2) | async-done | bytes 786464 | tf_op jit(solution)/shard_map/all_to_all | solution.py:262
  146.6 0.9 copy-done.4
  147.4 6.0 %all-to-all-start.3 = ((bf16[64,48,384]{2,1,0:T(8,128)(2,1)}), bf16[64,48,384]{2,1,0:T(8,128)(2,1)S(1)}, u32[]{:S(2)}, u32[]{:S(2)}) async-start(bf16[64,48,384]{2,1,0:T(8,128)(2,1)} %bitcast.18), calls=%async_computation.3 | async-start | bytes 4718592 | tf_op jit(solution)/shard_map/all_to_all | solution.py:262
  153.4 2.2 %copy-done.3 = bf16[4096,512]{1,0:T(8,128)(2,1)S(1)} copy-done((bf16[4096,512]{1,0:T(8,128)(2,1)S(1)}, bf16[4096,512]{1,0:T(8,128)(2,1)}, u32[]{:S(2)}) %copy-start.3) | copy-done | bytes 4194328
  155.6 2.5 %shard_map.97 = (f32[384,1024]{1,0:T(8,128)S(1)}, bf16[384,1024]{1,0:T(8,128)(2,1)S(1)}, bf16[384,1024]{1,0:T(8,128)(2,1)S(1)}, bf16[384,1024]{1,0:T(8,128)(2,1)S(1)}) custom-call(s32[4,384]{1,0:T(4,128)S(1)} %get-tuple-element.24.slots_ref, bf16[3072,128]{1,0:T(8,128)(2,1)S(1)} %bitcast.13, bf16[4096,512]{1,0:T(8,128)(2,1)S(1)} %copy-done.3), custom_call_target="tpu_custom_call" | custom-call | tf_op jit(solution)/shard_map/pallas_call | solution.py:362
  158.1 0.7 collective-permute-start.16
  158.8 2.5 %collective-permute-start.17 = (bf16[384,1024]{1,0:T(8,128)(2,1)S(1)}, bf16[384,1024]{1,0:T(8,128)(2,1)S(1)}, u32[]{:S(2)}, u32[]{:S(2)}) collective-permute-start(bf16[384,1024]{1,0:T(8,128)(2,1)S(1)} %get-tuple-element.35), channel_id=1, source_target_pairs={{0,2},{1,3},{2,0},{3,1},{4,6},{5,7},{6,4},{7,5},{8,10},{9,11},{10,... | collective-permute-start | bytes 2359304 | tf_op jit(solution)/shard_map/ppermute | solution.py:272
  161.3 2.0 collective-permute-start.18
  163.3 16.5 %collective-permute-done.16 = bf16[384,1024]{1,0:T(8,128)(2,1)S(1)} collective-permute-done((bf16[384,1024]{1,0:T(8,128)(2,1)S(1)}, bf16[384,1024]{1,0:T(8,128)(2,1)S(1)}, u32[]{:S(2)}, u32[]{:S(2)}) %collective-permute-start.16) | collective-permute-done | bytes 786464 | tf_op jit(solution)/shard_map/ppermute | solution.py:272
  179.8 16.1 %collective-permute-done.17 = bf16[384,1024]{1,0:T(8,128)(2,1)S(1)} collective-permute-done((bf16[384,1024]{1,0:T(8,128)(2,1)S(1)}, bf16[384,1024]{1,0:T(8,128)(2,1)S(1)}, u32[]{:S(2)}, u32[]{:S(2)}) %collective-permute-start.17) | collective-permute-done | bytes 786464 | tf_op jit(solution)/shard_map/ppermute | solution.py:272
  195.8 0.6 collective-permute-done.18
  196.4 1.5 add_convert_fusion
  197.9 12.4 %all-to-all-done.3 = bf16[64,48,384]{2,1,0:T(8,128)(2,1)S(1)} async-done(((bf16[64,48,384]{2,1,0:T(8,128)(2,1)}), bf16[64,48,384]{2,1,0:T(8,128)(2,1)S(1)}, u32[]{:S(2)}, u32[]{:S(2)}) %all-to-all-start.3) | async-done | bytes 2359328 | tf_op jit(solution)/shard_map/all_to_all | solution.py:262
  210.3 2.6 %shard_map.99 = (bf16[384,512]{1,0:T(8,128)(2,1)}, bf16[384,512]{1,0:T(8,128)(2,1)}, bf16[384,512]{1,0:T(8,128)(2,1)}) custom-call(s32[4,384]{1,0:T(4,128)S(1)} %get-tuple-element.24.slots_ref, bf16[3072,384]{1,0:T(8,128)(2,1)S(1)} %bitcast.11), custom_call_target="tpu_custom_call" | custom-call | tf_op jit(solution)/shard_map/pallas_call | solution.py:373
  (33 shorter events, 0.7 us)
Async XLA Ops:
  0.6 1.6 collective-permute-start.2
  3.7 29.0 %collective-permute-start.5 = (bf16[128,512]{1,0:T(8,128)(2,1)}, bf16[128,512]{1,0:T(8,128)(2,1)S(1)}, u32[]{:S(2)}, u32[]{:S(2)}) collective-permute-start(bf16[128,512]{1,0:T(8,128)(2,1)} %pad_maximum_fusion), channel_id=1, source_target_pairs={{0,96},{4,164},{8,104},{12,172},{16,112},{20,180},{24,120},{28,188... | collective-permute-start | bytes 393224 | tf_op jit(solution)/shard_map/ppermute | solution.py:280
  8.3 24.4 %collective-permute-start.4 = (bf16[128,512]{1,0:T(8,128)(2,1)}, bf16[128,512]{1,0:T(8,128)(2,1)S(1)}, u32[]{:S(2)}, u32[]{:S(2)}) collective-permute-start(bf16[128,512]{1,0:T(8,128)(2,1)} %pad_maximum_fusion), channel_id=1, source_target_pairs={{0,64},{4,196},{8,72},{12,204},{16,80},{20,212},{24,88},{28,220},{... | collective-permute-start | bytes 393224 | tf_op jit(solution)/shard_map/ppermute | solution.py:280
  11.9 20.8 %collective-permute-start.3 = (bf16[128,512]{1,0:T(8,128)(2,1)}, bf16[128,512]{1,0:T(8,128)(2,1)}, u32[]{:S(2)}, u32[]{:S(2)}) collective-permute-start(bf16[128,512]{1,0:T(8,128)(2,1)} %pad_maximum_fusion), channel_id=1, source_target_pairs={{0,32},{4,228},{8,40},{12,236},{16,48},{20,244},{24,56},{28,252},{... | collective-permute-start | bytes 393224 | tf_op jit(solution)/shard_map/ppermute | solution.py:280
  12.9 18.1 %collective-permute-start.1 = (bf16[64,512]{1,0:T(8,128)(2,1)}, bf16[64,512]{1,0:T(8,128)(2,1)S(1)}, u32[]{:S(2)}, u32[]{:S(2)}) collective-permute-start(bf16[64,512]{1,0:T(8,128)(2,1)} %bitcast.16), channel_id=1, source_target_pairs={{0,128},{4,132},{8,136},{12,140},{16,144},{20,148},{24,152},{28,15... | collective-permute-start | bytes 196616 | tf_op jit(solution)/shard_map/ppermute | solution.py:280
  13.5 47.8 %collective-permute-start = (bf16[384,1024]{1,0:T(8,128)(2,1)}, bf16[384,1024]{1,0:T(8,128)(2,1)S(1)}, u32[]{:S(2)}, u32[]{:S(2)}) collective-permute-start(bf16[384,1024]{1,0:T(8,128)(2,1)} %refs_0_.1), channel_id=1, source_target_pairs={{0,1},{1,2},{2,3},{3,0},{4,5},{5,6},{6,7},{7,4},{8,9},{9,10},{10,1... | collective-permute-start | bytes 2359304 | tf_op jit(solution)/shard_map/ppermute | solution.py:272
  20.6 12.1 %copy-start.11 = (bf16[512,64]{0,1:T(8,128)(2,1)S(1)}, bf16[512,64]{0,1:T(8,128)(2,1)}, u32[]{:S(2)}) copy-start(bf16[512,64]{0,1:T(8,128)(2,1)} %param.10) | copy-start | bytes 196612
  20.6 67.3 %all-to-all-start = ((bf16[64,48,384]{2,1,0:T(8,128)(2,1)}), bf16[64,48,384]{2,1,0:T(8,128)(2,1)S(1)}, u32[]{:S(2)}, u32[]{:S(2)}) async-start(bf16[64,48,384]{2,1,0:T(8,128)(2,1)} %bitcast.19), calls=%async_computation | async-start | bytes 4718592 | tf_op jit(solution)/shard_map/all_to_all | solution.py:262
  31.0 32.0 %collective-permute-start.9 = (bf16[384,1024]{1,0:T(8,128)(2,1)}, bf16[384,1024]{1,0:T(8,128)(2,1)S(1)}, u32[]{:S(2)}, u32[]{:S(2)}) collective-permute-start(bf16[384,1024]{1,0:T(8,128)(2,1)} %refs_0_.1), channel_id=1, source_target_pairs={{0,3},{1,0},{2,1},{3,2},{4,7},{5,4},{6,5},{7,6},{8,11},{9,8},{10,9... | collective-permute-start | bytes 2359304 | tf_op jit(solution)/shard_map/ppermute | solution.py:272
  33.7 40.8 %copy-start.10 = (bf16[384,1024]{1,0:T(8,128)(2,1)S(1)}, bf16[384,1024]{1,0:T(8,128)(2,1)}, u32[]{:S(2)}) copy-start(bf16[384,1024]{1,0:T(8,128)(2,1)} %refs_0_.1) | copy-start | bytes 2359300
  33.7 26.1 %collective-permute-start.6 = (bf16[512,512]{1,0:T(8,128)(2,1)S(1)}, bf16[512,512]{1,0:T(8,128)(2,1)S(1)}, u32[]{:S(2)}, u32[]{:S(2)}) collective-permute-start(bf16[512,512]{1,0:T(8,128)(2,1)S(1)} %shard_map.95.refs_5_), channel_id=1, source_target_pairs={{0,8},{4,28},{8,16},{12,4},{16,24},{20,12},{24,0},{28,20},{32,40},... | collective-permute-start | bytes 1572872 | tf_op jit(solution)/shard_map/ppermute | solution.py:280
  35.2 29.5 %collective-permute-start.11 = (bf16[512,512]{1,0:T(8,128)(2,1)S(1)}, bf16[512,512]{1,0:T(8,128)(2,1)S(1)}, u32[]{:S(2)}, u32[]{:S(2)}) collective-permute-start(bf16[512,512]{1,0:T(8,128)(2,1)S(1)} %shard_map.95.refs_5_), channel_id=1, source_target_pairs={{0,24},{4,12},{8,0},{12,20},{16,8},{20,28},{24,16},{28,4},{32,56},... | collective-permute-start | bytes 1572872 | tf_op jit(solution)/shard_map/ppermute | solution.py:280
  59.8 12.8 %collective-permute-start.7 = (bf16[512,512]{1,0:T(8,128)(2,1)S(1)}, bf16[512,512]{1,0:T(8,128)(2,1)S(1)}, u32[]{:S(2)}, u32[]{:S(2)}) collective-permute-start(bf16[512,512]{1,0:T(8,128)(2,1)S(1)} %collective-permute-done.6.refs_6_), channel_id=1, source_target_pairs={{0,8},{4,28},{8,16},{12,4},{16,24},{20,12},{24,0},{28,20},{32,40},... | collective-permute-start | bytes 1572872 | tf_op jit(solution)/shard_map/ppermute | solution.py:280
  61.3 9.1 %collective-permute-start.8 = (bf16[192,1024]{1,0:T(8,128)(2,1)S(1)}, bf16[192,1024]{1,0:T(8,128)(2,1)S(1)}, u32[]{:S(2)}, u32[]{:S(2)}) collective-permute-start(bf16[192,1024]{1,0:T(8,128)(2,1)S(1)} %slice.8), channel_id=1, source_target_pairs={{0,1},{1,2},{2,3},{3,0},{4,5},{5,6},{6,7},{7,4},{8,9},{9,10},{10,1... | collective-permute-start | bytes 1179656 | tf_op jit(solution)/shard_map/ppermute | solution.py:272
  63.0 7.9 %collective-permute-start.10 = (bf16[192,1024]{1,0:T(8,128)(2,1)S(1)}, bf16[192,1024]{1,0:T(8,128)(2,1)S(1)}, u32[]{:S(2)}, u32[]{:S(2)}) collective-permute-start(bf16[192,1024]{1,0:T(8,128)(2,1)S(1)} %slice.9), channel_id=1, source_target_pairs={{0,3},{1,0},{2,1},{3,2},{4,7},{5,4},{6,5},{7,6},{8,11},{9,8},{10,9... | collective-permute-start | bytes 1179656 | tf_op jit(solution)/shard_map/ppermute | solution.py:272
  64.7 7.8 %collective-permute-start.12 = (bf16[512,512]{1,0:T(8,128)(2,1)S(1)}, bf16[512,512]{1,0:T(8,128)(2,1)S(1)}, u32[]{:S(2)}, u32[]{:S(2)}) collective-permute-start(bf16[512,512]{1,0:T(8,128)(2,1)S(1)} %shard_map.95.refs_5_), channel_id=1, source_target_pairs={{0,4},{4,0},{8,12},{12,8},{16,20},{20,16},{24,28},{28,24},{32,36},... | collective-permute-start | bytes 1572872 | tf_op jit(solution)/shard_map/ppermute | solution.py:280
  64.7 7.8 %collective-permute-start.13 = (bf16[512,512]{1,0:T(8,128)(2,1)S(1)}, bf16[512,512]{1,0:T(8,128)(2,1)S(1)}, u32[]{:S(2)}, u32[]{:S(2)}) collective-permute-start(bf16[512,512]{1,0:T(8,128)(2,1)S(1)} %collective-permute-done.6.refs_6_), channel_id=1, source_target_pairs={{0,4},{4,0},{8,12},{12,8},{16,20},{20,16},{24,28},{28,24},{32,36},... | collective-permute-start | bytes 1572872 | tf_op jit(solution)/shard_map/ppermute | solution.py:280
  70.4 2.2 %collective-permute-start.14 = (bf16[512,512]{1,0:T(8,128)(2,1)S(1)}, bf16[512,512]{1,0:T(8,128)(2,1)S(1)}, u32[]{:S(2)}, u32[]{:S(2)}) collective-permute-start(bf16[512,512]{1,0:T(8,128)(2,1)S(1)} %collective-permute-done.11.refs_7_), channel_id=1, source_target_pairs={{0,4},{4,0},{8,12},{12,8},{16,20},{20,16},{24,28},{28,24},{32,36},... | collective-permute-start | bytes 1572872 | tf_op jit(solution)/shard_map/ppermute | solution.py:280
  72.6 1.9 collective-permute-start.15
  78.3 2.1 copy-start.2
  87.8 29.6 %all-to-all-start.1 = ((bf16[64,48,128]{2,1,0:T(8,128)(2,1)}), bf16[64,48,128]{2,1,0:T(8,128)(2,1)S(1)}, u32[]{:S(2)}, u32[]{:S(2)}) async-start(bf16[64,48,128]{2,1,0:T(8,128)(2,1)} %bitcast.20), calls=%async_computation.1 | async-start | bytes 1572864 | tf_op jit(solution)/shard_map/all_to_all | solution.py:262
  103.4 3.6 %copy-start = (f32[4,768,768]{2,1,0:T(8,128)}, f32[4,768,768]{2,1,0:T(8,128)S(1)}, u32[]{:S(2)}) copy-start(f32[4,768,768]{2,1,0:T(8,128)S(1)} %get-tuple-element.39.probs_ref) | copy-start | bytes 28311556
  107.0 1.4 copy-start.6
  108.4 1.2 copy-start.8
  117.4 6.0 %copy-start.9 = (f32[4,128,768]{2,1,0:T(8,128)S(1)}, f32[4,128,768]{2,1,0:T(8,128)}, u32[]{:S(2)}) copy-start(f32[4,128,768]{2,1,0:T(8,128)} %copy-done.8) | copy-start | bytes 4718596
  117.4 29.1 %all-to-all-start.2 = ((bf16[64,48,128]{2,1,0:T(8,128)(2,1)}), bf16[64,48,128]{2,1,0:T(8,128)(2,1)S(1)}, u32[]{:S(2)}, u32[]{:S(2)}) async-start(bf16[64,48,128]{2,1,0:T(8,128)(2,1)} %bitcast.21), calls=%async_computation.2 | async-start | bytes 1572864 | tf_op jit(solution)/shard_map/all_to_all | solution.py:262
  123.4 3.7 %copy-start.1 = (f32[4,768,768]{2,1,0:T(8,128)S(1)}, f32[4,768,768]{2,1,0:T(8,128)}, u32[]{:S(2)}) copy-start(f32[4,768,768]{2,1,0:T(8,128)} %copy-done) | copy-start | bytes 28311556
  127.1 1.7 copy-start.7
  146.6 0.9 copy-start.4
  147.4 6.0 %copy-start.5 = (bf16[64,48,128]{2,1,0:T(8,128)(2,1)S(1)}, bf16[64,48,128]{2,1,0:T(8,128)(2,1)}, u32[]{:S(2)}) copy-start(bf16[64,48,128]{2,1,0:T(8,128)(2,1)} %copy-done.4) | copy-start | bytes 2359300
  147.4 62.8 %all-to-all-start.3 = ((bf16[64,48,384]{2,1,0:T(8,128)(2,1)}), bf16[64,48,384]{2,1,0:T(8,128)(2,1)S(1)}, u32[]{:S(2)}, u32[]{:S(2)}) async-start(bf16[64,48,384]{2,1,0:T(8,128)(2,1)} %bitcast.18), calls=%async_computation.3 | async-start | bytes 4718592 | tf_op jit(solution)/shard_map/all_to_all | solution.py:262
  153.4 2.2 %copy-start.3 = (bf16[4096,512]{1,0:T(8,128)(2,1)S(1)}, bf16[4096,512]{1,0:T(8,128)(2,1)}, u32[]{:S(2)}) copy-start(bf16[4096,512]{1,0:T(8,128)(2,1)} %copy-done.2) | copy-start | bytes 12582916
  158.1 21.7 %collective-permute-start.16 = (bf16[384,1024]{1,0:T(8,128)(2,1)S(1)}, bf16[384,1024]{1,0:T(8,128)(2,1)S(1)}, u32[]{:S(2)}, u32[]{:S(2)}) collective-permute-start(bf16[384,1024]{1,0:T(8,128)(2,1)S(1)} %get-tuple-element.34), channel_id=1, source_target_pairs={{0,1},{1,2},{2,3},{3,0},{4,5},{5,6},{6,7},{7,4},{8,9},{9,10},{10,1... | collective-permute-start | bytes 2359304 | tf_op jit(solution)/shard_map/ppermute | solution.py:272
  158.8 37.1 %collective-permute-start.17 = (bf16[384,1024]{1,0:T(8,128)(2,1)S(1)}, bf16[384,1024]{1,0:T(8,128)(2,1)S(1)}, u32[]{:S(2)}, u32[]{:S(2)}) collective-permute-start(bf16[384,1024]{1,0:T(8,128)(2,1)S(1)} %get-tuple-element.35), channel_id=1, source_target_pairs={{0,2},{1,3},{2,0},{3,1},{4,6},{5,7},{6,4},{7,5},{8,10},{9,11},{10,... | collective-permute-start | bytes 2359304 | tf_op jit(solution)/shard_map/ppermute | solution.py:272
  161.3 35.1 %collective-permute-start.18 = (bf16[384,1024]{1,0:T(8,128)(2,1)S(1)}, bf16[384,1024]{1,0:T(8,128)(2,1)S(1)}, u32[]{:S(2)}, u32[]{:S(2)}) collective-permute-start(bf16[384,1024]{1,0:T(8,128)(2,1)S(1)} %get-tuple-element.36), channel_id=1, source_target_pairs={{0,3},{1,0},{2,1},{3,2},{4,7},{5,4},{6,5},{7,6},{8,11},{9,8},{10,9... | collective-permute-start | bytes 2359304 | tf_op jit(solution)/shard_map/ppermute | solution.py:272

commit v5 on v4

--- a/solution.py
+++ b/solution.py
@@ -52,7 +52,13 @@
     return jnp.concatenate(pieces, axis=1)
 
 
-def pack_kernel(ids_ref, q_ref, k_ref, v_ref, out_ref, slots_ref, wide):
+def pack_kernel(ids_ref, q_hbm, k_hbm, v_hbm, out_ref, slots_ref, wide, held, staged, arrive, leave):
+    fetches = [
+        pltpu.make_async_copy(hbm, held.at[t], arrive.at[t])
+        for t, hbm in enumerate((q_hbm, k_hbm, v_hbm))
+    ]
+    for fetch in fetches:
+        fetch.start()
     heads, _, tokens = ids_ref.shape
     rows = CLUSTERS * CAP
     before = (
@@ -70,8 +76,12 @@
         rank = jnp.sum(named * earlier, axis=0, keepdims=True)
         slot = ids * CAP + rank.astype(jnp.int32)
         slots_ref[h : h + 1, :] = slot
+    for fetch in fetches:
+        fetch.wait()
+    for h in range(heads):
+        slot = slots_ref[h : h + 1, :]
         data = jnp.concatenate(
-            [q_ref[:, head_cols(h)], k_ref[:, head_cols(h)], v_ref[:, head_cols(h)], ones], axis=1
+            [held[t, :, h * HD : (h + 1) * HD] for t in range(3)] + [ones], axis=1
         )
         placed = dot_nn(slot_onehot(slot), data)
         used = placed[:, 3 * HD :]
@@ -80,8 +90,18 @@
         wide[0, where, :] = placed[:, :HD]
         wide[1, where, :] = placed[:, HD : 2 * HD] + mark
         wide[2, where, :] = placed[:, 2 * HD : 3 * HD]
-    for t in range(3):
-        out_ref[:, t * HD : (t + 1) * HD] = wide[t].astype(jnp.bfloat16)
+    parts = staged.shape[0]
+    span = staged.shape[1]
+    sends = []
+    for p in range(parts):
+        some = slice(p * span, (p + 1) * span)
+        for t in range(3):
+            staged[p, :, t * HD : (t + 1) * HD] = wide[t, some, :].astype(jnp.bfloat16)
+        send = pltpu.make_async_copy(staged.at[p], out_ref.at[some], leave.at[p])
+        send.start()
+        sends.append(send)
+    for send in sends:
+        send.wait()
 
 
 def collect_kernel(*refs):
@@ -281,17 +301,27 @@
 
     shard = out_weight.T
     depth, width = shard.shape
-    pair = jnp.concatenate([shard, along(shard, lambda z, x, c: (z, x, c + 1))], axis=0)
+    partner = along(shard, lambda z, x, c: (z, x, c + 1))
+    pair = call(collect_kernel, sds((2 * depth, width)), [], 2)(shard, partner)
     opposite = along(shard, lambda z, x, c: (z + 4, x, c))
     near_by = [along(pair, lambda z, x, c, d=d: (z + d * (1 - 2 * c), x, c)) for d in (1, 2, 3)]
     column = call(collect_kernel, sds((8 * depth, width)), [], 5, micros=60)(shard, opposite, *near_by)
     right, left = turn(mixed_grad, 1), turn(mixed_grad, 3)
 
-    payload, slots = call(
+    hbm = pl.BlockSpec(memory_space=pl.ANY)
+    payload, slots = pl.pallas_call(
         pack_kernel,
-        (far_out((slots_all, 3 * HD)), sds((heads, tokens), jnp.int32)),
-        [pltpu.VMEM((3, slots_all, HD), jnp.float32)],
-        4,
+        out_shape=(far_out((slots_all, 3 * HD)), sds((heads, tokens), jnp.int32)),
+        in_specs=[VMEM, hbm, hbm, hbm],
+        out_specs=(hbm, VMEM),
+        scratch_shapes=[
+            pltpu.VMEM((3, slots_all, HD), jnp.float32),
+            pltpu.VMEM((3, tokens, heads * HD), jnp.bfloat16),
+            pltpu.VMEM((4, slots_all // 4, 3 * HD), jnp.bfloat16),
+            pltpu.SemaphoreType.DMA((3,)),
+            pltpu.SemaphoreType.DMA((4,)),
+        ],
+        compiler_params=PARAMS,
     )(far(cluster.transpose(0, 2, 1)), far(query), far(key), far(value))
     arrived = exchange(payload)
     onward = lambda x: along(x, lambda z, x, c: (z, x + 1 - 2 * c, c))
@@ -364,7 +394,7 @@
         (sds((tokens, cols), jnp.float32),) + (sds((tokens, cols)),) * 3,
         [pltpu.VMEM((slots_all, HD), jnp.float32)],
         3,
-    )(slots, near(att_back), near(wt))
+    )(slots, far(att_back), near(wt))
     mixed = own
     for d, part in zip((1, 2, 3), sends):
         mixed = mixed + turn(part, d).astype(jnp.float32)

time: 214 us -> 213 us (level)
    pallas_call x1 -> x2, Pallas kernels: 5.56 us -> 6.34 us  [the longest x1 5.49 us: local(): pl.pallas_call(pack_kernel, out_shape=(far_out((slots_all, 3 * HD)), sds(...]
    unnamed x24 -> x20, local copies, waits for them, and re-layouts: 16.7 us -> 16.7 us
where the time goes in v5:
time: 213 us; the launch traced here: 212 us
  waiting for transfers between devices  105 us (49%)
  starting transfers between devices  54.3 us (25%)
  Pallas kernels  33.7 us (16%)
  local copies, waits for them, and re-layouts  16.7 us (8%)
    ppermute x7, waiting for transfers between devices, turn(): return lax.ppermute(x, 'head', [(i, (i + d) % 4) for i in range(4)])  38.8 us
    all_to_all x4, waiting for transfers between devices, exchange(): return lax.all_to_all(x, 'seq', split_axis=0, concat_axis=0, tiled=True)  37.2 us
    ppermute x12, waiting for transfers between devices, along(): lax.ppermute(x, 'seq', [(place(*s), place(*move(*s))) for s in spots])  29.2 us
    all_to_all x4, starting transfers between devices, exchange(): return lax.all_to_all(x, 'seq', split_axis=0, concat_axis=0, tiled=True)  28.4 us
    unnamed x20, local copies, waits for them, and re-layouts  16.7 us
    ppermute x12, starting transfers between devices, along(): lax.ppermute(x, 'seq', [(place(*s), place(*move(*s))) for s in spots])  13.9 us
    ppermute x7, starting transfers between devices, turn(): return lax.ppermute(x, 'head', [(i, (i + d) % 4) for i in range(4)])  11.9 us
    pallas_call x1, Pallas kernels, local(): pl.pallas_call(forward_kernel, grid=(heads,), out_shape=(far_out((slots_a...  9.12 us
  transfers between devices with their start and end apart: 23, of which 13 were waited for; matrix products, arithmetic and copies ran while one was open for 1% of the time, Pallas kernels for 14%

profile of v5, /device:TPU:2, one launch (start us, length us, event | category | flops | bytes accessed | tf_op | source)
XLA Modules:
  0.0 212.1 jit_solution(13954038702207389311)
XLA Ops:
  0.7 1.4 collective-permute-done.2.refs_1_
  2.2 0.8 shard_map.95
  3.0 4.7 %collective-permute-start.5 = (bf16[128,512]{1,0:T(8,128)(2,1)S(1)}, bf16[128,512]{1,0:T(8,128)(2,1)S(1)}, u32[]{:S(2)}, u32[]{:S(2)}) collective-permute-start(bf16[128,512]{1,0:T(8,128)(2,1)S(1)} %shard_map.95), channel_id=1, source_target_pairs={{0,96},{4,164},{8,104},{12,172},{16,112},{20,180},{24,120},{28,188... | collective-permute-start | bytes 393224 | tf_op jit(solution)/shard_map/ppermute | solution.py:300
  7.7 3.6 %collective-permute-start.4 = (bf16[128,512]{1,0:T(8,128)(2,1)S(1)}, bf16[128,512]{1,0:T(8,128)(2,1)S(1)}, u32[]{:S(2)}, u32[]{:S(2)}) collective-permute-start(bf16[128,512]{1,0:T(8,128)(2,1)S(1)} %shard_map.95), channel_id=1, source_target_pairs={{0,64},{4,196},{8,72},{12,204},{16,80},{20,212},{24,88},{28,220},{... | collective-permute-start | bytes 393224 | tf_op jit(solution)/shard_map/ppermute | solution.py:300
  11.3 1.0 collective-permute-start.3
  12.3 0.5 collective-permute-start.1
  12.9 1.6 collective-permute-start
  14.5 5.5 %shard_map.93 = (bf16[3072,384]{1,0:T(8,128)(2,1)}, s32[4,384]{1,0:T(4,128)S(1)}) custom-call(s32[4,1,384]{2,1,0:T(1,128)} %bitcast.18, bf16[384,512]{1,0:T(8,128)(2,1)} %q_hbm.1, bf16[384,512]{1,0:T(8,128)(2,1)} %k_hbm.1, bf16[384,512]{1,0:T(8,128)(2,1)} %v_hbm.1), custom_call_target="tpu_custom_call" | custom-call | tf_op jit(solution)/shard_map/pallas_call | solution.py:312
  20.0 10.2 %all-to-all-start = ((bf16[64,48,384]{2,1,0:T(8,128)(2,1)}), bf16[64,48,384]{2,1,0:T(8,128)(2,1)S(1)}, u32[]{:S(2)}, u32[]{:S(2)}) async-start(bf16[64,48,384]{2,1,0:T(8,128)(2,1)} %bitcast.15), calls=%async_computation | async-start | bytes 4718592 | tf_op jit(solution)/shard_map/all_to_all | solution.py:282
  30.2 1.7 collective-permute-start.9
  32.0 1.0 shard_map.96.refs_5_
  33.0 1.5 collective-permute-start.6
  34.5 0.6 collective-permute-start.11
  35.1 24.0 %collective-permute-done.6.refs_6_ = bf16[512,512]{1,0:T(8,128)(2,1)S(1)} collective-permute-done((bf16[512,512]{1,0:T(8,128)(2,1)S(1)}, bf16[512,512]{1,0:T(8,128)(2,1)S(1)}, u32[]{:S(2)}, u32[]{:S(2)}) %collective-permute-start.6) | collective-permute-done | bytes 524320 | tf_op jit(solution)/shard_map/ppermute | solution.py:300
  59.1 1.4 collective-permute-start.7
  60.5 1.7 collective-permute-start.8
  62.2 1.7 collective-permute-start.10
  64.0 0.5 collective-permute-start.13
  64.5 5.1 %collective-permute-done.8.refs_2_ = bf16[192,1024]{1,0:T(8,128)(2,1)S(1)} collective-permute-done((bf16[192,1024]{1,0:T(8,128)(2,1)S(1)}, bf16[192,1024]{1,0:T(8,128)(2,1)S(1)}, u32[]{:S(2)}, u32[]{:S(2)}) %collective-permute-start.8) | collective-permute-done | bytes 393248 | tf_op jit(solution)/shard_map/ppermute | solution.py:292
  70.1 1.8 collective-permute-done.7.refs_8_
  71.9 1.9 collective-permute-done.15.refs_12_
  73.8 3.8 %shard_map.97 = (bf16[3072,128]{1,0:T(8,128)(2,1)}, bf16[4096,512]{1,0:T(8,128)(2,1)S(1)}) custom-call(s32[4,384]{1,0:T(4,128)S(1)} %get-tuple-element.24.slots_ref, bf16[384,1024]{1,0:T(8,128)(2,1)S(1)} %copy-done.8, bf16[384,1024]{1,0:T(8,128)(2,1)S(1)} %collective-permute-done.refs_1_, bf16[192,1024]{1,0:T(8,128)(2,1)S(1)} %collective-permute-done.8.refs_2_, ...), custom_call_target="tpu_custom_call" | custom-call | tf_op jit(solution)/shard_map/pallas_call | solution.py:362
  77.6 2.1 copy-done.2
  79.6 7.4 %all-to-all-done = bf16[64,48,384]{2,1,0:T(8,128)(2,1)S(1)} async-done(((bf16[64,48,384]{2,1,0:T(8,128)(2,1)}), bf16[64,48,384]{2,1,0:T(8,128)(2,1)S(1)}, u32[]{:S(2)}, u32[]{:S(2)}) %all-to-all-start) | async-done | bytes 2359328 | tf_op jit(solution)/shard_map/all_to_all | solution.py:282
  87.1 6.4 %all-to-all-start.1 = ((bf16[64,48,128]{2,1,0:T(8,128)(2,1)}), bf16[64,48,128]{2,1,0:T(8,128)(2,1)S(1)}, u32[]{:S(2)}, u32[]{:S(2)}) async-start(bf16[64,48,128]{2,1,0:T(8,128)(2,1)} %bitcast.16), calls=%async_computation.1 | async-start | bytes 1572864 | tf_op jit(solution)/shard_map/all_to_all | solution.py:282
  93.5 9.1 %shard_map.94 = (bf16[3072,128]{1,0:T(8,128)(2,1)}, bf16[12,768,128]{2,1,0:T(8,128)(2,1)S(1)}, f32[4,768,768]{2,1,0:T(8,128)S(1)}, f32[4,128,768]{2,1,0:T(8,128)S(1)}) custom-call(bf16[3072,384]{1,0:T(8,128)(2,1)S(1)} %bitcast.10), custom_call_target="tpu_custom_call" | custom-call | tf_op jit(solution)/shard_map/pallas_call | solution.py:339
  102.7 3.6 %copy-done = f32[4,768,768]{2,1,0:T(8,128)} copy-done((f32[4,768,768]{2,1,0:T(8,128)}, f32[4,768,768]{2,1,0:T(8,128)S(1)}, u32[]{:S(2)}) %copy-start) | copy-done | bytes 9437208
  106.3 1.4 copy-done.4
  107.7 1.2 copy-done.6
  108.9 7.8 %all-to-all-done.1 = bf16[64,48,128]{2,1,0:T(8,128)(2,1)S(1)} async-done(((bf16[64,48,128]{2,1,0:T(8,128)(2,1)}), bf16[64,48,128]{2,1,0:T(8,128)(2,1)S(1)}, u32[]{:S(2)}, u32[]{:S(2)}) %all-to-all-start.1) | async-done | bytes 786464 | tf_op jit(solution)/shard_map/all_to_all | solution.py:282
  116.7 5.9 %all-to-all-start.2 = ((bf16[64,48,128]{2,1,0:T(8,128)(2,1)}), bf16[64,48,128]{2,1,0:T(8,128)(2,1)S(1)}, u32[]{:S(2)}, u32[]{:S(2)}) async-start(bf16[64,48,128]{2,1,0:T(8,128)(2,1)} %bitcast.17), calls=%async_computation.2 | async-start | bytes 1572864 | tf_op jit(solution)/shard_map/all_to_all | solution.py:282
  122.7 3.7 %copy-done.1 = f32[4,768,768]{2,1,0:T(8,128)S(1)} copy-done((f32[4,768,768]{2,1,0:T(8,128)S(1)}, f32[4,768,768]{2,1,0:T(8,128)}, u32[]{:S(2)}) %copy-start.1) | copy-done | bytes 9437208
  126.4 1.7 copy-done.5
  128.0 7.2 %shard_map.99 = bf16[3072,384]{1,0:T(8,128)(2,1)} custom-call(bf16[3072,128]{1,0:T(8,128)(2,1)S(1)} %bitcast.12, bf16[12,768,128]{2,1,0:T(8,128)(2,1)S(1)} %copy-done.5, f32[4,768,768]{2,1,0:T(8,128)S(1)} %copy-done.1, f32[4,128,768]{2,1,0:T(8,128)S(1)} %copy-done.7), custom_call_target="tpu_custom_call" | custom-call | tf_op jit(solution)/shard_map/pallas_call | solution.py:372
  135.2 10.6 %all-to-all-done.2 = bf16[64,48,128]{2,1,0:T(8,128)(2,1)S(1)} async-done(((bf16[64,48,128]{2,1,0:T(8,128)(2,1)}), bf16[64,48,128]{2,1,0:T(8,128)(2,1)S(1)}, u32[]{:S(2)}, u32[]{:S(2)}) %all-to-all-start.2) | async-done | bytes 786464 | tf_op jit(solution)/shard_map/all_to_all | solution.py:282
  145.8 0.9 copy-done.9
  146.7 5.8 %all-to-all-start.3 = ((bf16[64,48,384]{2,1,0:T(8,128)(2,1)}), bf16[64,48,384]{2,1,0:T(8,128)(2,1)S(1)}, u32[]{:S(2)}, u32[]{:S(2)}) async-start(bf16[64,48,384]{2,1,0:T(8,128)(2,1)} %bitcast.13), calls=%async_computation.3 | async-start | bytes 4718592 | tf_op jit(solution)/shard_map/all_to_all | solution.py:282
  152.6 2.2 %copy-done.3 = bf16[4096,512]{1,0:T(8,128)(2,1)S(1)} copy-done((bf16[4096,512]{1,0:T(8,128)(2,1)S(1)}, bf16[4096,512]{1,0:T(8,128)(2,1)}, u32[]{:S(2)}) %copy-start.3) | copy-done | bytes 4194328
  154.7 3.6 %shard_map.98 = (f32[384,1024]{1,0:T(8,128)S(1)}, bf16[384,1024]{1,0:T(8,128)(2,1)S(1)}, bf16[384,1024]{1,0:T(8,128)(2,1)S(1)}, bf16[384,1024]{1,0:T(8,128)(2,1)S(1)}) custom-call(s32[4,384]{1,0:T(4,128)S(1)} %get-tuple-element.24.slots_ref, bf16[3072,128]{1,0:T(8,128)(2,1)} %bitcast.14, bf16[4096,512]{1,0:T(8,128)(2,1)S(1)} %copy-done.3), custom_call_target="tpu_custom_call" | custom-call | tf_op jit(solution)/shard_map/pallas_call | solution.py:392
  158.3 0.7 collective-permute-start.16
  159.0 2.5 %collective-permute-start.17 = (bf16[384,1024]{1,0:T(8,128)(2,1)S(1)}, bf16[384,1024]{1,0:T(8,128)(2,1)S(1)}, u32[]{:S(2)}, u32[]{:S(2)}) collective-permute-start(bf16[384,1024]{1,0:T(8,128)(2,1)S(1)} %get-tuple-element.35), channel_id=1, source_target_pairs={{0,2},{1,3},{2,0},{3,1},{4,6},{5,7},{6,4},{7,5},{8,10},{9,11},{10,... | collective-permute-start | bytes 2359304 | tf_op jit(solution)/shard_map/ppermute | solution.py:292
  161.5 2.0 collective-permute-start.18
  163.5 16.5 %collective-permute-done.16 = bf16[384,1024]{1,0:T(8,128)(2,1)S(1)} collective-permute-done((bf16[384,1024]{1,0:T(8,128)(2,1)S(1)}, bf16[384,1024]{1,0:T(8,128)(2,1)S(1)}, u32[]{:S(2)}, u32[]{:S(2)}) %collective-permute-start.16) | collective-permute-done | bytes 786464 | tf_op jit(solution)/shard_map/ppermute | solution.py:292
  180.0 16.1 %collective-permute-done.17 = bf16[384,1024]{1,0:T(8,128)(2,1)S(1)} collective-permute-done((bf16[384,1024]{1,0:T(8,128)(2,1)S(1)}, bf16[384,1024]{1,0:T(8,128)(2,1)S(1)}, u32[]{:S(2)}, u32[]{:S(2)}) %collective-permute-start.17) | collective-permute-done | bytes 786464 | tf_op jit(solution)/shard_map/ppermute | solution.py:292
  196.1 0.6 collective-permute-done.18
  196.7 1.4 add_convert_fusion
  198.1 11.3 %all-to-all-done.3 = bf16[64,48,384]{2,1,0:T(8,128)(2,1)S(1)} async-done(((bf16[64,48,384]{2,1,0:T(8,128)(2,1)}), bf16[64,48,384]{2,1,0:T(8,128)(2,1)S(1)}, u32[]{:S(2)}, u32[]{:S(2)}) %all-to-all-start.3) | async-done | bytes 2359328 | tf_op jit(solution)/shard_map/all_to_all | solution.py:282
  209.4 2.7 %shard_map.100 = (bf16[384,512]{1,0:T(8,128)(2,1)}, bf16[384,512]{1,0:T(8,128)(2,1)}, bf16[384,512]{1,0:T(8,128)(2,1)}) custom-call(s32[4,384]{1,0:T(4,128)S(1)} %get-tuple-element.24.slots_ref, bf16[3072,384]{1,0:T(8,128)(2,1)S(1)} %bitcast.11), custom_call_target="tpu_custom_call" | custom-call | tf_op jit(solution)/shard_map/pallas_call | solution.py:403
  (29 shorter events, 0.7 us)
Async XLA Ops:
  0.6 1.6 collective-permute-start.2
  3.0 28.9 %collective-permute-start.5 = (bf16[128,512]{1,0:T(8,128)(2,1)S(1)}, bf16[128,512]{1,0:T(8,128)(2,1)S(1)}, u32[]{:S(2)}, u32[]{:S(2)}) collective-permute-start(bf16[128,512]{1,0:T(8,128)(2,1)S(1)} %shard_map.95), channel_id=1, source_target_pairs={{0,96},{4,164},{8,104},{12,172},{16,112},{20,180},{24,120},{28,188... | collective-permute-start | bytes 393224 | tf_op jit(solution)/shard_map/ppermute | solution.py:300
  7.7 24.2 %collective-permute-start.4 = (bf16[128,512]{1,0:T(8,128)(2,1)S(1)}, bf16[128,512]{1,0:T(8,128)(2,1)S(1)}, u32[]{:S(2)}, u32[]{:S(2)}) collective-permute-start(bf16[128,512]{1,0:T(8,128)(2,1)S(1)} %shard_map.95), channel_id=1, source_target_pairs={{0,64},{4,196},{8,72},{12,204},{16,80},{20,212},{24,88},{28,220},{... | collective-permute-start | bytes 393224 | tf_op jit(solution)/shard_map/ppermute | solution.py:300
  11.3 20.6 %collective-permute-start.3 = (bf16[128,512]{1,0:T(8,128)(2,1)S(1)}, bf16[128,512]{1,0:T(8,128)(2,1)}, u32[]{:S(2)}, u32[]{:S(2)}) collective-permute-start(bf16[128,512]{1,0:T(8,128)(2,1)S(1)} %shard_map.95), channel_id=1, source_target_pairs={{0,32},{4,228},{8,40},{12,236},{16,48},{20,244},{24,56},{28,252},{... | collective-permute-start | bytes 393224 | tf_op jit(solution)/shard_map/ppermute | solution.py:300
  12.3 17.9 %collective-permute-start.1 = (bf16[64,512]{1,0:T(8,128)(2,1)}, bf16[64,512]{1,0:T(8,128)(2,1)}, u32[]{:S(2)}, u32[]{:S(2)}) collective-permute-start(bf16[64,512]{1,0:T(8,128)(2,1)} %bitcast.3.refs_0_), channel_id=1, source_target_pairs={{0,128},{4,132},{8,136},{12,140},{16,144},{20,148},{24,152},{28,15... | collective-permute-start | bytes 196616 | tf_op jit(solution)/shard_map/ppermute | solution.py:300
  12.9 47.6 %collective-permute-start = (bf16[384,1024]{1,0:T(8,128)(2,1)}, bf16[384,1024]{1,0:T(8,128)(2,1)S(1)}, u32[]{:S(2)}, u32[]{:S(2)}) collective-permute-start(bf16[384,1024]{1,0:T(8,128)(2,1)} %refs_0_.1), channel_id=1, source_target_pairs={{0,1},{1,2},{2,3},{3,0},{4,5},{5,6},{6,7},{7,4},{8,9},{9,10},{10,1... | collective-permute-start | bytes 2359304 | tf_op jit(solution)/shard_map/ppermute | solution.py:292
  20.0 67.1 %all-to-all-start = ((bf16[64,48,384]{2,1,0:T(8,128)(2,1)}), bf16[64,48,384]{2,1,0:T(8,128)(2,1)S(1)}, u32[]{:S(2)}, u32[]{:S(2)}) async-start(bf16[64,48,384]{2,1,0:T(8,128)(2,1)} %bitcast.15), calls=%async_computation | async-start | bytes 4718592 | tf_op jit(solution)/shard_map/all_to_all | solution.py:282
  30.2 32.0 %collective-permute-start.9 = (bf16[384,1024]{1,0:T(8,128)(2,1)}, bf16[384,1024]{1,0:T(8,128)(2,1)S(1)}, u32[]{:S(2)}, u32[]{:S(2)}) collective-permute-start(bf16[384,1024]{1,0:T(8,128)(2,1)} %refs_0_.1), channel_id=1, source_target_pairs={{0,3},{1,0},{2,1},{3,2},{4,7},{5,4},{6,5},{7,6},{8,11},{9,8},{10,9... | collective-permute-start | bytes 2359304 | tf_op jit(solution)/shard_map/ppermute | solution.py:292
  33.0 40.8 %copy-start.8 = (bf16[384,1024]{1,0:T(8,128)(2,1)S(1)}, bf16[384,1024]{1,0:T(8,128)(2,1)}, u32[]{:S(2)}) copy-start(bf16[384,1024]{1,0:T(8,128)(2,1)} %refs_0_.1) | copy-start | bytes 2359300
  33.0 26.1 %collective-permute-start.6 = (bf16[512,512]{1,0:T(8,128)(2,1)S(1)}, bf16[512,512]{1,0:T(8,128)(2,1)S(1)}, u32[]{:S(2)}, u32[]{:S(2)}) collective-permute-start(bf16[512,512]{1,0:T(8,128)(2,1)S(1)} %shard_map.96.refs_5_), channel_id=1, source_target_pairs={{0,8},{4,28},{8,16},{12,4},{16,24},{20,12},{24,0},{28,20},{32,40},... | collective-permute-start | bytes 1572872 | tf_op jit(solution)/shard_map/ppermute | solution.py:300
  34.5 29.4 %collective-permute-start.11 = (bf16[512,512]{1,0:T(8,128)(2,1)S(1)}, bf16[512,512]{1,0:T(8,128)(2,1)S(1)}, u32[]{:S(2)}, u32[]{:S(2)}) collective-permute-start(bf16[512,512]{1,0:T(8,128)(2,1)S(1)} %shard_map.96.refs_5_), channel_id=1, source_target_pairs={{0,24},{4,12},{8,0},{12,20},{16,8},{20,28},{24,16},{28,4},{32,56},... | collective-permute-start | bytes 1572872 | tf_op jit(solution)/shard_map/ppermute | solution.py:300
  59.1 12.7 %collective-permute-start.7 = (bf16[512,512]{1,0:T(8,128)(2,1)S(1)}, bf16[512,512]{1,0:T(8,128)(2,1)S(1)}, u32[]{:S(2)}, u32[]{:S(2)}) collective-permute-start(bf16[512,512]{1,0:T(8,128)(2,1)S(1)} %collective-permute-done.6.refs_6_), channel_id=1, source_target_pairs={{0,8},{4,28},{8,16},{12,4},{16,24},{20,12},{24,0},{28,20},{32,40},... | collective-permute-start | bytes 1572872 | tf_op jit(solution)/shard_map/ppermute | solution.py:300
  60.5 9.1 %collective-permute-start.8 = (bf16[192,1024]{1,0:T(8,128)(2,1)S(1)}, bf16[192,1024]{1,0:T(8,128)(2,1)S(1)}, u32[]{:S(2)}, u32[]{:S(2)}) collective-permute-start(bf16[192,1024]{1,0:T(8,128)(2,1)S(1)} %slice.8), channel_id=1, source_target_pairs={{0,1},{1,2},{2,3},{3,0},{4,5},{5,6},{6,7},{7,4},{8,9},{9,10},{10,1... | collective-permute-start | bytes 1179656 | tf_op jit(solution)/shard_map/ppermute | solution.py:292
  62.2 7.9 %collective-permute-start.10 = (bf16[192,1024]{1,0:T(8,128)(2,1)S(1)}, bf16[192,1024]{1,0:T(8,128)(2,1)S(1)}, u32[]{:S(2)}, u32[]{:S(2)}) collective-permute-start(bf16[192,1024]{1,0:T(8,128)(2,1)S(1)} %slice.9), channel_id=1, source_target_pairs={{0,3},{1,0},{2,1},{3,2},{4,7},{5,4},{6,5},{7,6},{8,11},{9,8},{10,9... | collective-permute-start | bytes 1179656 | tf_op jit(solution)/shard_map/ppermute | solution.py:292
  64.0 7.9 %collective-permute-start.12 = (bf16[512,512]{1,0:T(8,128)(2,1)S(1)}, bf16[512,512]{1,0:T(8,128)(2,1)S(1)}, u32[]{:S(2)}, u32[]{:S(2)}) collective-permute-start(bf16[512,512]{1,0:T(8,128)(2,1)S(1)} %shard_map.96.refs_5_), channel_id=1, source_target_pairs={{0,4},{4,0},{8,12},{12,8},{16,20},{20,16},{24,28},{28,24},{32,36},... | collective-permute-start | bytes 1572872 | tf_op jit(solution)/shard_map/ppermute | solution.py:300
  64.0 7.9 %collective-permute-start.13 = (bf16[512,512]{1,0:T(8,128)(2,1)S(1)}, bf16[512,512]{1,0:T(8,128)(2,1)S(1)}, u32[]{:S(2)}, u32[]{:S(2)}) collective-permute-start(bf16[512,512]{1,0:T(8,128)(2,1)S(1)} %collective-permute-done.6.refs_6_), channel_id=1, source_target_pairs={{0,4},{4,0},{8,12},{12,8},{16,20},{20,16},{24,28},{28,24},{32,36},... | collective-permute-start | bytes 1572872 | tf_op jit(solution)/shard_map/ppermute | solution.py:300
  69.6 2.3 %collective-permute-start.14 = (bf16[512,512]{1,0:T(8,128)(2,1)S(1)}, bf16[512,512]{1,0:T(8,128)(2,1)S(1)}, u32[]{:S(2)}, u32[]{:S(2)}) collective-permute-start(bf16[512,512]{1,0:T(8,128)(2,1)S(1)} %collective-permute-done.11.refs_7_), channel_id=1, source_target_pairs={{0,4},{4,0},{8,12},{12,8},{16,20},{20,16},{24,28},{28,24},{32,36},... | collective-permute-start | bytes 1572872 | tf_op jit(solution)/shard_map/ppermute | solution.py:300
  71.9 1.9 collective-permute-start.15
  77.6 2.1 copy-start.2
  87.1 29.6 %all-to-all-start.1 = ((bf16[64,48,128]{2,1,0:T(8,128)(2,1)}), bf16[64,48,128]{2,1,0:T(8,128)(2,1)S(1)}, u32[]{:S(2)}, u32[]{:S(2)}) async-start(bf16[64,48,128]{2,1,0:T(8,128)(2,1)} %bitcast.16), calls=%async_computation.1 | async-start | bytes 1572864 | tf_op jit(solution)/shard_map/all_to_all | solution.py:282
  102.7 3.6 %copy-start = (f32[4,768,768]{2,1,0:T(8,128)}, f32[4,768,768]{2,1,0:T(8,128)S(1)}, u32[]{:S(2)}) copy-start(f32[4,768,768]{2,1,0:T(8,128)S(1)} %get-tuple-element.39.probs_ref) | copy-start | bytes 28311556
  106.3 1.4 copy-start.4
  107.7 1.2 copy-start.6
  116.7 6.0 %copy-start.7 = (f32[4,128,768]{2,1,0:T(8,128)S(1)}, f32[4,128,768]{2,1,0:T(8,128)}, u32[]{:S(2)}) copy-start(f32[4,128,768]{2,1,0:T(8,128)} %copy-done.6) | copy-start | bytes 4718596
  116.7 29.1 %all-to-all-start.2 = ((bf16[64,48,128]{2,1,0:T(8,128)(2,1)}), bf16[64,48,128]{2,1,0:T(8,128)(2,1)S(1)}, u32[]{:S(2)}, u32[]{:S(2)}) async-start(bf16[64,48,128]{2,1,0:T(8,128)(2,1)} %bitcast.17), calls=%async_computation.2 | async-start | bytes 1572864 | tf_op jit(solution)/shard_map/all_to_all | solution.py:282
  122.7 3.7 %copy-start.1 = (f32[4,768,768]{2,1,0:T(8,128)S(1)}, f32[4,768,768]{2,1,0:T(8,128)}, u32[]{:S(2)}) copy-start(f32[4,768,768]{2,1,0:T(8,128)} %copy-done) | copy-start | bytes 28311556
  126.4 1.7 copy-start.5
  145.8 0.9 copy-start.9
  146.7 62.7 %all-to-all-start.3 = ((bf16[64,48,384]{2,1,0:T(8,128)(2,1)}), bf16[64,48,384]{2,1,0:T(8,128)(2,1)S(1)}, u32[]{:S(2)}, u32[]{:S(2)}) async-start(bf16[64,48,384]{2,1,0:T(8,128)(2,1)} %bitcast.13), calls=%async_computation.3 | async-start | bytes 4718592 | tf_op jit(solution)/shard_map/all_to_all | solution.py:282
  152.5 2.2 %copy-start.3 = (bf16[4096,512]{1,0:T(8,128)(2,1)S(1)}, bf16[4096,512]{1,0:T(8,128)(2,1)}, u32[]{:S(2)}) copy-start(bf16[4096,512]{1,0:T(8,128)(2,1)} %copy-done.2) | copy-start | bytes 12582916
  158.3 21.7 %collective-permute-start.16 = (bf16[384,1024]{1,0:T(8,128)(2,1)S(1)}, bf16[384,1024]{1,0:T(8,128)(2,1)S(1)}, u32[]{:S(2)}, u32[]{:S(2)}) collective-permute-start(bf16[384,1024]{1,0:T(8,128)(2,1)S(1)} %get-tuple-element.34), channel_id=1, source_target_pairs={{0,1},{1,2},{2,3},{3,0},{4,5},{5,6},{6,7},{7,4},{8,9},{9,10},{10,1... | collective-permute-start | bytes 2359304 | tf_op jit(solution)/shard_map/ppermute | solution.py:292
  159.0 37.0 %collective-permute-start.17 = (bf16[384,1024]{1,0:T(8,128)(2,1)S(1)}, bf16[384,1024]{1,0:T(8,128)(2,1)S(1)}, u32[]{:S(2)}, u32[]{:S(2)}) collective-permute-start(bf16[384,1024]{1,0:T(8,128)(2,1)S(1)} %get-tuple-element.35), channel_id=1, source_target_pairs={{0,2},{1,3},{2,0},{3,1},{4,6},{5,7},{6,4},{7,5},{8,10},{9,11},{10,... | collective-permute-start | bytes 2359304 | tf_op jit(solution)/shard_map/ppermute | solution.py:292
  161.5 35.1 %collective-permute-start.18 = (bf16[384,1024]{1,0:T(8,128)(2,1)S(1)}, bf16[384,1024]{1,0:T(8,128)(2,1)S(1)}, u32[]{:S(2)}, u32[]{:S(2)}) collective-permute-start(bf16[384,1024]{1,0:T(8,128)(2,1)S(1)} %get-tuple-element.36), channel_id=1, source_target_pairs={{0,3},{1,0},{2,1},{3,2},{4,7},{5,4},{6,5},{7,6},{8,11},{9,8},{10,9... | collective-permute-start | bytes 2359304 | tf_op jit(solution)/shard_map/ppermute | solution.py:292
